TPU v7x, 256 devices: a whole 4x4x8 slice. The times are simulated.
256 devices in a mesh: tile: 32 (over z, y), batch: 8 (over x, core).
Axes of the slice: x: 4, y: 4, z: 8, core: 2. Of those that a mesh axis runs over, the one named last changes fastest.
Arguments:
- object_field: float32 [2, 8192, 512], P(None, 'tile'), may hold values from -5 to 5
- probe_modes: float32 [4, 2, 256, 256], replicated, may hold values from -4 to 4
- amplitudes: float32 [256, 256, 256], P(('tile', 'batch')), may hold values from 0.2 to 4
- positions: int32 [256, 2], P(('tile', 'batch')), may hold values from 0 to 7936, as said below
- shifts: float32 [256, 2], P(('tile', 'batch')), may hold values from -0.5 to 0.5
Outputs:
- new_object: float32 [2, 8192, 512], P(None, 'tile')
- probe_direction: float32 [4, 2, 256, 256], replicated
- shift_grad: float32 [256, 2], P(('tile', 'batch'))
Inputs may be any that keep to these rules, and one draw needn't show every extreme that they name: `positions`: pattern p's corner row lies in strip p // 8, that is from 256 * (p // 8) to that plus 256 - 1, but never past 8192 - 256; its corner column is at most 256, so every patch lies inside the object.
All inputs are finite; a program needn't handle non-finite values.
Results may differ from a plain program's by a relative error of at most 0.0003.
Values sent between devices are 32-bit elements; how exact they have to be, the bound alone decides.
No kernel may reach another device: no remote copies, remote signals or barrier semaphores. Data moves between devices by JAX's collectives and lax.ppermute only.
A program may use at most 128 MiB of HBM per device.

v0:
```python
import math

import jax
import jax.numpy as jnp
from jax import lax
from jax.sharding import PartitionSpec as P

full_turn = 2.0 * math.pi
amplitude_floor = 0.5
highest = lax.Precision.HIGHEST


def shifted(block, axis, distance):
    devices = range(lax.axis_size(axis))
    route = [(i - distance, i) for i in devices if i - distance in devices]
    return lax.ppermute(block, axis, route)


def left_apply(mat_real, mat_imag, data_real, data_imag):
    first_term = jnp.einsum("um,kmn->kun", mat_real + mat_imag, data_real, precision=highest)
    second_term = jnp.einsum("um,kmn->kun", mat_real, data_imag - data_real, precision=highest)
    third_term = jnp.einsum("um,kmn->kun", mat_imag, data_real + data_imag, precision=highest)
    return (first_term - third_term, first_term + second_term)


def right_apply(data_real, data_imag, mat_real, mat_imag):
    first_term = jnp.einsum("kun,nv->kuv", data_real + data_imag, mat_real, precision=highest)
    second_term = jnp.einsum("kun,nv->kuv", data_real, mat_imag - mat_real, precision=highest)
    third_term = jnp.einsum("kun,nv->kuv", data_imag, mat_real + mat_imag, precision=highest)
    return (first_term - third_term, first_term + second_term)


def transform(data_real, data_imag, mat_real, mat_imag):
    half_real, half_imag = left_apply(mat_real, mat_imag, data_real, data_imag)
    return right_apply(half_real, half_imag, mat_real, mat_imag)


def on_device(object_field, probe_modes, amplitudes, positions, shifts):
    strip_rows = object_field.shape[1]
    column_count = object_field.shape[2]
    mode_count = probe_modes.shape[0]
    pattern_side = probe_modes.shape[2]
    indices = jnp.arange(pattern_side)
    frequency = ((indices + pattern_side // 2) % pattern_side - pattern_side // 2).astype(
        jnp.float32
    ) / pattern_side
    products = (indices[:, None] * indices[None, :] % pattern_side).astype(jnp.float32)
    table_angle = -full_turn / pattern_side * products
    table_real = jnp.cos(table_angle) / math.sqrt(pattern_side)
    table_imag = jnp.sin(table_angle) / math.sqrt(pattern_side)
    rim_rows = shifted(object_field[:, : pattern_side - 1, :], "tile", -1)
    extended = jnp.concatenate([object_field, rim_rows], axis=1)
    probe_real, probe_imag = transform(probe_modes[:, 0], probe_modes[:, 1], table_real, table_imag)
    base_row = lax.axis_index("tile") * strip_rows
    zero_index = jnp.int32(0)

    def visit(carry, pattern_item):
        totals, grad_real, grad_imag, mass = carry
        measured, corner, shift_pair = pattern_item
        row_start = corner[0] - base_row
        col_start = corner[1]
        patch = lax.dynamic_slice(
            extended, (zero_index, row_start, col_start), (2, pattern_side, pattern_side)
        )
        patch_real = patch[0][None]
        patch_imag = patch[1][None]
        phase_angle = -full_turn * (
            shift_pair[0] * frequency[:, None] + shift_pair[1] * frequency[None, :]
        )
        ramp_real = jnp.cos(phase_angle)[None]
        ramp_imag = jnp.sin(phase_angle)[None]
        spec_real = ramp_real * probe_real - ramp_imag * probe_imag
        spec_imag = ramp_real * probe_imag + ramp_imag * probe_real
        shifted_real, shifted_imag = transform(spec_real, spec_imag, table_real, -table_imag)
        exit_real = shifted_real * patch_real - shifted_imag * patch_imag
        exit_imag = shifted_real * patch_imag + shifted_imag * patch_real
        far_real, far_imag = transform(exit_real, exit_imag, table_real, table_imag)
        intensity = jnp.sum(far_real * far_real + far_imag * far_imag, axis=0)
        ratio = (measured / jnp.maximum(jnp.sqrt(intensity), amplitude_floor))[None]
        revised_real, revised_imag = transform(
            far_real * ratio, far_imag * ratio, table_real, -table_imag
        )
        change_real = revised_real - exit_real
        change_imag = revised_imag - exit_imag
        num_real = jnp.sum(shifted_real * change_real + shifted_imag * change_imag, axis=0)
        num_imag = jnp.sum(shifted_real * change_imag - shifted_imag * change_real, axis=0)
        weight_term = jnp.sum(shifted_real * shifted_real + shifted_imag * shifted_imag, axis=0)
        chi_real = patch_real * change_real + patch_imag * change_imag
        chi_imag = patch_real * change_imag - patch_imag * change_real
        hat_real, hat_imag = transform(chi_real, chi_imag, table_real, table_imag)
        cross = jnp.sum(hat_real * spec_imag - hat_imag * spec_real, axis=0)
        grad_pair = (
            full_turn
            / pattern_side
            * jnp.stack([jnp.sum(frequency[:, None] * cross), jnp.sum(frequency[None, :] * cross)])
        )
        grad_real = grad_real + ramp_real * hat_real + ramp_imag * hat_imag
        grad_imag = grad_imag + ramp_real * hat_imag - ramp_imag * hat_real
        mass = mass + patch[0] * patch[0] + patch[1] * patch[1]
        old_block = lax.dynamic_slice(
            totals, (zero_index, row_start, col_start), (3, pattern_side, pattern_side)
        )
        new_block = old_block + jnp.stack([num_real, num_imag, weight_term])
        totals = lax.dynamic_update_slice(totals, new_block, (zero_index, row_start, col_start))
        return ((totals, grad_real, grad_imag, mass), grad_pair)

    start_carry = (
        jnp.zeros((3, strip_rows + pattern_side - 1, column_count), jnp.float32),
        jnp.zeros((mode_count, pattern_side, pattern_side), jnp.float32),
        jnp.zeros((mode_count, pattern_side, pattern_side), jnp.float32),
        jnp.zeros((pattern_side, pattern_side), jnp.float32),
    )
    final_carry, shift_grad = lax.scan(visit, start_carry, (amplitudes, positions, shifts))
    totals, grad_real, grad_imag, mass = final_carry
    summed = lax.psum(totals, "batch")
    spilled = shifted(summed[:, strip_rows:], "tile", 1)
    owned = summed[:, :strip_rows] + jnp.pad(
        spilled, ((0, 0), (0, strip_rows - pattern_side + 1), (0, 0))
    )
    new_object = object_field + owned[:2] / (owned[2] + 1.0)[None]
    field_real, field_imag = transform(grad_real, grad_imag, table_real, -table_imag)
    sum_real, sum_imag, sum_mass = lax.psum((field_real, field_imag, mass), ("tile", "batch"))
    probe_direction = jnp.stack([sum_real, sum_imag], axis=1) / jnp.sqrt(sum_mass + 1.0)[None, None]
    return (new_object, probe_direction, shift_grad)


def solution(mesh):
    return jax.shard_map(
        on_device,
        mesh=mesh,
        in_specs=(
            P(None, "tile", None),
            P(),
            P(("tile", "batch"), None, None),
            P(("tile", "batch"), None),
            P(("tile", "batch"), None),
        ),
        out_specs=(P(None, "tile", None), P(), P(("tile", "batch"), None)),
        check_vma=False,
    )
```

profile of v0, /device:TPU:8, one launch (start us, length us, event | category | flops | bytes accessed | tf_op | source)
XLA Modules:
  0.0 484.3 jit_solution(8917221598449892411)
XLA Ops:
  7.2 4.2 collective-permute-start
  11.5 3.3 convolution_bitcast_fusion.2
  26.2 2.8 multiply_add_fusion.3
  29.0 5.3 %fusion.74 = f32[4,256,256]{2,1,0:T(8,128)} fusion(f32[4,256,256]{2,1,0:T(8,128)S(1)} %get-tuple-element.68), kind=kOutput, calls=%fused_computation.127 | convolution fusion | flops 806486016 | bytes 2097152 | tf_op jit(solution)/shard_map/while/body/eval_jaxpr/um,kmn->kun/dot_general | solution.py:20
  34.2 3.9 fusion.14
  41.3 3.9 fusion.15
  48.0 2.8 convolution_subtract_fusion.8
  53.1 3.2 multiply_subtract_fusion.2
  56.3 2.8 fusion.98
  64.5 2.9 fusion.32
  67.4 2.8 convolution_subtract_fusion.6
  70.3 2.8 add_reduce_fusion.2
  73.2 2.8 fusion.48
  76.0 3.1 fusion.10
  79.1 2.8 fusion.11
  81.9 2.7 fusion.28
  84.6 2.9 fusion.9
  87.5 3.6 add_reduce_fusion.1
  91.1 2.8 fusion.95
  93.9 2.8 fusion.6
  96.7 2.8 fusion.7
  99.5 2.7 fusion.24
  102.3 3.0 convolution_subtract_fusion.2
  105.3 4.8 subtract_reduce_fusion
  115.9 9.1 %dynamic_update_slice.7 = f32[3,511,512]{2,1,0:T(8,128)} dynamic-update-slice(f32[3,511,512]{2,1,0:T(8,128)} %broadcast_in_dim.9, f32[3,256,256]{2,1,0:T(8,128)} %pad_maximum_fusion, s32[]{:T(128)} %constant.71.clone.1, s32[]{:T(128)S(6)} %select_n.117, s32[]{:T(128)S(6)} %select_n.118) | dynamic-update-slice | bytes 1572868 | tf_op jit(solution)/shard_map/while/body/eval_jaxpr/dynamic_update_slice | solution.py:104
  125.5 4.2 fusion.4
  129.7 2.8 fusion.5
  135.3 3.8 fusion.2
  139.1 4.0 fusion.3
  143.8 56.8 %all-reduce.5.cloned.1.call-done = f32[3,511,512]{2,1,0:T(8,128)} async-done(((f32[3,511,512]{2,1,0:T(8,128)}), f32[3,511,512]{2,1,0:T(8,128)}) %all-reduce.5.cloned.1.call-update) | async-done | bytes 3139600 | tf_op jit(solution)/shard_map/psum | solution.py:115
  202.1 3.4 collective-permute-start.1
  208.1 262.1 %all-reduce.7.cloned.1.call-done = (f32[4,1,256,256]{3,2,0,1:T(8,128)}, f32[4,1,256,256]{3,2,0,1:T(8,128)}, f32[256,256]{1,0:T(8,128)}) async-done(((f32[4,1,256,256]{3,2,0,1:T(8,128)}, f32[4,1,256,256]{3,2,0,1:T(8,128)}, f32[256,256]{1,0:T(8,128)}), (f32[4,1,256,256]{3,2,0,1:T(8,128)}, f32[4,1,256,256]{3,2,0,1:T(8,128)}, f32[256,256]{1,0:T(8,128)})) %all-reduce.7.cloned.1.call-update) | async-done | bytes 2359312 | tf_op jit(solution)/shard_map/psum | solution.py:122
  (67 shorter events, 41.9 us)
Async XLA Ops:
  7.2 193.4 %all-reduce.5.cloned.1.call-start = ((), (), s32[]{:S(2)}) async-start(), calls=%async_computation | async-start | bytes 6291456 | tf_op jit(solution)/shard_map/psum | solution.py:115
  7.2 7.6 %copy-start.6 = (f32[4,2,256,256]{3,2,1,0:T(8,128)S(1)}, f32[4,2,256,256]{3,2,1,0:T(8,128)}, u32[]{:S(2)}) copy-start(f32[4,2,256,256]{3,2,1,0:T(8,128)} %param.6) | copy-start | bytes 6291460
  7.2 43.6 %collective-permute-start = (f32[2,255,512]{2,1,0:T(8,128)}, f32[2,255,512]{2,1,0:T(8,128)}, u32[]{:S(2)}, u32[]{:S(2)}) collective-permute-start(f32[2,255,512]{2,1,0:T(8,128)} %bitcast.185), channel_id=1, source_target_pairs={{8,0},{16,8},{24,16},{32,24},{40,32},{48,40},{56,48},{64,56},{72,6... | collective-permute-start | bytes 3133448 | tf_op jit(solution)/shard_map/ppermute | solution.py:16
  17.0 2.2 copy-start.14
  26.1 2.8 copy-start.3
  29.0 12.4 %copy-start = (f32[4,256,256]{2,1,0:T(8,128)}, f32[4,256,256]{2,1,0:T(8,128)S(1)}, u32[]{:S(2)}) copy-start(f32[4,256,256]{2,1,0:T(8,128)S(1)} %get-tuple-element.67) | copy-start | bytes 3145732
  34.2 3.9 copy-start.15
  48.0 2.8 copy-start.9
  52.2 0.8 copy-start.7
  70.2 2.9 copy-start.13
  102.3 3.1 copy-start.1
  102.3 3.1 copy-start.4
  125.0 345.1 %all-reduce.7.cloned.1.call-start = ((), (), s32[]{:S(2)}) async-start(), calls=%async_computation.1 | async-start | bytes 4718592 | tf_op jit(solution)/shard_map/psum | solution.py:122
  125.5 4.2 copy-start.2
  125.5 4.2 copy-start.5
  139.1 4.0 copy-start.8
  143.8 61.7 %copy-start.12 = (f32[256,256]{1,0:T(8,128)S(1)}, f32[256,256]{1,0:T(8,128)}, u32[]{:S(2)}) copy-start(f32[256,256]{1,0:T(8,128)} %get-tuple-element.69) | copy-start | bytes 786436
  202.1 272.3 %collective-permute-start.1 = (f32[3,255,512]{2,1,0:T(8,128)S(1)}, f32[3,255,512]{2,1,0:T(8,128)S(1)}, u32[]{:S(2)}, u32[]{:S(2)}) collective-permute-start(f32[3,255,512]{2,1,0:T(8,128)S(1)} %slice.69), channel_id=1, source_target_pairs={{0,8},{8,16},{16,24},{24,32},{32,40},{40,48},{48,56},{56,64},{64,7... | collective-permute-start | bytes 4700168 | tf_op jit(solution)/shard_map/ppermute | solution.py:16
  472.9 2.6 copy-start.11
  474.4 1.6 copy-start.10
Sparse Core Ops, SparseCore 0:
  125.1 75.3 all-reduce.4
  206.9 263.1 all-reduce.6
where the time goes:
time: 494 us; the launch traced here: 484 us
  waiting for transfers between devices  319 us (65%)
  matrix products  110 us (22%)
  between operations  18.6 us (4%)
  local copies, waits for them, and re-layouts  17.4 us (4%)
  other arithmetic  11.2 us (2%)
  starting transfers between devices  8.11 us (2%)
    psum x1, waiting for transfers between devices, on_device(): lax.psum((field_real, field_imag, mass), ('tile', 'batch'))  262 us
    psum x1, waiting for transfers between devices, on_device(): summed = lax.psum(totals, 'batch')  56.8 us
    dot_general x6, matrix products, right_apply(): jnp.einsum('kun,nv->kuv', data_real, mat_imag - mat_real, precision=highest)  20.4 us
    dot_general x6, matrix products, left_apply(): jnp.einsum('um,kmn->kun', mat_real + mat_imag, data_real, precision=highest)  19.6 us
    dot_general x6, matrix products, left_apply(): jnp.einsum('um,kmn->kun', mat_real, data_imag - data_real, precision=high...  18.9 us
    dot_general x6, matrix products, right_apply(): jnp.einsum('kun,nv->kuv', data_imag, mat_real + mat_imag, precision=highest)  18.3 us
    dot_general x6, matrix products, left_apply(): jnp.einsum('um,kmn->kun', mat_imag, data_real + data_imag, precision=high...  17.2 us
    dot_general x6, matrix products, right_apply(): jnp.einsum('kun,nv->kuv', data_real + data_imag, mat_real, precision=high...  15.8 us
  transfers between devices with their start and end apart: 4, of which 2 were waited for; matrix products, arithmetic and copies ran while one was open for 13% of the time, Pallas kernels for 0%

commit v1 on v0

v1 whole, which is shorter than its diff:
```python
import math

import jax
import jax.numpy as jnp
import ml_dtypes
import numpy as np
from jax import lax
from jax.experimental import pallas as pl
from jax.experimental.pallas import tpu as pltpu
from jax.sharding import Mesh
from jax.sharding import PartitionSpec as P

SIDE = 256
MODES = 4
WIDE = 2 * SIDE
full_turn = 2.0 * math.pi
amplitude_floor = 0.5
bf16 = jnp.bfloat16
f32 = jnp.float32

AXES = (("z", 8), ("y", 4), ("x", 4), ("c", 2))
TILE = ("z", "y")
BATCH = ("x", "c")
OWNERS = 8
ROWS = SIDE // OWNERS
PLANE = ("y", "x")
PARTS = 16


def numpy_split(matrix):
    high = matrix.astype(ml_dtypes.bfloat16)
    low = (matrix - high.astype(np.float64)).astype(ml_dtypes.bfloat16)
    return high, low


def right_block(real, imag):
    return np.block([[real, imag], [-imag, real]])


def left_block(real, imag):
    return np.block([[real, -imag], [imag, real]])


def right_three(real, imag):
    high, low = numpy_split(right_block(real, imag))
    return np.concatenate([high, high, low], axis=0)


def left_three(real, imag):
    high, low = numpy_split(left_block(real, imag))
    return np.concatenate([high, high, low], axis=1)


def tables():
    idx = np.arange(SIDE)
    forward = np.exp(-2j * np.pi * (idx[:, None] * idx[None, :] % SIDE) / SIDE) / math.sqrt(SIDE)
    backward = np.conj(forward)
    freq = (((idx + SIDE // 2) % SIDE) - SIDE // 2) / SIDE
    along_rows = backward @ (freq[:, None] * forward)
    along_cols = forward @ (freq[:, None] * backward)
    return forward, backward, along_rows, along_cols


def split(value):
    high = value.astype(bf16)
    low = (value - high.astype(f32)).astype(bf16)
    return high, low


def put_right(stage, row, real, imag):
    rows = slice(row, row + SIDE)
    for at, part in enumerate((real, imag)):
        high, low = split(part)
        stage[rows, at * SIDE : (at + 1) * SIDE] = high
        stage[rows, WIDE + at * SIDE : WIDE + (at + 1) * SIDE] = low
        stage[rows, 2 * WIDE + at * SIDE : 2 * WIDE + (at + 1) * SIDE] = high


def put_left(stage, col, real, imag):
    cols = slice(col, col + SIDE)
    for at, part in enumerate((real, imag)):
        high, low = split(part)
        stage[at * SIDE : (at + 1) * SIDE, cols] = high
        stage[WIDE + at * SIDE : WIDE + (at + 1) * SIDE, cols] = low
        stage[2 * WIDE + at * SIDE : 2 * WIDE + (at + 1) * SIDE, cols] = high


def product(left, right):
    return jnp.dot(left, right, preferred_element_type=f32)


def probe_kernel(
    corner_ref,
    shift_ref,
    probe_ref,
    fwd_real_ref,
    fwd_imag_ref,
    right_fwd_ref,
    right_bwd_ref,
    left_slope_ref,
    right_slope_ref,
    shifted_ref,
    slope_rows_ref,
    slope_cols_ref,
    left_adjoint_ref,
    right_adjoint_ref,
    stage,
    stage_left,
    wide,
    tall,
    left_shift,
    right_shift,
):
    lane = lax.broadcasted_iota(jnp.int32, (1, SIDE), 1)
    freq = (((lane + SIDE // 2) & (SIDE - 1)) - SIDE // 2).astype(f32) / SIDE

    def ramp(offset, shift):
        whole = ((offset * lane) & (SIDE - 1)).astype(f32) / SIDE
        turns = whole + shift * freq
        angle = -full_turn * (turns - jnp.floor(turns + 0.5))
        return jnp.cos(angle), jnp.sin(angle)

    rows_real, rows_imag = ramp(corner_ref[0, 0], shift_ref[0, 0])
    cols_real, cols_imag = ramp(corner_ref[0, 1], shift_ref[0, 1])
    fwd_real = fwd_real_ref[...]
    fwd_imag = fwd_imag_ref[...]
    for at, (real, imag, sign) in enumerate(
        (
            (rows_real, rows_imag, -1.0),
            (rows_real, -rows_imag, -1.0),
            (cols_real, cols_imag, 1.0),
            (cols_real, -cols_imag, 1.0),
        )
    ):
        mat_imag = sign * fwd_imag
        put_right(
            stage,
            at * SIDE,
            fwd_real * real - mat_imag * imag,
            fwd_real * imag + mat_imag * real,
        )
    wide[: 2 * SIDE] = product(stage[: 2 * SIDE], right_fwd_ref[...])
    wide[2 * SIDE :] = product(stage[2 * SIDE :], right_bwd_ref[...])

    def store_left(target, row):
        for at in range(2):
            high, low = split(wide[row : row + SIDE, at * SIDE : (at + 1) * SIDE])
            for third, part in enumerate((high, high, low)):
                base = third * WIDE
                if at == 0:
                    target[:SIDE, base : base + SIDE] = part
                    target[SIDE:, base + SIDE : base + WIDE] = part
                else:
                    target[SIDE:, base : base + SIDE] = part
                    target[:SIDE, base + SIDE : base + WIDE] = -part

    def store_right(target, row):
        for at in range(2):
            high, low = split(wide[row : row + SIDE, at * SIDE : (at + 1) * SIDE])
            for third, part in enumerate((high, high, low)):
                base = third * WIDE
                if at == 0:
                    target[base : base + SIDE, :SIDE] = part
                    target[base + SIDE : base + WIDE, SIDE:] = part
                else:
                    target[base : base + SIDE, SIDE:] = part
                    target[base + SIDE : base + WIDE, :SIDE] = -part

    store_left(left_shift, 0)
    store_left(left_adjoint_ref, SIDE)
    store_right(right_shift, 2 * SIDE)
    store_right(right_adjoint_ref, 3 * SIDE)

    for k in range(MODES):
        put_right(stage, k * SIDE, probe_ref[k, 0], probe_ref[k, 1])
        put_left(stage_left, k * SIDE, probe_ref[k, 0], probe_ref[k, 1])
    tall[...] = product(left_slope_ref[...], stage_left[...])
    for k in range(MODES):
        slope_rows_ref[k, 0] = tall[:SIDE, k * SIDE : (k + 1) * SIDE]
        slope_rows_ref[k, 1] = tall[SIDE:, k * SIDE : (k + 1) * SIDE]
    wide[...] = product(stage[...], right_slope_ref[...])
    for k in range(MODES):
        slope_cols_ref[k, 0] = wide[k * SIDE : (k + 1) * SIDE, :SIDE]
        slope_cols_ref[k, 1] = wide[k * SIDE : (k + 1) * SIDE, SIDE:]
    wide[...] = product(stage[...], right_shift[...])
    for k in range(MODES):
        rows = slice(k * SIDE, (k + 1) * SIDE)
        put_left(stage_left, k * SIDE, wide[rows, :SIDE], wide[rows, SIDE:])
    tall[...] = product(left_shift[...], stage_left[...])
    for k in range(MODES):
        shifted_ref[k, 0] = tall[:SIDE, k * SIDE : (k + 1) * SIDE]
        shifted_ref[k, 1] = tall[SIDE:, k * SIDE : (k + 1) * SIDE]


def pattern_kernel(
    corner_ref,
    core_ref,
    object_ref,
    near_ref,
    far_ref,
    amplitude_ref,
    shifted_ref,
    slope_rows_ref,
    slope_cols_ref,
    left_fwd_ref,
    right_fwd_ref,
    left_adjoint_ref,
    right_adjoint_ref,
    block_ref,
    keep_ref,
    send_ref,
    shift_grad_ref,
    stage,
    stage_left,
    wide,
    tall,
    exit_wave,
    patch,
    grads,
):
    core = core_ref[0, 0]
    row_start = corner_ref[0, 0] & (SIDE - 1)
    col_start = corner_ref[0, 1]
    half = SIDE // 2
    row_at = lax.broadcasted_iota(jnp.int32, (SIDE, SIDE), 0)
    col_at = lax.broadcasted_iota(jnp.int32, (SIDE, SIDE), 1)
    here = row_at >= row_start
    left = col_at >= col_start
    first = core == 0
    for part in range(2):
        own = jnp.where(left, object_ref[part, :, :SIDE], object_ref[part, :, SIDE:])
        near = near_ref[part]
        far = far_ref[part]
        rim = jnp.concatenate([jnp.where(first, near, far), jnp.where(first, far, near)], axis=0)
        rim = jnp.where(left, rim[:, :SIDE], rim[:, SIDE:])
        patch[part] = jnp.where(here, own, rim)

    for k in range(MODES):
        real, imag = shifted_ref[k, 0], shifted_ref[k, 1]
        exit_real = real * patch[0] - imag * patch[1]
        exit_imag = real * patch[1] + imag * patch[0]
        exit_wave[k, 0] = exit_real
        exit_wave[k, 1] = exit_imag
        put_right(stage, k * SIDE, exit_real, exit_imag)
    wide[...] = product(stage[...], right_fwd_ref[...])
    for k in range(MODES):
        rows = slice(k * SIDE, (k + 1) * SIDE)
        put_left(stage_left, k * SIDE, wide[rows, :SIDE], wide[rows, SIDE:])
    tall[...] = product(left_fwd_ref[...], stage_left[...])
    intensity = jnp.zeros((SIDE, SIDE), f32)
    for k in range(MODES):
        cols = slice(k * SIDE, (k + 1) * SIDE)
        real, imag = tall[:SIDE, cols], tall[SIDE:, cols]
        intensity = intensity + (real * real + imag * imag)
    ratio = amplitude_ref[0] / jnp.maximum(jnp.sqrt(intensity), amplitude_floor)
    for k in range(MODES):
        cols = slice(k * SIDE, (k + 1) * SIDE)
        put_left(stage_left, k * SIDE, tall[:SIDE, cols] * ratio, -(tall[SIDE:, cols] * ratio))
    tall[...] = product(left_fwd_ref[...], stage_left[...])
    for k in range(MODES):
        cols = slice(k * SIDE, (k + 1) * SIDE)
        put_right(stage, k * SIDE, tall[:SIDE, cols], tall[SIDE:, cols])
    wide[...] = product(stage[...], right_fwd_ref[...])

    num_real = jnp.zeros((SIDE, SIDE), f32)
    num_imag = jnp.zeros((SIDE, SIDE), f32)
    weight = jnp.zeros((SIDE, SIDE), f32)
    for k in range(MODES):
        rows = slice(k * SIDE, (k + 1) * SIDE)
        real, imag = shifted_ref[k, 0], shifted_ref[k, 1]
        change_real = wide[rows, :SIDE] - exit_wave[k, 0]
        change_imag = -wide[rows, SIDE:] - exit_wave[k, 1]
        num_real = num_real + (real * change_real + imag * change_imag)
        num_imag = num_imag + (real * change_imag - imag * change_real)
        weight = weight + (real * real + imag * imag)
        put_right(
            stage,
            k * SIDE,
            patch[0] * change_real + patch[1] * change_imag,
            patch[0] * change_imag - patch[1] * change_real,
        )
    tag = jnp.where(
        lax.broadcasted_iota(jnp.int32, (8, SIDE), 0) == 0, row_start, col_start
    ).astype(f32)
    for owner in range(OWNERS):
        rows = slice(owner * ROWS, (owner + 1) * ROWS)
        block_ref[owner, :ROWS] = num_real[rows]
        block_ref[owner, ROWS : 2 * ROWS] = num_imag[rows]
        block_ref[owner, 2 * ROWS : 3 * ROWS] = weight[rows]
        block_ref[owner, 3 * ROWS :] = tag

    wide[...] = product(stage[...], right_adjoint_ref[...])
    for k in range(MODES):
        rows = slice(k * SIDE, (k + 1) * SIDE)
        put_left(stage_left, k * SIDE, wide[rows, :SIDE], wide[rows, SIDE:])
    tall[...] = product(left_adjoint_ref[...], stage_left[...])
    row_dot = jnp.zeros((SIDE, SIDE), f32)
    col_dot = jnp.zeros((SIDE, SIDE), f32)
    for k in range(MODES):
        cols = slice(k * SIDE, (k + 1) * SIDE)
        real, imag = tall[:SIDE, cols], tall[SIDE:, cols]
        row_dot = row_dot + (real * slope_rows_ref[k, 1] - imag * slope_rows_ref[k, 0])
        col_dot = col_dot + (real * slope_cols_ref[k, 1] - imag * slope_cols_ref[k, 0])
        grads[2 * k] = real
        grads[2 * k + 1] = imag
    shift_grad_ref[0, 0] = full_turn / SIDE * jnp.sum(row_dot)
    shift_grad_ref[0, 1] = full_turn / SIDE * jnp.sum(col_dot)
    mass = patch[0] * patch[0] + patch[1] * patch[1]
    mass = pltpu.roll(mass, (SIDE - row_start) & (SIDE - 1), 0)
    grads[2 * MODES] = pltpu.roll(mass, (SIDE - col_start) & (SIDE - 1), 1)
    keep_rows = pl.multiple_of(core * half, half)
    send_rows = pl.multiple_of((1 - core) * half, half)
    for channel in range(2 * MODES + 1):
        for target, base in ((keep_ref, keep_rows), (send_ref, send_rows)):
            value = grads[channel, pl.ds(base, half), :]
            for part in range(PARTS):
                target[part, channel] = value[part * 8 : (part + 1) * 8]


def gather_kernel(owner_ref, blocks_ref, own_ref, spill_ref):
    base = owner_ref[0, 0] * ROWS
    row_at = (base + lax.broadcasted_iota(jnp.int32, (ROWS, SIDE), 0)).astype(f32)
    col_at = lax.broadcasted_iota(jnp.int32, (ROWS, SIDE), 1).astype(f32)
    zero = jnp.zeros((ROWS, SIDE), f32)
    for channel in range(3):
        sums = [zero, zero, zero, zero]
        for sender in range(OWNERS):
            value = blocks_ref[sender, channel * ROWS : (channel + 1) * ROWS]
            here = row_at >= blocks_ref[sender, 3 * ROWS : 3 * ROWS + 1]
            left = col_at >= blocks_ref[sender, 3 * ROWS + 1 : 3 * ROWS + 2]
            value_here = jnp.where(here, value, 0.0)
            value_next = jnp.where(here, 0.0, value)
            sums[0] = sums[0] + jnp.where(left, value_here, 0.0)
            sums[1] = sums[1] + jnp.where(left, 0.0, value_here)
            sums[2] = sums[2] + jnp.where(left, value_next, 0.0)
            sums[3] = sums[3] + jnp.where(left, 0.0, value_next)
        own_ref[channel, :, :SIDE] = sums[0]
        own_ref[channel, :, SIDE:] = sums[1]
        spill_ref[channel, :, :SIDE] = sums[2]
        spill_ref[channel, :, SIDE:] = sums[3]


VMEM = pl.BlockSpec(memory_space=pltpu.VMEM)
SMEM = pl.BlockSpec(memory_space=pltpu.SMEM)
LIMIT = 48 * 1024 * 1024


def on_device(object_field, probe_modes, amplitudes, positions, shifts):
    forward, backward, along_rows, along_cols = tables()
    fwd_real = jnp.asarray(forward.real.astype(np.float32))
    fwd_imag = jnp.asarray(forward.imag.astype(np.float32))
    right_fwd = jnp.asarray(right_three(forward.real, forward.imag))
    right_bwd = jnp.asarray(right_three(backward.real, backward.imag))
    left_fwd = jnp.asarray(left_three(forward.real, forward.imag))
    left_slope = jnp.asarray(left_three(along_rows.real, along_rows.imag))
    right_slope = jnp.asarray(right_three(along_cols.real, along_cols.imag))

    core = lax.axis_index("c")
    owner = lax.axis_index(BATCH)
    tiles = 32
    half = SIDE // 2

    part_rows = lax.dynamic_slice_in_dim(object_field, core * half, half, axis=1)
    near = lax.ppermute(part_rows, TILE, [(i + 1, i) for i in range(tiles - 1)])
    far = lax.ppermute(near, "c", [(0, 1), (1, 0)])

    field = jax.ShapeDtypeStruct((MODES, 2, SIDE, SIDE), f32)
    stages = [
        pltpu.VMEM((MODES * SIDE, 3 * WIDE), bf16),
        pltpu.VMEM((3 * WIDE, MODES * SIDE), bf16),
        pltpu.VMEM((MODES * SIDE, WIDE), f32),
        pltpu.VMEM((WIDE, MODES * SIDE), f32),
    ]
    shifted, slope_rows, slope_cols, left_adjoint, right_adjoint = pl.pallas_call(
        probe_kernel,
        out_shape=(
            field,
            field,
            field,
            jax.ShapeDtypeStruct((WIDE, 3 * WIDE), bf16),
            jax.ShapeDtypeStruct((3 * WIDE, WIDE), bf16),
        ),
        in_specs=[SMEM, SMEM] + [VMEM] * 7,
        out_specs=(VMEM,) * 5,
        scratch_shapes=stages
        + [pltpu.VMEM((WIDE, 3 * WIDE), bf16), pltpu.VMEM((3 * WIDE, WIDE), bf16)],
        compiler_params=pltpu.CompilerParams(vmem_limit_bytes=LIMIT),
        cost_estimate=pl.CostEstimate(
            flops=int(8e9), bytes_accessed=int(1.6e7), transcendentals=2048
        ),
    )(
        positions,
        shifts,
        probe_modes,
        fwd_real,
        fwd_imag,
        right_fwd,
        right_bwd,
        left_slope,
        right_slope,
    )

    blocks, keep, send, shift_grad = pl.pallas_call(
        pattern_kernel,
        out_shape=(
            jax.ShapeDtypeStruct((OWNERS, 3 * ROWS + 8, SIDE), f32),
            jax.ShapeDtypeStruct((PARTS, 2 * MODES + 1, 8, SIDE), f32),
            jax.ShapeDtypeStruct((PARTS, 2 * MODES + 1, 8, SIDE), f32),
            jax.ShapeDtypeStruct((1, 2), f32),
        ),
        in_specs=[SMEM, SMEM] + [VMEM] * 11,
        out_specs=(VMEM, VMEM, VMEM, SMEM),
        scratch_shapes=stages
        + [
            pltpu.VMEM((MODES, 2, SIDE, SIDE), f32),
            pltpu.VMEM((2, SIDE, SIDE), f32),
            pltpu.VMEM((2 * MODES + 1, SIDE, SIDE), f32),
        ],
        compiler_params=pltpu.CompilerParams(vmem_limit_bytes=LIMIT),
        cost_estimate=pl.CostEstimate(
            flops=int(1e10), bytes_accessed=int(2e7), transcendentals=65536
        ),
    )(
        positions,
        jnp.reshape(core, (1, 1)),
        object_field,
        near,
        far,
        amplitudes,
        shifted,
        slope_rows,
        slope_cols,
        left_fwd,
        right_fwd,
        left_adjoint,
        right_adjoint,
    )

    other = lax.ppermute(send, "c", [(0, 1), (1, 0)])
    received = lax.all_to_all(blocks, BATCH, 0, 0)
    own, spill = pl.pallas_call(
        gather_kernel,
        out_shape=(jax.ShapeDtypeStruct((3, ROWS, 2 * SIDE), f32),) * 2,
        in_specs=[SMEM, VMEM],
        out_specs=(VMEM, VMEM),
    )(jnp.reshape(owner, (1, 1)), received)
    spilled = lax.ppermute(spill, TILE, [(i, i + 1) for i in range(tiles - 1)])

    scattered = lax.all_to_all(keep + other, PLANE, 0, 0)
    owned = own + spilled
    strip_part = lax.dynamic_slice_in_dim(object_field, owner * ROWS, ROWS, axis=1)
    new_part = strip_part + owned[:2] / (owned[2] + 1.0)[None]
    new_object = lax.all_gather(new_part, BATCH, axis=1, tiled=True)

    column = jnp.sum(scattered, axis=0)
    columns = lax.all_to_all(jnp.broadcast_to(column[None], (8,) + column.shape), "z", 0, 0)
    total = jnp.sum(columns, axis=0)
    direction = total[: 2 * MODES] / jnp.sqrt(total[2 * MODES] + 1.0)[None]
    spread = lax.all_to_all(jnp.broadcast_to(direction[None], (PARTS,) + direction.shape), PLANE, 0, 0)
    swapped = lax.ppermute(spread, "c", [(0, 1), (1, 0)])
    top = jnp.where(core == 0, spread, swapped)
    bottom = jnp.where(core == 0, swapped, spread)
    rows = jnp.concatenate([top, bottom], axis=0)
    probe_direction = jnp.swapaxes(rows, 0, 1).reshape(MODES, 2, SIDE, SIDE)
    return (new_object, probe_direction, shift_grad)


def solution(mesh):
    names = tuple(name for name, _ in AXES)
    sizes = tuple(size for _, size in AXES)
    slice_mesh = Mesh(np.asarray(mesh.devices).reshape(sizes), names)
    return jax.shard_map(
        on_device,
        mesh=slice_mesh,
        in_specs=(
            P(None, TILE, None),
            P(),
            P(names, None, None),
            P(names, None),
            P(names, None),
        ),
        out_specs=(P(None, TILE, None), P(), P(names, None)),
        check_vma=False,
    )
```

time: 494 us -> 185 us (0.37)
  the two profiles are of different devices: /device:TPU:8 before, /device:TPU:1 now
where the time goes in v1:
time: 185 us; the launch traced here: 184 us
  waiting for transfers between devices  70.8 us (38%)
  Pallas kernels  32.2 us (17%)
  blocking collectives  26.9 us (15%)
  starting transfers between devices  25.5 us (14%)
  between operations  14.2 us (8%)
  local copies, waits for them, and re-layouts  11.1 us (6%)
  other arithmetic  3.7 us (2%)
    all_to_all x1, blocking collectives, on_device(): scattered = lax.all_to_all(keep + other, PLANE, 0, 0)  26.9 us
    pallas_call x1, Pallas kernels, on_device(): pl.pallas_call(pattern_kernel, out_shape=(jax.ShapeDtypeStruct((OWNERS, 3...  17.1 us
    all_to_all x1, waiting for transfers between devices, on_device(): lax.all_to_all(jnp.broadcast_to(direction[None], (PARTS,) + direction.sha...  15.8 us
    all_to_all x1, waiting for transfers between devices, on_device(): received = lax.all_to_all(blocks, BATCH, 0, 0)  12.9 us
    pallas_call x1, Pallas kernels, on_device(): pl.pallas_call(probe_kernel, out_shape=(field, field, field, jax.ShapeDty...  12.8 us
    all_gather x1, waiting for transfers between devices, on_device(): new_object = lax.all_gather(new_part, BATCH, axis=1, tiled=True)  12.7 us
    ppermute x1, waiting for transfers between devices, on_device(): near = lax.ppermute(part_rows, TILE, [(i + 1, i) for i in range(tiles - 1)])  12.1 us
    all_to_all x1, waiting for transfers between devices, on_device(): lax.all_to_all(jnp.broadcast_to(column[None], (8,) + column.shape), 'z',...  11 us
  transfers between devices with their start and end apart: 9, of which 7 were waited for; matrix products, arithmetic and copies ran while one was open for 1% of the time, Pallas kernels for 8%

profile of v1, /device:TPU:1, one launch (start us, length us, event | category | flops | bytes accessed | tf_op | source)
XLA Modules:
  0.0 184.4 jit_solution(8799429285353558879)
XLA Ops:
  7.2 1.1 constant_dynamic-slice_fusion
  8.3 1.4 collective-permute-start
  9.7 12.1 %collective-permute-done.near_ref = f32[2,128,512]{2,1,0:T(8,128)S(1)} collective-permute-done((f32[2,128,512]{2,1,0:T(8,128)S(1)}, f32[2,128,512]{2,1,0:T(8,128)S(1)}, u32[]{:S(2)}, u32[]{:S(2)}) %collective-permute-start) | collective-permute-done | bytes 524320 | tf_op jit(solution)/shard_map/ppermute | solution.py:364
  21.8 3.5 %collective-permute-start.1 = (f32[2,128,512]{2,1,0:T(8,128)S(1)}, f32[2,128,512]{2,1,0:T(8,128)S(1)}, u32[]{:S(2)}, u32[]{:S(2)}) collective-permute-start(f32[2,128,512]{2,1,0:T(8,128)S(1)} %collective-permute-done.near_ref), channel_id=1, source_target_pairs={{0,1},{1,0},{2,3},{3,2},{4,5},{5,4},{6,7},{7,6},{8,9},{9,8},{10,11... | collective-permute-start | bytes 1572872 | tf_op jit(solution)/shard_map/ppermute | solution.py:365
  25.3 0.7 copy-done.2
  26.0 0.7 copy-done.3
  26.6 1.4 copy-done.4
  28.0 0.9 copy-done.5
  29.0 0.9 copy-done.6
  29.9 12.8 %shard_map.139 = (f32[4,2,256,256]{3,2,1,0:T(8,128)}, f32[4,2,256,256]{3,2,1,0:T(8,128)}, f32[4,2,256,256]{3,2,1,0:T(8,128)}, bf16[512,1536]{1,0:T(8,128)(2,1)S(1)}, bf16[1536,512]{1,0:T(8,128)(2,1)S(1)}) custom-call(s32[1,2]{1,0:T(1,128)S(1)} %copy-done.3, f32[1,2]{1,0:T(1,128)S(1)} %copy-done.2, f32[4,2,256,256]{3,2,1,0:T(8,128)} %probe_ref.1, ...), custom_call_target="tpu_custom_call" | custom-call | flops 8000000000 | bytes 16000000 | tf_op jit(solution)/shard_map/pallas_call | solution.py:374
  42.8 1.2 copy-done.7
  44.0 1.2 copy-done.8
  45.1 17.1 %shard_map.140 = (f32[8,104,256]{2,1,0:T(8,128)}, f32[16,9,8,256]{3,2,1,0:T(8,128)S(1)}, f32[16,9,8,256]{3,2,1,0:T(8,128)S(1)}, f32[1,2]{1,0:T(1,128)}) custom-call(s32[1,2]{1,0:T(1,128)S(1)} %copy-done.3, s32[1,1]{1,0:T(1,128)} %bitcast.1.core_ref, f32[2,256,512]{2,1,0:T(8,128)S(1)} %copy-done, f32[2,128,512]{2,1,0:T(8,128)S(1)} %collective-permute-done.near_ref, ...), custom_call_target="tpu_custom_call" | custom-call | flops 10000000000 | bytes 20000000 | tf_op jit(solution)/shard_map/pallas_call | solution.py:403
  62.4 2.8 %collective-permute-done.3 = f32[16,9,8,256]{3,2,1,0:T(8,128)S(1)} collective-permute-done((f32[16,9,8,256]{3,2,1,0:T(8,128)S(1)}, f32[16,9,8,256]{3,2,1,0:T(8,128)S(1)}, u32[]{:S(2)}, u32[]{:S(2)}) %collective-permute-start.3) | collective-permute-done | bytes 1179680 | tf_op jit(solution)/shard_map/ppermute | solution.py:439
  65.4 26.9 %all_to_all.20 = f32[16,9,8,256]{3,2,1,0:T(8,128)S(1)} all-to-all(f32[16,9,8,256]{3,2,1,0:T(8,128)S(1)} %add.39), channel_id=1, replica_groups=mesh['z'=8,'y'=4,'x'=4,'c'=2] {'y','x'}, dimensions={0} | all-to-all | bytes 2359296 | tf_op jit(solution)/shard_map/all_to_all | solution.py:449
  92.3 4.7 %all-to-all-start = ((f32[8,104,256]{2,1,0:T(8,128)}), f32[8,104,256]{2,1,0:T(8,128)S(1)}, u32[]{:S(2)}, u32[]{:S(2)}) async-start(f32[8,104,256]{2,1,0:T(8,128)} %get-tuple-element.19), calls=%async_computation | async-start | bytes 1703936 | tf_op jit(solution)/shard_map/all_to_all | solution.py:440
  97.1 12.9 %all-to-all-done.blocks_ref = f32[8,104,256]{2,1,0:T(8,128)S(1)} async-done(((f32[8,104,256]{2,1,0:T(8,128)}), f32[8,104,256]{2,1,0:T(8,128)S(1)}, u32[]{:S(2)}, u32[]{:S(2)}) %all-to-all-start) | async-done | bytes 852000 | tf_op jit(solution)/shard_map/all_to_all | solution.py:440
  110.0 0.9 broadcast_in_dim.4
  111.0 8.2 %all-to-all-start.2 = ((f32[8,9,8,256]{3,2,1,0:T(8,128)}), f32[8,9,8,256]{3,2,1,0:T(8,128)S(1)}, u32[]{:S(2)}, u32[]{:S(2)}) async-start(f32[8,9,8,256]{3,2,1,0:T(8,128)} %broadcast_in_dim.4), calls=%async_computation.2 | async-start | bytes 1179648 | tf_op jit(solution)/shard_map/all_to_all | solution.py:456
  119.2 2.2 %shard_map.141 = (f32[3,32,512]{2,1,0:T(8,128)}, f32[3,32,512]{2,1,0:T(8,128)}) custom-call(s32[1,1]{1,0:T(1,128)} %bitcast.owner_ref, f32[8,104,256]{2,1,0:T(8,128)} %copy-done.9), custom_call_target="tpu_custom_call" | custom-call | tf_op jit(solution)/shard_map/pallas_call | solution.py:441
  121.4 1.9 %collective-permute-start.2 = (f32[3,32,512]{2,1,0:T(8,128)}, f32[3,32,512]{2,1,0:T(8,128)S(1)}, u32[]{:S(2)}, u32[]{:S(2)}) collective-permute-start(f32[3,32,512]{2,1,0:T(8,128)} %get-tuple-element.21), channel_id=1, source_target_pairs={{0,8},{8,16},{16,24},{24,32},{32,40},{40,48},{48,56},{56,64},{64,7... | collective-permute-start | bytes 589832 | tf_op jit(solution)/shard_map/ppermute | solution.py:447
  123.3 3.3 %collective-permute-done.2 = f32[3,32,512]{2,1,0:T(8,128)S(1)} collective-permute-done((f32[3,32,512]{2,1,0:T(8,128)}, f32[3,32,512]{2,1,0:T(8,128)S(1)}, u32[]{:S(2)}, u32[]{:S(2)}) %collective-permute-start.2) | collective-permute-done | bytes 196640 | tf_op jit(solution)/shard_map/ppermute | solution.py:447
  126.6 1.0 add.35
  127.6 11.0 %all-to-all-done.2 = f32[8,9,8,256]{3,2,1,0:T(8,128)S(1)} async-done(((f32[8,9,8,256]{3,2,1,0:T(8,128)}), f32[8,9,8,256]{3,2,1,0:T(8,128)S(1)}, u32[]{:S(2)}, u32[]{:S(2)}) %all-to-all-start.2) | async-done | bytes 589856 | tf_op jit(solution)/shard_map/all_to_all | solution.py:456
  138.6 1.1 broadcast_in_dim.5
  139.7 3.7 %all-to-all-start.3 = ((f32[16,8,8,256]{3,2,1,0:T(8,128)}), f32[16,8,8,256]{3,2,1,0:T(8,128)S(1)}, u32[]{:S(2)}, u32[]{:S(2)}) async-start(f32[16,8,8,256]{3,2,1,0:T(8,128)} %broadcast_in_dim.5), calls=%async_computation.3 | async-start | bytes 2097152 | tf_op jit(solution)/shard_map/all_to_all | solution.py:459
  143.4 0.7 fusion
  144.1 15.8 %all-to-all-done.3 = f32[16,8,8,256]{3,2,1,0:T(8,128)S(1)} async-done(((f32[16,8,8,256]{3,2,1,0:T(8,128)}), f32[16,8,8,256]{3,2,1,0:T(8,128)S(1)}, u32[]{:S(2)}, u32[]{:S(2)}) %all-to-all-start.3) | async-done | bytes 1048608 | tf_op jit(solution)/shard_map/all_to_all | solution.py:459
  160.0 2.0 %collective-permute-start.4 = (f32[16,8,8,256]{3,2,0,1:T(8,128)S(1)}, f32[16,8,8,256]{3,2,0,1:T(8,128)S(1)}, u32[]{:S(2)}, u32[]{:S(2)}) collective-permute-start(f32[16,8,8,256]{3,2,0,1:T(8,128)S(1)} %copy.19), channel_id=1, source_target_pairs={{0,1},{1,0},{2,3},{3,2},{4,5},{5,4},{6,7},{7,6},{8,9},{9,8},{10,11... | collective-permute-start | bytes 3145736 | tf_op jit(solution)/shard_map/ppermute | solution.py:460
  162.0 12.7 %all-gather.2.cloned.1.call-done = f32[2,256,512]{2,1,0:T(8,128)} async-done(((f32[2,32,512]{2,1,0:T(8,128)}), f32[2,256,512]{2,1,0:T(8,128)}) %all-gather.2.cloned.1.call-update) | async-done | bytes 1048592 | tf_op jit(solution)/shard_map/all_gather | solution.py:453
  175.0 1.5 pad_maximum_fusion
  176.5 1.0 copy.24
  (28 shorter events, 0.8 us)
Async XLA Ops:
  8.3 36.9 %copy-start = (f32[2,256,512]{2,1,0:T(8,128)S(1)}, f32[2,256,512]{2,1,0:T(8,128)}, u32[]{:S(2)}) copy-start(f32[2,256,512]{2,1,0:T(8,128)} %object_ref.1) | copy-start | bytes 3145732
  8.3 36.9 %copy-start.1 = (f32[1,256,256]{2,1,0:T(8,128)S(1)}, f32[1,256,256]{2,1,0:T(8,128)}, u32[]{:S(2)}) copy-start(f32[1,256,256]{2,1,0:T(8,128)} %amplitude_ref.1) | copy-start | bytes 786436
  8.3 13.5 %collective-permute-start = (f32[2,128,512]{2,1,0:T(8,128)S(1)}, f32[2,128,512]{2,1,0:T(8,128)S(1)}, u32[]{:S(2)}, u32[]{:S(2)}) collective-permute-start(f32[2,128,512]{2,1,0:T(8,128)S(1)} %constant_dynamic-slice_fusion), channel_id=1, source_target_pairs={{8,0},{16,8},{24,16},{32,24},{40,32},{48,40},{56,48},{64,56},{72,6... | collective-permute-start | bytes 1572872 | tf_op jit(solution)/shard_map/ppermute | solution.py:364
  21.8 23.3 %collective-permute-start.1 = (f32[2,128,512]{2,1,0:T(8,128)S(1)}, f32[2,128,512]{2,1,0:T(8,128)S(1)}, u32[]{:S(2)}, u32[]{:S(2)}) collective-permute-start(f32[2,128,512]{2,1,0:T(8,128)S(1)} %collective-permute-done.near_ref), channel_id=1, source_target_pairs={{0,1},{1,0},{2,3},{3,2},{4,5},{5,4},{6,7},{7,6},{8,9},{9,8},{10,11... | collective-permute-start | bytes 1572872 | tf_op jit(solution)/shard_map/ppermute | solution.py:365
  25.3 0.7 copy-start.2
  26.0 0.7 copy-start.3
  26.6 1.4 copy-start.4
  28.0 0.9 copy-start.5
  29.0 0.9 copy-start.6
  42.8 1.2 copy-start.7
  44.0 1.2 copy-start.8
  62.3 2.9 %collective-permute-start.3 = (f32[16,9,8,256]{3,2,1,0:T(8,128)S(1)}, f32[16,9,8,256]{3,2,1,0:T(8,128)S(1)}, u32[]{:S(2)}, u32[]{:S(2)}) collective-permute-start(f32[16,9,8,256]{3,2,1,0:T(8,128)S(1)} %get-tuple-element.23), channel_id=1, source_target_pairs={{0,1},{1,0},{2,3},{3,2},{4,5},{5,4},{6,7},{7,6},{8,9},{9,8},{10,11... | collective-permute-start | bytes 3538952 | tf_op jit(solution)/shard_map/ppermute | solution.py:439
  92.3 17.7 %all-to-all-start = ((f32[8,104,256]{2,1,0:T(8,128)}), f32[8,104,256]{2,1,0:T(8,128)S(1)}, u32[]{:S(2)}, u32[]{:S(2)}) async-start(f32[8,104,256]{2,1,0:T(8,128)} %get-tuple-element.19), calls=%async_computation | async-start | bytes 1703936 | tf_op jit(solution)/shard_map/all_to_all | solution.py:440
  110.0 9.2 %copy-start.9 = (f32[8,104,256]{2,1,0:T(8,128)}, f32[8,104,256]{2,1,0:T(8,128)S(1)}, u32[]{:S(2)}) copy-start(f32[8,104,256]{2,1,0:T(8,128)S(1)} %all-to-all-done.blocks_ref) | copy-start | bytes 2555908
  111.0 27.6 %all-to-all-start.2 = ((f32[8,9,8,256]{3,2,1,0:T(8,128)}), f32[8,9,8,256]{3,2,1,0:T(8,128)S(1)}, u32[]{:S(2)}, u32[]{:S(2)}) async-start(f32[8,9,8,256]{3,2,1,0:T(8,128)} %broadcast_in_dim.4), calls=%async_computation.2 | async-start | bytes 1179648 | tf_op jit(solution)/shard_map/all_to_all | solution.py:456
  121.4 5.2 %collective-permute-start.2 = (f32[3,32,512]{2,1,0:T(8,128)}, f32[3,32,512]{2,1,0:T(8,128)S(1)}, u32[]{:S(2)}, u32[]{:S(2)}) collective-permute-start(f32[3,32,512]{2,1,0:T(8,128)} %get-tuple-element.21), channel_id=1, source_target_pairs={{0,8},{8,16},{16,24},{24,32},{32,40},{40,48},{48,56},{56,64},{64,7... | collective-permute-start | bytes 589832 | tf_op jit(solution)/shard_map/ppermute | solution.py:447
  139.7 20.2 %all-to-all-start.3 = ((f32[16,8,8,256]{3,2,1,0:T(8,128)}), f32[16,8,8,256]{3,2,1,0:T(8,128)S(1)}, u32[]{:S(2)}, u32[]{:S(2)}) async-start(f32[16,8,8,256]{3,2,1,0:T(8,128)} %broadcast_in_dim.5), calls=%async_computation.3 | async-start | bytes 2097152 | tf_op jit(solution)/shard_map/all_to_all | solution.py:459
  143.4 31.4 %all-gather.2.cloned.1.call-start = ((), (), s32[]{:S(2)}) async-start(), calls=%async_computation.4 | async-start | bytes 1179648 | tf_op jit(solution)/shard_map/all_gather | solution.py:453
  160.0 14.7 %collective-permute-start.4 = (f32[16,8,8,256]{3,2,0,1:T(8,128)S(1)}, f32[16,8,8,256]{3,2,0,1:T(8,128)S(1)}, u32[]{:S(2)}, u32[]{:S(2)}) collective-permute-start(f32[16,8,8,256]{3,2,0,1:T(8,128)S(1)} %copy.19), channel_id=1, source_target_pairs={{0,1},{1,0},{2,3},{3,2},{4,5},{5,4},{6,7},{7,6},{8,9},{9,8},{10,11... | collective-permute-start | bytes 3145736 | tf_op jit(solution)/shard_map/ppermute | solution.py:460
  175.0 1.5 copy-start.10
Sparse Core Ops, SparseCore 0:
  146.6 28.0 all-gather.1

commit v2 on v0

v2 whole, which is shorter than its diff:
```python
import math

import jax
import jax.numpy as jnp
import numpy as np
from jax import lax
from jax.experimental import pallas as pl
from jax.experimental.pallas import tpu as pltpu
from jax.sharding import Mesh
from jax.sharding import PartitionSpec as P

SIDE = 256
MODES = 4
WIDE = 2 * SIDE
full_turn = 2.0 * math.pi
amplitude_floor = 0.5
bf16 = jnp.bfloat16
f32 = jnp.float32

AXES = (("zh", 4), ("zl", 2), ("y", 4), ("x", 4), ("c", 2))
TILE = ("zh", "zl", "y")
BATCH = ("x", "c")
OWNERS = 8
ROWS = SIDE // OWNERS
PLANE = ("zl", "y", "x")
PARTS = 32
LANES = 128


def tables():
    idx = np.arange(SIDE)
    forward = np.exp(-2j * np.pi * (idx[:, None] * idx[None, :] % SIDE) / SIDE) / math.sqrt(SIDE)
    backward = np.conj(forward)
    freq = (((idx + SIDE // 2) % SIDE) - SIDE // 2) / SIDE
    slope = backward @ (freq[:, None] * forward)
    return forward, slope


def two_parts(matrix):
    return np.stack([matrix.real, matrix.imag]).astype(np.float32)


def split(value):
    high = value.astype(bf16)
    low = (value - high.astype(f32)).astype(bf16)
    return high, low


def put_right(stage, row, real, imag):
    rows = slice(row, row + SIDE)
    for at, part in enumerate((real, imag)):
        high, low = split(part)
        stage[rows, at * SIDE : (at + 1) * SIDE] = high
        stage[rows, WIDE + at * SIDE : WIDE + (at + 1) * SIDE] = low


def put_left(stage, col, real, imag):
    cols = slice(col, col + SIDE)
    for at, part in enumerate((real, imag)):
        high, low = split(part)
        stage[at * SIDE : (at + 1) * SIDE, cols] = high
        stage[WIDE + at * SIDE : WIDE + (at + 1) * SIDE, cols] = low


def from_right(stage, matrix):
    fields = jnp.concatenate([stage[...], stage[:, :WIDE]], axis=1)
    return jnp.dot(fields, matrix[...], preferred_element_type=f32)


def from_left(matrix, stage):
    fields = jnp.concatenate([stage[...], stage[:WIDE]], axis=0)
    return jnp.dot(matrix[...], fields, preferred_element_type=f32)


def fill_left(target, real, imag):
    for at, value in enumerate((real, imag)):
        high, low = split(value)
        for third, part in enumerate((high, high, low)):
            base = third * WIDE
            if at == 0:
                target[:SIDE, base : base + SIDE] = part
                target[SIDE:, base + SIDE : base + WIDE] = part
            else:
                target[SIDE:, base : base + SIDE] = part
                target[:SIDE, base + SIDE : base + WIDE] = -part


def fill_right(target, real, imag):
    for at, value in enumerate((real, imag)):
        high, low = split(value)
        for third, part in enumerate((high, high, low)):
            base = third * WIDE
            if at == 0:
                target[base : base + SIDE, :SIDE] = part
                target[base + SIDE : base + WIDE, SIDE:] = part
            else:
                target[base : base + SIDE, SIDE:] = part
                target[base + SIDE : base + WIDE, :SIDE] = -part


def right_to_left(wide, stage_left):
    for k in range(MODES):
        rows = slice(k * SIDE, (k + 1) * SIDE)
        put_left(stage_left, k * SIDE, wide[rows, :SIDE], wide[rows, SIDE:])


def probe_kernel(
    corner_ref,
    shift_ref,
    probe_ref,
    forward_ref,
    shifted_ref,
    adjoint_ref,
    stage,
    stage_left,
    wide,
    tall,
    matrix_right,
    matrix_left,
):
    lane = lax.broadcasted_iota(jnp.int32, (1, SIDE), 1)
    freq = (((lane + SIDE // 2) & (SIDE - 1)) - SIDE // 2).astype(f32) / SIDE

    def ramp(offset, shift):
        whole = ((offset * lane) & (SIDE - 1)).astype(f32) / SIDE
        turns = whole + shift * freq
        angle = -full_turn * (turns - jnp.floor(turns + 0.5))
        return jnp.cos(angle), jnp.sin(angle)

    rows_real, rows_imag = ramp(corner_ref[0, 0], shift_ref[0, 0])
    cols_real, cols_imag = ramp(corner_ref[0, 1], shift_ref[0, 1])
    fwd_real = forward_ref[0]
    fwd_imag = forward_ref[1]
    for at, (real, imag) in enumerate(
        (
            (rows_real, rows_imag),
            (rows_real, -rows_imag),
            (cols_real, cols_imag),
            (cols_real, -cols_imag),
        )
    ):
        put_right(
            stage,
            at * SIDE,
            fwd_real * real + fwd_imag * imag,
            fwd_real * imag - fwd_imag * real,
        )
    fill_right(matrix_right, fwd_real, fwd_imag)
    wide[...] = from_right(stage, matrix_right)
    fill_left(matrix_left, wide[:SIDE, :SIDE], wide[:SIDE, SIDE:])
    adjoint_ref[0] = wide[SIDE : 2 * SIDE, :SIDE]
    adjoint_ref[1] = wide[SIDE : 2 * SIDE, SIDE:]
    adjoint_ref[2] = wide[2 * SIDE : 3 * SIDE, :SIDE]
    adjoint_ref[3] = -wide[2 * SIDE : 3 * SIDE, SIDE:]
    fill_right(matrix_right, wide[3 * SIDE :, :SIDE], -wide[3 * SIDE :, SIDE:])

    for k in range(MODES):
        put_right(stage, k * SIDE, probe_ref[k, 0], probe_ref[k, 1])
    wide[...] = from_right(stage, matrix_right)
    right_to_left(wide, stage_left)
    tall[...] = from_left(matrix_left, stage_left)
    for k in range(MODES):
        cols = slice(k * SIDE, (k + 1) * SIDE)
        shifted_ref[k, 0] = tall[:SIDE, cols]
        shifted_ref[k, 1] = tall[SIDE:, cols]


def partner(owner, steps, turn):
    return (((owner >> 1) + steps) & 3) * 2 + ((owner & 1) ^ turn)


def place(piece):
    row, lane = piece // 2 * 8, piece % 2 * LANES
    return slice(row, row + 8), slice(lane, lane + LANES)


def scatter(target, channel, value):
    for piece in range(PARTS):
        rows, lanes = place(piece)
        target[piece, channel] = value[rows, lanes]


def pattern_kernel(
    corner_ref,
    owner_ref,
    object_ref,
    near_ref,
    far_ref,
    amplitude_ref,
    shifted_ref,
    forward_ref,
    *rest,
):
    block_refs = rest[:4]
    staged_ref, mass_ref = rest[4:6]
    stage, stage_left, wide, tall, exit_wave, patch, left_fwd, right_fwd, nums = rest[6:]
    fill_right(right_fwd, forward_ref[0], forward_ref[1])
    fill_left(left_fwd, forward_ref[0], forward_ref[1])
    owner = owner_ref[0, 0]
    core = owner & 1
    row_start = corner_ref[0, 0] & (SIDE - 1)
    col_start = corner_ref[0, 1]
    row_at = lax.broadcasted_iota(jnp.int32, (SIDE, SIDE), 0)
    col_at = lax.broadcasted_iota(jnp.int32, (SIDE, SIDE), 1)
    here = row_at >= row_start
    left = col_at >= col_start
    first = core == 0
    for part in range(2):
        own = jnp.where(left, object_ref[part, :, :SIDE], object_ref[part, :, SIDE:])
        near = near_ref[part]
        far = far_ref[part]
        rim = jnp.concatenate([jnp.where(first, near, far), jnp.where(first, far, near)], axis=0)
        rim = jnp.where(left, rim[:, :SIDE], rim[:, SIDE:])
        patch[part] = jnp.where(here, own, rim)

    for k in range(MODES):
        real, imag = shifted_ref[k, 0], shifted_ref[k, 1]
        exit_real = real * patch[0] - imag * patch[1]
        exit_imag = real * patch[1] + imag * patch[0]
        exit_wave[k, 0] = exit_real
        exit_wave[k, 1] = exit_imag
        put_right(stage, k * SIDE, exit_real, exit_imag)
    wide[...] = from_right(stage, right_fwd)
    right_to_left(wide, stage_left)
    tall[...] = from_left(left_fwd, stage_left)
    intensity = jnp.zeros((SIDE, SIDE), f32)
    for k in range(MODES):
        cols = slice(k * SIDE, (k + 1) * SIDE)
        real, imag = tall[:SIDE, cols], tall[SIDE:, cols]
        intensity = intensity + (real * real + imag * imag)
    ratio = amplitude_ref[0] / jnp.maximum(jnp.sqrt(intensity), amplitude_floor)
    for k in range(MODES):
        cols = slice(k * SIDE, (k + 1) * SIDE)
        put_left(stage_left, k * SIDE, tall[:SIDE, cols] * ratio, -(tall[SIDE:, cols] * ratio))
    tall[...] = from_left(left_fwd, stage_left)
    for k in range(MODES):
        cols = slice(k * SIDE, (k + 1) * SIDE)
        put_right(stage, k * SIDE, tall[:SIDE, cols], tall[SIDE:, cols])
    wide[...] = from_right(stage, right_fwd)

    num_real = jnp.zeros((SIDE, SIDE), f32)
    num_imag = jnp.zeros((SIDE, SIDE), f32)
    weight = jnp.zeros((SIDE, SIDE), f32)
    for k in range(MODES):
        rows = slice(k * SIDE, (k + 1) * SIDE)
        real, imag = shifted_ref[k, 0], shifted_ref[k, 1]
        change_real = wide[rows, :SIDE] - exit_wave[k, 0]
        change_imag = -wide[rows, SIDE:] - exit_wave[k, 1]
        num_real = num_real + (real * change_real + imag * change_imag)
        num_imag = num_imag + (real * change_imag - imag * change_real)
        weight = weight + (real * real + imag * imag)
        put_right(
            staged_ref,
            k * SIDE,
            patch[0] * change_real + patch[1] * change_imag,
            patch[0] * change_imag - patch[1] * change_real,
        )
    nums[0] = num_real
    nums[1] = num_imag
    nums[2] = weight
    tag = jnp.where(
        lax.broadcasted_iota(jnp.int32, (8, SIDE), 0) == 0, row_start, col_start
    ).astype(f32)
    for steps, block_ref in enumerate(block_refs):
        for turn in range(2):
            base = pl.multiple_of(partner(owner, steps, turn) * ROWS, ROWS)
            for channel in range(3):
                rows = slice(channel * ROWS, (channel + 1) * ROWS)
                block_ref[turn, rows] = nums[channel, pl.ds(base, ROWS), :]
            block_ref[turn, 3 * ROWS :] = tag
    mass_ref[...] = patch[0] * patch[0] + patch[1] * patch[1]


def adjoint_kernel(
    corner_ref,
    owner_ref,
    staged_ref,
    mass_ref,
    adjoint_ref,
    keep_ref,
    send_ref,
    stage_left,
    wide,
    tall,
    matrix_left,
    matrix_right,
    mass,
):
    core = owner_ref[0, 0] & 1
    row_start = corner_ref[0, 0] & (SIDE - 1)
    col_start = corner_ref[0, 1]
    half = SIDE // 2
    fill_right(matrix_right, adjoint_ref[2], adjoint_ref[3])
    wide[...] = from_right(staged_ref, matrix_right)
    fill_left(matrix_left, adjoint_ref[0], adjoint_ref[1])
    right_to_left(wide, stage_left)
    tall[...] = from_left(matrix_left, stage_left)
    turned = pltpu.roll(mass_ref[...], (SIDE - row_start) & (SIDE - 1), 0)
    mass[...] = pltpu.roll(turned, (SIDE - col_start) & (SIDE - 1), 1)
    for target, at in ((keep_ref, core), (send_ref, 1 - core)):
        base = pl.multiple_of(at * half, half)
        for k in range(MODES):
            cols = slice(k * SIDE, (k + 1) * SIDE)
            for part in range(2):
                rows = pl.multiple_of(base + part * SIDE, half)
                scatter(target, 2 * k + part, tall[pl.ds(rows, half), cols])
        scatter(target, 2 * MODES, mass[pl.ds(base, half), :])


def slope_kernel(
    core_ref,
    probe_ref,
    slope_ref,
    keep_ref,
    send_ref,
    shift_grad_ref,
    stage,
    stage_left,
    wide,
    tall,
    matrix_left,
    matrix_right,
):
    first = core_ref[0, 0] == 0
    slope_real = slope_ref[0]
    slope_imag = slope_ref[1]
    fill_left(matrix_left, slope_real, slope_imag)
    fill_right(matrix_right, slope_real.T, slope_imag.T)
    for k in range(MODES):
        put_right(stage, k * SIDE, probe_ref[k, 0], probe_ref[k, 1])
        put_left(stage_left, k * SIDE, probe_ref[k, 0], probe_ref[k, 1])
    tall[...] = from_left(matrix_left, stage_left)
    wide[...] = from_right(stage, matrix_right)
    row_dot = jnp.zeros((8, LANES), f32)
    col_dot = jnp.zeros((8, LANES), f32)
    for piece in range(2 * PARTS):
        top = piece < PARTS
        rows, lanes = place(piece)
        for k in range(MODES):
            kept = [keep_ref[piece % PARTS, 2 * k + part] for part in range(2)]
            sent = [send_ref[piece % PARTS, 2 * k + part] for part in range(2)]
            real, imag = [
                jnp.where(first, a, b) if top else jnp.where(first, b, a)
                for a, b in zip(kept, sent)
            ]
            down = slice(rows.start + SIDE, rows.stop + SIDE)
            over = slice(lanes.start + k * SIDE, lanes.stop + k * SIDE)
            across = slice(rows.start + k * SIDE, rows.stop + k * SIDE)
            wider = slice(lanes.start + SIDE, lanes.stop + SIDE)
            row_dot = row_dot + (real * tall[down, over] - imag * tall[rows, over])
            col_dot = col_dot + (real * wide[across, wider] - imag * wide[across, lanes])
    shift_grad_ref[0, 0] = full_turn / SIDE * jnp.sum(row_dot)
    shift_grad_ref[0, 1] = full_turn / SIDE * jnp.sum(col_dot)


def gather_kernel(owner_ref, *rest):
    own_ref, spill_ref = rest[OWNERS:]
    base = owner_ref[0, 0] * ROWS
    row_at = (base + lax.broadcasted_iota(jnp.int32, (ROWS, SIDE), 0)).astype(f32)
    col_at = lax.broadcasted_iota(jnp.int32, (ROWS, SIDE), 1).astype(f32)
    sums = [[jnp.zeros((ROWS, SIDE), f32) for _ in range(4)] for _ in range(3)]
    for sender in range(OWNERS):
        block_ref = rest[sender].at[sender // 4]
        here = row_at >= block_ref[3 * ROWS : 3 * ROWS + 1]
        left = col_at >= block_ref[3 * ROWS + 1 : 3 * ROWS + 2]
        values = [block_ref[channel * ROWS : (channel + 1) * ROWS] for channel in range(3)]
        for channel, value in enumerate(values):
            value_here = jnp.where(here, value, 0.0)
            value_next = jnp.where(here, 0.0, value)
            terms = (
                jnp.where(left, value_here, 0.0),
                jnp.where(left, 0.0, value_here),
                jnp.where(left, value_next, 0.0),
                jnp.where(left, 0.0, value_next),
            )
            sums[channel] = [total + term for total, term in zip(sums[channel], terms)]
    for channel in range(3):
        own_ref[channel, :, :SIDE] = sums[channel][0]
        own_ref[channel, :, SIDE:] = sums[channel][1]
        spill_ref[channel, :, :SIDE] = sums[channel][2]
        spill_ref[channel, :, SIDE:] = sums[channel][3]


def update_kernel(owner_ref, object_ref, own_ref, spilled_ref, out_ref):
    rows = pl.ds(pl.multiple_of(owner_ref[0, 0] * ROWS, ROWS), ROWS)
    weight = own_ref[2] + spilled_ref[2] + 1.0
    for part in range(2):
        out_ref[part] = object_ref[part, rows, :] + (own_ref[part] + spilled_ref[part]) / weight


def strip_kernel(owner_ref, strip_ref, other_ref, out_ref):
    owner = owner_ref[0, 0]
    core = owner & 1
    across = owner >> 1
    for source, at in ((strip_ref, core), (other_ref, 1 - core)):
        for distance in range(4):
            block = 2 * ((across - distance) & 3) + at
            rows = pl.ds(pl.multiple_of(block * ROWS, ROWS), ROWS)
            for part in range(2):
                out_ref[part, rows, :] = source[distance, part]


def spread_kernel(parts_ref, out_ref):
    total = parts_ref[0]
    for sender in range(1, PARTS):
        total = total + parts_ref[sender]
    out_ref[...] = total


def direction_kernel(first_ref, second_ref, third_ref, fourth_ref, out_ref):
    total = (first_ref[...] + second_ref[...]) + (third_ref[...] + fourth_ref[...])
    direction = total[: 2 * MODES] / jnp.sqrt(total[2 * MODES :] + 1.0)
    for target in range(PARTS):
        out_ref[target] = direction


def assemble_kernel(core_ref, own_ref, other_ref, out_ref):
    core = core_ref[0, 0]
    half = SIDE // 2
    for source, at in ((own_ref, core), (other_ref, 1 - core)):
        base = pl.multiple_of(at * half, half)
        for piece in range(PARTS):
            rows, lanes = place(piece)
            down = pl.ds(pl.multiple_of(base + rows.start, 8), 8)
            for k in range(MODES):
                for part in range(2):
                    out_ref[k, part, down, lanes] = source[piece, 2 * k + part]


VMEM = pl.BlockSpec(memory_space=pltpu.VMEM)
SMEM = pl.BlockSpec(memory_space=pltpu.SMEM)
ANY = pl.BlockSpec(memory_space=pl.ANY)
MIB = 1024 * 1024


def params(mib):
    return pltpu.CompilerParams(vmem_limit_bytes=mib * MIB)


def cost(micros, transcendentals=0):
    return pl.CostEstimate(
        flops=int(micros * 1e9), bytes_accessed=int(1e6), transcendentals=transcendentals
    )


def shape(*sizes):
    return jax.ShapeDtypeStruct(sizes, f32)


def on_device(object_field, probe_modes, amplitudes, positions, shifts):
    forward, slope = tables()
    forward_table = jnp.asarray(two_parts(forward))

    core = lax.axis_index("c")
    core_block = jnp.reshape(core, (1, 1))
    across = lax.axis_index("x")
    owner_block = jnp.reshape(across * 2 + core, (1, 1))
    tiles = 32
    half = SIDE // 2
    cores = [(0, 1), (1, 0)]
    stage = pltpu.VMEM((MODES * SIDE, 2 * WIDE), bf16)
    stage_left = pltpu.VMEM((2 * WIDE, MODES * SIDE), bf16)
    wide = pltpu.VMEM((MODES * SIDE, WIDE), f32)
    tall = pltpu.VMEM((WIDE, MODES * SIDE), f32)
    matrix_left = pltpu.VMEM((WIDE, 3 * WIDE), bf16)
    matrix_right = pltpu.VMEM((3 * WIDE, WIDE), bf16)

    part_rows = lax.dynamic_slice_in_dim(object_field, core * half, half, axis=1)
    near = lax.ppermute(part_rows, TILE, [(i + 1, i) for i in range(tiles - 1)])

    shifted, adjoint = pl.pallas_call(
        probe_kernel,
        out_shape=(shape(MODES, 2, SIDE, SIDE), shape(4, SIDE, SIDE)),
        in_specs=[SMEM, SMEM, VMEM, VMEM],
        out_specs=(VMEM,) * 2,
        scratch_shapes=[stage, stage_left, wide, tall, matrix_right, matrix_left],
        compiler_params=params(22),
        cost_estimate=cost(8, 2048),
    )(positions, shifts, probe_modes, forward_table)

    near, shifted, adjoint = lax.optimization_barrier((near, shifted, adjoint))
    far = lax.ppermute(near, "c", cores)

    piece = shape(PARTS, 2 * MODES + 1, 8, LANES)
    *blocks, staged, mass = pl.pallas_call(
        pattern_kernel,
        out_shape=(shape(2, 3 * ROWS + 8, SIDE),) * 4
        + (jax.ShapeDtypeStruct((MODES * SIDE, 2 * WIDE), bf16), shape(SIDE, SIDE)),
        in_specs=[SMEM, SMEM] + [VMEM] * 6,
        out_specs=(VMEM,) * 6,
        scratch_shapes=[
            stage,
            stage_left,
            wide,
            tall,
            pltpu.VMEM((MODES, 2, SIDE, SIDE), f32),
            pltpu.VMEM((2, SIDE, SIDE), f32),
            matrix_left,
            matrix_right,
            pltpu.VMEM((3, SIDE, SIDE), f32),
        ],
        compiler_params=params(26),
        cost_estimate=cost(8, 65536),
    )(positions, owner_block, object_field, near, far, amplitudes, shifted, forward_table)

    keep, send = pl.pallas_call(
        adjoint_kernel,
        out_shape=(piece, piece),
        in_specs=[SMEM, SMEM] + [VMEM] * 3,
        out_specs=(VMEM,) * 2,
        scratch_shapes=[
            stage_left,
            wide,
            tall,
            matrix_left,
            matrix_right,
            pltpu.VMEM((SIDE, SIDE), f32),
        ],
        compiler_params=params(20),
        cost_estimate=cost(5),
    )(positions, owner_block, staged, mass, adjoint)

    received = [blocks[0]]
    for steps in range(1, 4):
        received.append(lax.ppermute(blocks[steps], "x", [(i, (i + steps) % 4) for i in range(4)]))
    received, send = lax.optimization_barrier((received, send))
    other = lax.ppermute(send, "c", cores)
    received = received + [lax.ppermute(block, "c", cores) for block in received]
    own, spill = pl.pallas_call(
        gather_kernel,
        out_shape=(shape(3, ROWS, 2 * SIDE), shape(3, ROWS, 2 * SIDE)),
        in_specs=[SMEM] + [VMEM] * OWNERS,
        out_specs=(VMEM,) * 2,
        compiler_params=params(8),
        cost_estimate=cost(2),
    )(owner_block, *received)
    summed, own, spill = lax.optimization_barrier((keep + other, own, spill))
    scattered = lax.all_to_all(summed, PLANE, 0, 0)

    shift_grad = pl.pallas_call(
        slope_kernel,
        out_shape=shape(1, 2),
        in_specs=[SMEM] + [VMEM] * 4,
        out_specs=SMEM,
        scratch_shapes=[stage, stage_left, wide, tall, matrix_left, matrix_right],
        compiler_params=params(22),
        cost_estimate=cost(8),
    )(core_block, probe_modes, jnp.asarray(two_parts(slope)), keep, send)

    spilled = lax.ppermute(spill, TILE, [(i, i + 1) for i in range(tiles - 1)])
    updated = pl.pallas_call(
        update_kernel,
        out_shape=shape(2, ROWS, 2 * SIDE),
        in_specs=[SMEM] + [VMEM] * 3,
        out_specs=VMEM,
        compiler_params=params(4),
        cost_estimate=cost(1),
    )(owner_block, object_field, own, spilled)
    scattered, updated, shift_grad = lax.optimization_barrier((scattered, updated, shift_grad))

    def around(value, axis):
        turns = [[(i, (i + step) % 4) for i in range(4)] for step in range(1, 4)]
        return [value] + [lax.ppermute(value, axis, turn) for turn in turns]

    column = pl.pallas_call(
        spread_kernel,
        out_shape=shape(2 * MODES + 1, 8, LANES),
        in_specs=[VMEM],
        out_specs=VMEM,
        compiler_params=params(8),
        cost_estimate=cost(1),
    )(scattered)
    columns = around(column, "zh")
    strip = jnp.stack(around(updated, "x"))
    columns, strip = lax.optimization_barrier((columns, strip))
    direction = pl.pallas_call(
        direction_kernel,
        out_shape=shape(PARTS, 2 * MODES, 8, LANES),
        in_specs=[VMEM] * 4,
        out_specs=VMEM,
        compiler_params=params(4),
        cost_estimate=cost(1, 2048),
    )(*columns)
    spread = lax.all_to_all(direction, PLANE, 0, 0)

    strip_other = lax.ppermute(strip, "c", cores)
    new_object = pl.pallas_call(
        strip_kernel,
        out_shape=shape(2, SIDE, 2 * SIDE),
        in_specs=[SMEM] + [VMEM] * 2,
        out_specs=VMEM,
        compiler_params=params(4),
        cost_estimate=cost(1),
    )(owner_block, strip, strip_other)

    spread, new_object = lax.optimization_barrier((spread, new_object))
    spread_other = lax.ppermute(spread, "c", cores)
    probe_direction = pl.pallas_call(
        assemble_kernel,
        out_shape=shape(MODES, 2, SIDE, SIDE),
        in_specs=[SMEM, VMEM, VMEM],
        out_specs=VMEM,
        compiler_params=params(8),
        cost_estimate=cost(1),
    )(core_block, spread, spread_other)
    return (new_object, probe_direction, shift_grad)


def solution(mesh):
    names = tuple(name for name, _ in AXES)
    sizes = tuple(size for _, size in AXES)
    slice_mesh = Mesh(np.asarray(mesh.devices).reshape(sizes), names)
    return jax.shard_map(
        on_device,
        mesh=slice_mesh,
        in_specs=(
            P(None, TILE, None),
            P(),
            P(names, None, None),
            P(names, None),
            P(names, None),
        ),
        out_specs=(P(None, TILE, None), P(), P(names, None)),
        check_vma=False,
    )
```

time: 494 us -> 126 us (0.26)
  the two profiles are of different devices: /device:TPU:8 before, /device:TPU:1 now
where the time goes in v2:
time: 126 us
  starting transfers between devices  54.3 us (43%)
  waiting for transfers between devices  29.4 us (23%)
  Pallas kernels  27 us (21%)
  local copies, waits for them, and re-layouts  12.8 us (10%)
    ppermute x6, starting transfers between devices, around(): return [value] + [lax.ppermute(value, axis, turn) for turn in turns]  12.9 us
    unnamed x38, local copies, waits for them, and re-layouts  11.7 us
    all_to_all x1, starting transfers between devices, on_device(): scattered = lax.all_to_all(summed, PLANE, 0, 0)  9.96 us
    pallas_call x1, Pallas kernels, on_device(): pl.pallas_call(pattern_kernel, out_shape=(shape(2, 3 * ROWS + 8, SIDE),)...  8.49 us
    all_to_all x1, starting transfers between devices, on_device(): spread = lax.all_to_all(direction, PLANE, 0, 0)  7.27 us
    all_to_all x1, waiting for transfers between devices, on_device(): spread = lax.all_to_all(direction, PLANE, 0, 0)  6.4 us
    ppermute x1, waiting for transfers between devices, on_device(): spilled = lax.ppermute(spill, TILE, [(i, i + 1) for i in range(tiles - 1)])  6.39 us
    pallas_call x1, Pallas kernels, on_device(): pl.pallas_call(probe_kernel, out_shape=(shape(MODES, 2, SIDE, SIDE), shap...  5.76 us
  transfers between devices with their start and end apart: 21, of which 13 were waited for; matrix products, arithmetic and copies ran while one was open for 0% of the time, Pallas kernels for 13%

profile of v2, /device:TPU:1, one launch (start us, length us, event | category | flops | bytes accessed | tf_op | source)
XLA Modules:
  0.0 125.6 jit_solution(8581615794194425048)
XLA Ops:
  1.7 1.4 %collective-permute-start = (f32[2,128,512]{2,1,0:T(8,128)S(1)}, f32[2,128,512]{2,1,0:T(8,128)S(1)}, u32[]{:S(2)}, u32[]{:S(2)}) collective-permute-start(f32[2,128,512]{2,1,0:T(8,128)S(1)} %constant_dynamic-slice_fusion), channel_id=1, source_target_pairs={{8,0},{16,8},{24,16},{32,24},{40,32},{48,40},{56,48},{64,56},{72,6... | collective-permute-start | bytes 1572872 | tf_op jit(solution)/shard_map/ppermute | solution.py:469
  3.2 1.6 %copy-done.1 = f32[4,2,256,256]{3,2,1,0:T(8,128)S(1)} copy-done((f32[4,2,256,256]{3,2,1,0:T(8,128)S(1)}, f32[4,2,256,256]{3,2,1,0:T(8,128)}, u32[]{:S(2)}) %copy-start.1) | copy-done | bytes 2097176
  7.1 5.8 %shard_map.94 = (f32[4,2,256,256]{3,2,1,0:T(8,128)S(1)}, f32[4,256,256]{2,1,0:T(8,128)S(1)}) custom-call(s32[1,2]{1,0:T(1,128)S(1)} %copy-done.8, f32[1,2]{1,0:T(1,128)S(1)} %copy-done.7, f32[4,2,256,256]{3,2,1,0:T(8,128)S(1)} %copy-done.1, f32[2,256,256]{2,1,0:T(8,128)S(1)} %copy-done.11), custom_call_target="tpu_custom_call" | custom-call | flops 8000000000 | bytes 1000000 | tf_op jit(solution)/shard_map/pallas_call | solution.py:471
  13.9 1.3 %copy-done.17 = f32[4,2,256,256]{3,2,1,0:T(8,128)} copy-done((f32[4,2,256,256]{3,2,1,0:T(8,128)}, f32[4,2,256,256]{3,2,1,0:T(8,128)S(1)}, u32[]{:S(2)}) %copy-start.17) | copy-done | bytes 2097176
  15.3 3.5 %collective-permute-start.1 = (f32[2,128,512]{2,1,0:T(8,128)S(1)}, f32[2,128,512]{2,1,0:T(8,128)S(1)}, u32[]{:S(2)}, u32[]{:S(2)}) collective-permute-start(f32[2,128,512]{2,1,0:T(8,128)S(1)} %collective-permute-done.near_ref), channel_id=1, source_target_pairs={{0,1},{1,0},{2,3},{3,2},{4,5},{5,4},{6,7},{7,6},{8,9},{9,8},{10,11... | collective-permute-start | bytes 1572872 | tf_op jit(solution)/shard_map/ppermute | solution.py:482
  18.8 1.5 %collective-permute-done.1.far_ref = f32[2,128,512]{2,1,0:T(8,128)S(1)} collective-permute-done((f32[2,128,512]{2,1,0:T(8,128)S(1)}, f32[2,128,512]{2,1,0:T(8,128)S(1)}, u32[]{:S(2)}, u32[]{:S(2)}) %collective-permute-start.1) | collective-permute-done | bytes 524320 | tf_op jit(solution)/shard_map/ppermute | solution.py:482
  20.3 1.6 %copy-done.18 = f32[4,2,256,256]{3,2,1,0:T(8,128)S(1)} copy-done((f32[4,2,256,256]{3,2,1,0:T(8,128)S(1)}, f32[4,2,256,256]{3,2,1,0:T(8,128)}, u32[]{:S(2)}) %copy-start.18) | copy-done | bytes 2097176
  21.9 8.5 %shard_map.95 = (f32[2,104,256]{2,1,0:T(8,128)S(1)}, f32[2,104,256]{2,1,0:T(8,128)S(1)}, f32[2,104,256]{2,1,0:T(8,128)S(1)}, f32[2,104,256]{2,1,0:T(8,128)S(1)},...) custom-call(s32[1,2]{1,0:T(1,128)S(1)} %copy-done.9, s32[1,1]{1,0:T(1,128)} %bitcast.owner_ref, ...), custom_call_target="tpu_custom_call" | custom-call | flops 8000000000 | bytes 1000000 | tf_op jit(solution)/shard_map/pallas_call | solution.py:485
  30.4 1.5 %collective-permute-start.2 = (f32[2,104,256]{2,1,0:T(8,128)S(1)}, f32[2,104,256]{2,1,0:T(8,128)S(1)}, u32[]{:S(2)}, u32[]{:S(2)}) collective-permute-start(f32[2,104,256]{2,1,0:T(8,128)S(1)} %get-tuple-element.45), channel_id=1, source_target_pairs={{0,2},{2,4},{4,6},{6,0},{1,3},{3,5},{5,7},{7,1},{8,10},{10,12},{12... | collective-permute-start | bytes 638984 | tf_op jit(solution)/shard_map/ppermute | solution.py:525
  31.9 2.4 %collective-permute-start.3 = (f32[2,104,256]{2,1,0:T(8,128)S(1)}, f32[2,104,256]{2,1,0:T(8,128)S(1)}, u32[]{:S(2)}, u32[]{:S(2)}) collective-permute-start(f32[2,104,256]{2,1,0:T(8,128)S(1)} %get-tuple-element.46), channel_id=1, source_target_pairs={{0,4},{2,6},{4,0},{6,2},{1,5},{3,7},{5,1},{7,3},{8,12},{10,14},{12... | collective-permute-start | bytes 638984 | tf_op jit(solution)/shard_map/ppermute | solution.py:525
  35.5 4.2 %shard_map.96 = (f32[32,9,8,128]{3,2,1,0:T(8,128)S(1)}, f32[32,9,8,128]{3,2,1,0:T(8,128)S(1)}) custom-call(s32[1,2]{1,0:T(1,128)S(1)} %copy-done.9, s32[1,1]{1,0:T(1,128)} %bitcast.owner_ref, bf16[1024,1024]{1,0:T(8,128)(2,1)S(1)} %get-tuple-element.40.staged_ref, f32[256,256]{1,0:T(8,128)S(1)} %get-tuple-element.41.mass_ref, f32[4,256,256]{2,1,0:T(8,128)S(1)} %copy-done.16), custom_call_target="tpu_custom_call" | custom-call | flops 5000000000 | bytes 1000000 | tf_op jit(solution)/shard_map/pallas_call | solution.py:506
  39.7 4.2 %collective-permute-done.3.rest_2_ = f32[2,104,256]{2,1,0:T(8,128)S(1)} collective-permute-done((f32[2,104,256]{2,1,0:T(8,128)S(1)}, f32[2,104,256]{2,1,0:T(8,128)S(1)}, u32[]{:S(2)}, u32[]{:S(2)}) %collective-permute-start.3) | collective-permute-done | bytes 213024 | tf_op jit(solution)/shard_map/ppermute | solution.py:525
  43.9 1.2 collective-permute-start.5
  46.1 1.8 %collective-permute-done.6.rest_4_ = f32[2,104,256]{2,1,0:T(8,128)S(1)} collective-permute-done((f32[2,104,256]{2,1,0:T(8,128)S(1)}, f32[2,104,256]{2,1,0:T(8,128)S(1)}, u32[]{:S(2)}, u32[]{:S(2)}) %collective-permute-start.6) | collective-permute-done | bytes 213024 | tf_op jit(solution)/shard_map/ppermute | solution.py:528
  50.3 10.0 %all-to-all-start = ((f32[32,9,8,128]{3,2,1,0:T(8,128)}), f32[32,9,8,128]{3,2,1,0:T(8,128)S(1)}, u32[]{:S(2)}, u32[]{:S(2)}) async-start(f32[32,9,8,128]{3,2,1,0:T(8,128)} %add.11), calls=%async_computation | async-start | bytes 2359296 | tf_op jit(solution)/shard_map/all_to_all | solution.py:538
  60.3 3.1 %collective-permute-start.10 = (f32[3,32,512]{2,1,0:T(8,128)}, f32[3,32,512]{2,1,0:T(8,128)S(1)}, u32[]{:S(2)}, u32[]{:S(2)}) collective-permute-start(f32[3,32,512]{2,1,0:T(8,128)} %copy-done.6), channel_id=1, source_target_pairs={{0,8},{8,16},{16,24},{24,32},{32,40},{40,48},{48,56},{56,64},{64,7... | collective-permute-start | bytes 589832 | tf_op jit(solution)/shard_map/ppermute | solution.py:550
  63.4 1.6 %copy-done.2 = f32[4,2,256,256]{3,2,1,0:T(8,128)S(1)} copy-done((f32[4,2,256,256]{3,2,1,0:T(8,128)S(1)}, f32[4,2,256,256]{3,2,1,0:T(8,128)}, u32[]{:S(2)}) %copy-start.2) | copy-done | bytes 2097176
  65.0 1.3 %copy-done.4 = f32[32,9,8,128]{3,2,1,0:T(8,128)S(1)} copy-done((f32[32,9,8,128]{3,2,1,0:T(8,128)S(1)}, f32[32,9,8,128]{3,2,1,0:T(8,128)}, u32[]{:S(2)}) %copy-start.4) | copy-done | bytes 1179672
  67.3 4.5 %shard_map.99 = f32[1,2]{1,0:T(1,128)} custom-call(s32[1,1]{1,0:T(1,128)} %bitcast.1.core_ref, f32[4,2,256,256]{3,2,1,0:T(8,128)S(1)} %copy-done.2, f32[2,256,256]{2,1,0:T(8,128)S(1)} %copy-done.10, f32[32,9,8,128]{3,2,1,0:T(8,128)S(1)} %get-tuple-element.43.keep_ref, f32[32,9,8,128]{3,2,1,0:T(8,128)S(1)} %copy-done.4), custom_call_target="tpu_custom_call" | custom-call | flops 8000000000 | bytes 1000000 | tf_op jit(solution)/shard_map/pallas_call | solution.py:540
  71.8 6.4 %collective-permute-done.10.spilled_ref = f32[3,32,512]{2,1,0:T(8,128)S(1)} collective-permute-done((f32[3,32,512]{2,1,0:T(8,128)}, f32[3,32,512]{2,1,0:T(8,128)S(1)}, u32[]{:S(2)}, u32[]{:S(2)}) %collective-permute-start.10) | collective-permute-done | bytes 196640 | tf_op jit(solution)/shard_map/ppermute | solution.py:550
  78.3 1.8 %collective-permute-start.16 = (f32[2,32,512]{2,1,0:T(8,128)S(1)}, f32[2,32,512]{2,1,0:T(8,128)S(1)}, u32[]{:S(2)}, u32[]{:S(2)}) collective-permute-start(f32[2,32,512]{2,1,0:T(8,128)S(1)} %shard_map.98), channel_id=1, source_target_pairs={{0,6},{2,0},{4,2},{6,4},{1,7},{3,1},{5,3},{7,5},{8,14},{10,8},{12,... | collective-permute-start | bytes 393224 | tf_op jit(solution)/shard_map/ppermute | solution.py:563
  80.9 6.6 %collective-permute-start.13 = (f32[9,8,128]{2,1,0:T(8,128)S(1)}, f32[9,8,128]{2,1,0:T(8,128)S(1)}, u32[]{:S(2)}, u32[]{:S(2)}) collective-permute-start(f32[9,8,128]{2,1,0:T(8,128)S(1)} %shard_map.100.first_ref), channel_id=1, source_target_pairs={{0,192},{64,0},{128,64},{192,128},{1,193},{65,1},{129,65},{193,129... | collective-permute-start | bytes 110600 | tf_op jit(solution)/shard_map/ppermute | solution.py:563
  87.5 2.9 %collective-permute-start.12 = (f32[9,8,128]{2,1,0:T(8,128)S(1)}, f32[9,8,128]{2,1,0:T(8,128)S(1)}, u32[]{:S(2)}, u32[]{:S(2)}) collective-permute-start(f32[9,8,128]{2,1,0:T(8,128)S(1)} %shard_map.100.first_ref), channel_id=1, source_target_pairs={{0,128},{64,192},{128,0},{192,64},{1,129},{65,193},{129,1},{193,65... | collective-permute-start | bytes 110600 | tf_op jit(solution)/shard_map/ppermute | solution.py:563
  91.3 2.9 %collective-permute-done.12.third_ref = f32[9,8,128]{2,1,0:T(8,128)S(1)} collective-permute-done((f32[9,8,128]{2,1,0:T(8,128)S(1)}, f32[9,8,128]{2,1,0:T(8,128)S(1)}, u32[]{:S(2)}, u32[]{:S(2)}) %collective-permute-start.12) | collective-permute-done | bytes 36896 | tf_op jit(solution)/shard_map/ppermute | solution.py:563
  94.2 1.5 %collective-permute-done.11.second_ref = f32[9,8,128]{2,1,0:T(8,128)S(1)} collective-permute-done((f32[9,8,128]{2,1,0:T(8,128)S(1)}, f32[9,8,128]{2,1,0:T(8,128)S(1)}, u32[]{:S(2)}, u32[]{:S(2)}) %collective-permute-start.11) | collective-permute-done | bytes 36896 | tf_op jit(solution)/shard_map/ppermute | solution.py:563
  96.8 7.3 %all-to-all-start.1 = ((f32[32,8,8,128]{3,2,1,0:T(8,128)}), f32[32,8,8,128]{3,2,1,0:T(8,128)S(1)}, u32[]{:S(2)}, u32[]{:S(2)}) async-start(f32[32,8,8,128]{3,2,1,0:T(8,128)} %shard_map.101), calls=%async_computation.1 | async-start | bytes 2097152 | tf_op jit(solution)/shard_map/all_to_all | solution.py:584
  104.0 3.5 %collective-permute-start.17 = (f32[4,2,32,512]{3,2,1,0:T(8,128)S(1)}, f32[4,2,32,512]{3,2,1,0:T(8,128)S(1)}, u32[]{:S(2)}, u32[]{:S(2)}) collective-permute-start(f32[4,2,32,512]{3,2,1,0:T(8,128)S(1)} %pad_maximum_fusion.strip_ref), channel_id=1, source_target_pairs={{0,1},{1,0},{2,3},{3,2},{4,5},{5,4},{6,7},{7,6},{8,9},{9,8},{10,11... | collective-permute-start | bytes 1572872 | tf_op jit(solution)/shard_map/ppermute | solution.py:586
  107.6 1.5 %collective-permute-done.17.other_ref = f32[4,2,32,512]{3,2,1,0:T(8,128)S(1)} collective-permute-done((f32[4,2,32,512]{3,2,1,0:T(8,128)S(1)}, f32[4,2,32,512]{3,2,1,0:T(8,128)S(1)}, u32[]{:S(2)}, u32[]{:S(2)}) %collective-permute-start.17) | collective-permute-done | bytes 524320 | tf_op jit(solution)/shard_map/ppermute | solution.py:586
  110.1 6.4 %all-to-all-done.1.own_ref = f32[32,8,8,128]{3,2,1,0:T(8,128)S(1)} async-done(((f32[32,8,8,128]{3,2,1,0:T(8,128)}), f32[32,8,8,128]{3,2,1,0:T(8,128)S(1)}, u32[]{:S(2)}, u32[]{:S(2)}) %all-to-all-start.1) | async-done | bytes 1048608 | tf_op jit(solution)/shard_map/all_to_all | solution.py:584
  116.5 5.3 %collective-permute-start.18 = (f32[32,8,8,128]{3,2,1,0:T(8,128)S(1)}, f32[32,8,8,128]{3,2,1,0:T(8,128)S(1)}, u32[]{:S(2)}, u32[]{:S(2)}) collective-permute-start(f32[32,8,8,128]{3,2,1,0:T(8,128)S(1)} %all-to-all-done.1.own_ref), channel_id=1, source_target_pairs={{0,1},{1,0},{2,3},{3,2},{4,5},{5,4},{6,7},{7,6},{8,9},{9,8},{10,11... | collective-permute-start | bytes 3145736 | tf_op jit(solution)/shard_map/ppermute | solution.py:597
  121.8 2.3 %collective-permute-done.18.other_ref = f32[32,8,8,128]{3,2,1,0:T(8,128)S(1)} collective-permute-done((f32[32,8,8,128]{3,2,1,0:T(8,128)S(1)}, f32[32,8,8,128]{3,2,1,0:T(8,128)S(1)}, u32[]{:S(2)}, u32[]{:S(2)}) %collective-permute-start.18) | collective-permute-done | bytes 1048608 | tf_op jit(solution)/shard_map/ppermute | solution.py:597
  124.1 1.5 %shard_map.103 = f32[4,2,256,256]{3,2,1,0:T(8,128)} custom-call(s32[1,1]{1,0:T(1,128)} %bitcast.1.core_ref, f32[32,8,8,128]{3,2,1,0:T(8,128)S(1)} %all-to-all-done.1.own_ref, f32[32,8,8,128]{3,2,1,0:T(8,128)S(1)} %collective-permute-done.18.other_ref), custom_call_target="tpu_custom_call" | custom-call | flops 1000000000 | bytes 1000000 | tf_op jit(solution)/shard_map/pallas_call | solution.py:598
  (61 shorter events, 14.1 us)
Async XLA Ops:
  1.7 18.6 %copy-start = (f32[2,256,512]{2,1,0:T(8,128)S(1)}, f32[2,256,512]{2,1,0:T(8,128)}, u32[]{:S(2)}) copy-start(f32[2,256,512]{2,1,0:T(8,128)} %object_ref.3) | copy-start | bytes 3145732
  1.7 13.5 %collective-permute-start = (f32[2,128,512]{2,1,0:T(8,128)S(1)}, f32[2,128,512]{2,1,0:T(8,128)S(1)}, u32[]{:S(2)}, u32[]{:S(2)}) collective-permute-start(f32[2,128,512]{2,1,0:T(8,128)S(1)} %constant_dynamic-slice_fusion), channel_id=1, source_target_pairs={{8,0},{16,8},{24,16},{32,24},{40,32},{48,40},{56,48},{64,56},{72,6... | collective-permute-start | bytes 1572872 | tf_op jit(solution)/shard_map/ppermute | solution.py:469
  3.2 1.6 %copy-start.1 = (f32[4,2,256,256]{3,2,1,0:T(8,128)S(1)}, f32[4,2,256,256]{3,2,1,0:T(8,128)}, u32[]{:S(2)}) copy-start(f32[4,2,256,256]{3,2,1,0:T(8,128)} %probe_ref.3) | copy-start | bytes 6291460
  7.1 13.2 %copy-start.5 = (f32[1,256,256]{2,1,0:T(8,128)S(1)}, f32[1,256,256]{2,1,0:T(8,128)}, u32[]{:S(2)}) copy-start(f32[1,256,256]{2,1,0:T(8,128)} %amplitude_ref.1) | copy-start | bytes 786436
  7.1 13.2 %copy-start.9 = (s32[1,2]{1,0:T(1,128)S(1)}, s32[1,2]{1,0:T(1,128)}, u32[]{:S(2)}) copy-start(s32[1,2]{1,0:T(1,128)} %corner_ref.5) | copy-start | bytes 28
  7.1 13.2 %copy-start.12 = (f32[2,256,256]{2,1,0:T(8,128)S(1)}, f32[2,256,256]{2,1,0:T(8,128)}, u32[]{:S(2)}) copy-start(f32[2,256,256]{2,1,0:T(8,128)} %constant.20.clone.forward_ref) | copy-start | bytes 1572868
  13.9 1.3 %copy-start.17 = (f32[4,2,256,256]{3,2,1,0:T(8,128)}, f32[4,2,256,256]{3,2,1,0:T(8,128)S(1)}, u32[]{:S(2)}) copy-start(f32[4,2,256,256]{3,2,1,0:T(8,128)S(1)} %get-tuple-element.39.shifted_ref) | copy-start | bytes 6291460
  15.3 5.0 %collective-permute-start.1 = (f32[2,128,512]{2,1,0:T(8,128)S(1)}, f32[2,128,512]{2,1,0:T(8,128)S(1)}, u32[]{:S(2)}, u32[]{:S(2)}) collective-permute-start(f32[2,128,512]{2,1,0:T(8,128)S(1)} %collective-permute-done.near_ref), channel_id=1, source_target_pairs={{0,1},{1,0},{2,3},{3,2},{4,5},{5,4},{6,7},{7,6},{8,9},{9,8},{10,11... | collective-permute-start | bytes 1572872 | tf_op jit(solution)/shard_map/ppermute | solution.py:482
  20.3 1.6 %copy-start.18 = (f32[4,2,256,256]{3,2,1,0:T(8,128)S(1)}, f32[4,2,256,256]{3,2,1,0:T(8,128)}, u32[]{:S(2)}) copy-start(f32[4,2,256,256]{3,2,1,0:T(8,128)} %copy-done.17) | copy-start | bytes 6291460
  21.9 13.6 %copy-start.16 = (f32[4,256,256]{2,1,0:T(8,128)S(1)}, f32[4,256,256]{2,1,0:T(8,128)}, u32[]{:S(2)}) copy-start(f32[4,256,256]{2,1,0:T(8,128)} %copy-done.15) | copy-start | bytes 3145732
  30.4 9.3 %collective-permute-start.2 = (f32[2,104,256]{2,1,0:T(8,128)S(1)}, f32[2,104,256]{2,1,0:T(8,128)S(1)}, u32[]{:S(2)}, u32[]{:S(2)}) collective-permute-start(f32[2,104,256]{2,1,0:T(8,128)S(1)} %get-tuple-element.45), channel_id=1, source_target_pairs={{0,2},{2,4},{4,6},{6,0},{1,3},{3,5},{5,7},{7,1},{8,10},{10,12},{12... | collective-permute-start | bytes 638984 | tf_op jit(solution)/shard_map/ppermute | solution.py:525
  31.9 12.0 %collective-permute-start.3 = (f32[2,104,256]{2,1,0:T(8,128)S(1)}, f32[2,104,256]{2,1,0:T(8,128)S(1)}, u32[]{:S(2)}, u32[]{:S(2)}) collective-permute-start(f32[2,104,256]{2,1,0:T(8,128)S(1)} %get-tuple-element.46), channel_id=1, source_target_pairs={{0,4},{2,6},{4,0},{6,2},{1,5},{3,7},{5,1},{7,3},{8,12},{10,14},{12... | collective-permute-start | bytes 638984 | tf_op jit(solution)/shard_map/ppermute | solution.py:525
  34.3 9.6 %collective-permute-start.4 = (f32[2,104,256]{2,1,0:T(8,128)S(1)}, f32[2,104,256]{2,1,0:T(8,128)S(1)}, u32[]{:S(2)}, u32[]{:S(2)}) collective-permute-start(f32[2,104,256]{2,1,0:T(8,128)S(1)} %get-tuple-element.47), channel_id=1, source_target_pairs={{0,6},{2,0},{4,2},{6,4},{1,7},{3,1},{5,3},{7,5},{8,14},{10,8},{12,... | collective-permute-start | bytes 638984 | tf_op jit(solution)/shard_map/ppermute | solution.py:525
  39.7 9.4 %copy-start.3 = (f32[32,9,8,128]{3,2,1,0:T(8,128)}, f32[32,9,8,128]{3,2,1,0:T(8,128)S(1)}, u32[]{:S(2)}) copy-start(f32[32,9,8,128]{3,2,1,0:T(8,128)S(1)} %get-tuple-element.49.send_ref) | copy-start | bytes 3538948
  43.9 5.3 %collective-permute-start.5 = (f32[32,9,8,128]{3,2,1,0:T(8,128)S(1)}, f32[32,9,8,128]{3,2,1,0:T(8,128)S(1)}, u32[]{:S(2)}, u32[]{:S(2)}) collective-permute-start(f32[32,9,8,128]{3,2,1,0:T(8,128)S(1)} %get-tuple-element.49.send_ref), channel_id=1, source_target_pairs={{0,1},{1,0},{2,3},{3,2},{4,5},{5,4},{6,7},{7,6},{8,9},{9,8},{10,11... | collective-permute-start | bytes 3538952 | tf_op jit(solution)/shard_map/ppermute | solution.py:527
  45.1 2.8 %collective-permute-start.6 = (f32[2,104,256]{2,1,0:T(8,128)S(1)}, f32[2,104,256]{2,1,0:T(8,128)S(1)}, u32[]{:S(2)}, u32[]{:S(2)}) collective-permute-start(f32[2,104,256]{2,1,0:T(8,128)S(1)} %get-tuple-element.50.rest_0_), channel_id=1, source_target_pairs={{0,1},{1,0},{2,3},{3,2},{4,5},{5,4},{6,7},{7,6},{8,9},{9,8},{10,11... | collective-permute-start | bytes 638984 | tf_op jit(solution)/shard_map/ppermute | solution.py:528
  45.1 3.1 %collective-permute-start.7 = (f32[2,104,256]{2,1,0:T(8,128)S(1)}, f32[2,104,256]{2,1,0:T(8,128)S(1)}, u32[]{:S(2)}, u32[]{:S(2)}) collective-permute-start(f32[2,104,256]{2,1,0:T(8,128)S(1)} %collective-permute-done.2.rest_1_), channel_id=1, source_target_pairs={{0,1},{1,0},{2,3},{3,2},{4,5},{5,4},{6,7},{7,6},{8,9},{9,8},{10,11... | collective-permute-start | bytes 638984 | tf_op jit(solution)/shard_map/ppermute | solution.py:528
  45.6 2.9 %collective-permute-start.8 = (f32[2,104,256]{2,1,0:T(8,128)S(1)}, f32[2,104,256]{2,1,0:T(8,128)S(1)}, u32[]{:S(2)}, u32[]{:S(2)}) collective-permute-start(f32[2,104,256]{2,1,0:T(8,128)S(1)} %collective-permute-done.3.rest_2_), channel_id=1, source_target_pairs={{0,1},{1,0},{2,3},{3,2},{4,5},{5,4},{6,7},{7,6},{8,9},{9,8},{10,11... | collective-permute-start | bytes 638984 | tf_op jit(solution)/shard_map/ppermute | solution.py:528
  45.6 3.2 %collective-permute-start.9 = (f32[2,104,256]{2,1,0:T(8,128)S(1)}, f32[2,104,256]{2,1,0:T(8,128)S(1)}, u32[]{:S(2)}, u32[]{:S(2)}) collective-permute-start(f32[2,104,256]{2,1,0:T(8,128)S(1)} %collective-permute-done.4.rest_3_), channel_id=1, source_target_pairs={{0,1},{1,0},{2,3},{3,2},{4,5},{5,4},{6,7},{7,6},{8,9},{9,8},{10,11... | collective-permute-start | bytes 638984 | tf_op jit(solution)/shard_map/ppermute | solution.py:528
  50.3 28.0 %all-to-all-start = ((f32[32,9,8,128]{3,2,1,0:T(8,128)}), f32[32,9,8,128]{3,2,1,0:T(8,128)S(1)}, u32[]{:S(2)}, u32[]{:S(2)}) async-start(f32[32,9,8,128]{3,2,1,0:T(8,128)} %add.11), calls=%async_computation | async-start | bytes 2359296 | tf_op jit(solution)/shard_map/all_to_all | solution.py:538
  60.3 18.0 %collective-permute-start.10 = (f32[3,32,512]{2,1,0:T(8,128)}, f32[3,32,512]{2,1,0:T(8,128)S(1)}, u32[]{:S(2)}, u32[]{:S(2)}) collective-permute-start(f32[3,32,512]{2,1,0:T(8,128)} %copy-done.6), channel_id=1, source_target_pairs={{0,8},{8,16},{16,24},{24,32},{32,40},{40,48},{48,56},{56,64},{64,7... | collective-permute-start | bytes 589832 | tf_op jit(solution)/shard_map/ppermute | solution.py:550
  63.4 1.6 %copy-start.2 = (f32[4,2,256,256]{3,2,1,0:T(8,128)S(1)}, f32[4,2,256,256]{3,2,1,0:T(8,128)}, u32[]{:S(2)}) copy-start(f32[4,2,256,256]{3,2,1,0:T(8,128)} %probe_ref.3) | copy-start | bytes 6291460
  67.3 10.9 %copy-start.14 = (f32[3,32,512]{2,1,0:T(8,128)S(1)}, f32[3,32,512]{2,1,0:T(8,128)}, u32[]{:S(2)}) copy-start(f32[3,32,512]{2,1,0:T(8,128)} %copy-done.13) | copy-start | bytes 589828
  78.3 12.1 %collective-permute-start.16 = (f32[2,32,512]{2,1,0:T(8,128)S(1)}, f32[2,32,512]{2,1,0:T(8,128)S(1)}, u32[]{:S(2)}, u32[]{:S(2)}) collective-permute-start(f32[2,32,512]{2,1,0:T(8,128)S(1)} %shard_map.98), channel_id=1, source_target_pairs={{0,6},{2,0},{4,2},{6,4},{1,7},{3,1},{5,3},{7,5},{8,14},{10,8},{12,... | collective-permute-start | bytes 393224 | tf_op jit(solution)/shard_map/ppermute | solution.py:563
  80.1 11.2 %collective-permute-start.15 = (f32[2,32,512]{2,1,0:T(8,128)S(1)}, f32[2,32,512]{2,1,0:T(8,128)S(1)}, u32[]{:S(2)}, u32[]{:S(2)}) collective-permute-start(f32[2,32,512]{2,1,0:T(8,128)S(1)} %shard_map.98), channel_id=1, source_target_pairs={{0,4},{2,6},{4,0},{6,2},{1,5},{3,7},{5,1},{7,3},{8,12},{10,14},{12... | collective-permute-start | bytes 393224 | tf_op jit(solution)/shard_map/ppermute | solution.py:563
  80.8 10.5 %collective-permute-start.14 = (f32[2,32,512]{2,1,0:T(8,128)S(1)}, f32[2,32,512]{2,1,0:T(8,128)S(1)}, u32[]{:S(2)}, u32[]{:S(2)}) collective-permute-start(f32[2,32,512]{2,1,0:T(8,128)S(1)} %shard_map.98), channel_id=1, source_target_pairs={{0,2},{2,4},{4,6},{6,0},{1,3},{3,5},{5,7},{7,1},{8,10},{10,12},{12... | collective-permute-start | bytes 393224 | tf_op jit(solution)/shard_map/ppermute | solution.py:563
  80.9 10.4 %collective-permute-start.13 = (f32[9,8,128]{2,1,0:T(8,128)S(1)}, f32[9,8,128]{2,1,0:T(8,128)S(1)}, u32[]{:S(2)}, u32[]{:S(2)}) collective-permute-start(f32[9,8,128]{2,1,0:T(8,128)S(1)} %shard_map.100.first_ref), channel_id=1, source_target_pairs={{0,192},{64,0},{128,64},{192,128},{1,193},{65,1},{129,65},{193,129... | collective-permute-start | bytes 110600 | tf_op jit(solution)/shard_map/ppermute | solution.py:563
  87.5 6.7 %collective-permute-start.12 = (f32[9,8,128]{2,1,0:T(8,128)S(1)}, f32[9,8,128]{2,1,0:T(8,128)S(1)}, u32[]{:S(2)}, u32[]{:S(2)}) collective-permute-start(f32[9,8,128]{2,1,0:T(8,128)S(1)} %shard_map.100.first_ref), channel_id=1, source_target_pairs={{0,128},{64,192},{128,0},{192,64},{1,129},{65,193},{129,1},{193,65... | collective-permute-start | bytes 110600 | tf_op jit(solution)/shard_map/ppermute | solution.py:563
  90.4 5.3 %collective-permute-start.11 = (f32[9,8,128]{2,1,0:T(8,128)S(1)}, f32[9,8,128]{2,1,0:T(8,128)S(1)}, u32[]{:S(2)}, u32[]{:S(2)}) collective-permute-start(f32[9,8,128]{2,1,0:T(8,128)S(1)} %shard_map.100.first_ref), channel_id=1, source_target_pairs={{0,64},{64,128},{128,192},{192,0},{1,65},{65,129},{129,193},{193,1... | collective-permute-start | bytes 110600 | tf_op jit(solution)/shard_map/ppermute | solution.py:563
  96.8 19.8 %all-to-all-start.1 = ((f32[32,8,8,128]{3,2,1,0:T(8,128)}), f32[32,8,8,128]{3,2,1,0:T(8,128)S(1)}, u32[]{:S(2)}, u32[]{:S(2)}) async-start(f32[32,8,8,128]{3,2,1,0:T(8,128)} %shard_map.101), calls=%async_computation.1 | async-start | bytes 2097152 | tf_op jit(solution)/shard_map/all_to_all | solution.py:584
  104.0 5.1 %collective-permute-start.17 = (f32[4,2,32,512]{3,2,1,0:T(8,128)S(1)}, f32[4,2,32,512]{3,2,1,0:T(8,128)S(1)}, u32[]{:S(2)}, u32[]{:S(2)}) collective-permute-start(f32[4,2,32,512]{3,2,1,0:T(8,128)S(1)} %pad_maximum_fusion.strip_ref), channel_id=1, source_target_pairs={{0,1},{1,0},{2,3},{3,2},{4,5},{5,4},{6,7},{7,6},{8,9},{9,8},{10,11... | collective-permute-start | bytes 1572872 | tf_op jit(solution)/shard_map/ppermute | solution.py:586
  116.5 7.6 %collective-permute-start.18 = (f32[32,8,8,128]{3,2,1,0:T(8,128)S(1)}, f32[32,8,8,128]{3,2,1,0:T(8,128)S(1)}, u32[]{:S(2)}, u32[]{:S(2)}) collective-permute-start(f32[32,8,8,128]{3,2,1,0:T(8,128)S(1)} %all-to-all-done.1.own_ref), channel_id=1, source_target_pairs={{0,1},{1,0},{2,3},{3,2},{4,5},{5,4},{6,7},{7,6},{8,9},{9,8},{10,11... | collective-permute-start | bytes 3145736 | tf_op jit(solution)/shard_map/ppermute | solution.py:597
  (8 other events, 8.0 us)

commit v3 on v2

--- a/solution.py
+++ b/solution.py
@@ -523,7 +523,6 @@
     received = [blocks[0]]
     for steps in range(1, 4):
         received.append(lax.ppermute(blocks[steps], "x", [(i, (i + steps) % 4) for i in range(4)]))
-    received, send = lax.optimization_barrier((received, send))
     other = lax.ppermute(send, "c", cores)
     received = received + [lax.ppermute(block, "c", cores) for block in received]
     own, spill = pl.pallas_call(
@@ -532,9 +531,9 @@
         in_specs=[SMEM] + [VMEM] * OWNERS,
         out_specs=(VMEM,) * 2,
         compiler_params=params(8),
-        cost_estimate=cost(2),
+        cost_estimate=cost(12),
     )(owner_block, *received)
-    summed, own, spill = lax.optimization_barrier((keep + other, own, spill))
+    summed = keep + other
     scattered = lax.all_to_all(summed, PLANE, 0, 0)
 
     shift_grad = pl.pallas_call(
@@ -571,8 +570,7 @@
         cost_estimate=cost(1),
     )(scattered)
     columns = around(column, "zh")
-    strip = jnp.stack(around(updated, "x"))
-    columns, strip = lax.optimization_barrier((columns, strip))
+    columns, updated = lax.optimization_barrier((columns, updated))
     direction = pl.pallas_call(
         direction_kernel,
         out_shape=shape(PARTS, 2 * MODES, 8, LANES),
@@ -583,6 +581,7 @@
     )(*columns)
     spread = lax.all_to_all(direction, PLANE, 0, 0)
 
+    strip = jnp.stack(around(updated, "x"))
     strip_other = lax.ppermute(strip, "c", cores)
     new_object = pl.pallas_call(
         strip_kernel,
@@ -590,7 +589,7 @@
         in_specs=[SMEM] + [VMEM] * 2,
         out_specs=VMEM,
         compiler_params=params(4),
-        cost_estimate=cost(1),
+        cost_estimate=cost(15),
     )(owner_block, strip, strip_other)
 
     spread, new_object = lax.optimization_barrier((spread, new_object))

time: 126 us -> 117 us (0.929)
  waiting for transfers between devices: 29.4 us -> 23 us
  local copies, waits for them, and re-layouts: 12.8 us -> 9.87 us
  Pallas kernels: 27 us -> 29 us
  starting transfers between devices: 54.3 us -> 52.5 us
    ppermute x3, waiting for transfers between devices: 4.16 us -> 0.01 us  [on_device(): lax.ppermute(blocks[steps], 'x', [(i, (i + steps) % 4) for i in range(4)])]
    unnamed x38 -> x36, local copies, waits for them, and re-layouts: 11.7 us -> 8.78 us
    all_to_all x1, starting transfers between devices: 9.96 us -> 7.99 us  [on_device(): scattered = lax.all_to_all(summed, PLANE, 0, 0)]
    ppermute x1, waiting for transfers between devices: 6.39 us -> 4.57 us  [on_device(): spilled = lax.ppermute(spill, TILE, [(i, i + 1) for i in range(tiles - 1)])]
    ppermute x6, starting transfers between devices: 12.9 us -> 14.5 us  [around(): return [value] + [lax.ppermute(value, axis, turn) for turn in turns]]
  transfers between devices with their start and end apart: 21 -> 21, of which waited for: 13 -> 12; matrix products, arithmetic and copies ran while one was open for 0% -> 1% of each run, Pallas kernels for 13% -> 12%
where the time goes in v3:
time: 117 us; the launch traced here: 116 us
  starting transfers between devices  52.5 us (45%)
  Pallas kernels  29 us (25%)
  waiting for transfers between devices  23 us (20%)
  local copies, waits for them, and re-layouts  9.87 us (8%)
  other arithmetic  1.17 us (1%)
    ppermute x6, starting transfers between devices, around(): return [value] + [lax.ppermute(value, axis, turn) for turn in turns]  14.5 us
    pallas_call x1, Pallas kernels, on_device(): pl.pallas_call(pattern_kernel, out_shape=(shape(2, 3 * ROWS + 8, SIDE),)...  9.3 us
    unnamed x36, local copies, waits for them, and re-layouts  8.78 us
    all_to_all x1, starting transfers between devices, on_device(): scattered = lax.all_to_all(summed, PLANE, 0, 0)  7.99 us
    all_to_all x1, waiting for transfers between devices, on_device(): spread = lax.all_to_all(direction, PLANE, 0, 0)  7.59 us
    all_to_all x1, starting transfers between devices, on_device(): spread = lax.all_to_all(direction, PLANE, 0, 0)  6.56 us
    pallas_call x1, Pallas kernels, on_device(): pl.pallas_call(probe_kernel, out_shape=(shape(MODES, 2, SIDE, SIDE), shap...  5.76 us
    ppermute x3, starting transfers between devices, on_device(): lax.ppermute(blocks[steps], 'x', [(i, (i + steps) % 4) for i in range(4)])  4.97 us
  transfers between devices with their start and end apart: 21, of which 12 were waited for; matrix products, arithmetic and copies ran while one was open for 1% of the time, Pallas kernels for 12%

profile of v3, /device:TPU:1, one launch (start us, length us, event | category | flops | bytes accessed | tf_op | source)
XLA Modules:
  0.0 116.4 jit_solution(10902635778940107748)
XLA Ops:
  1.7 1.4 %collective-permute-start = (f32[2,128,512]{2,1,0:T(8,128)S(1)}, f32[2,128,512]{2,1,0:T(8,128)S(1)}, u32[]{:S(2)}, u32[]{:S(2)}) collective-permute-start(f32[2,128,512]{2,1,0:T(8,128)S(1)} %constant_dynamic-slice_fusion), channel_id=1, source_target_pairs={{8,0},{16,8},{24,16},{32,24},{40,32},{48,40},{56,48},{64,56},{72,6... | collective-permute-start | bytes 1572872 | tf_op jit(solution)/shard_map/ppermute | solution.py:469
  3.2 1.6 %copy-done.1 = f32[4,2,256,256]{3,2,1,0:T(8,128)S(1)} copy-done((f32[4,2,256,256]{3,2,1,0:T(8,128)S(1)}, f32[4,2,256,256]{3,2,1,0:T(8,128)}, u32[]{:S(2)}) %copy-start.1) | copy-done | bytes 2097176
  7.1 5.8 %shard_map.94 = (f32[4,2,256,256]{3,2,1,0:T(8,128)S(1)}, f32[4,256,256]{2,1,0:T(8,128)S(1)}) custom-call(s32[1,2]{1,0:T(1,128)S(1)} %copy-done.9, f32[1,2]{1,0:T(1,128)S(1)} %copy-done.8, f32[4,2,256,256]{3,2,1,0:T(8,128)S(1)} %copy-done.1, f32[2,256,256]{2,1,0:T(8,128)S(1)} %copy-done.12), custom_call_target="tpu_custom_call" | custom-call | flops 8000000000 | bytes 1000000 | tf_op jit(solution)/shard_map/pallas_call | solution.py:471
  13.9 1.3 %copy-done.16 = f32[4,2,256,256]{3,2,1,0:T(8,128)} copy-done((f32[4,2,256,256]{3,2,1,0:T(8,128)}, f32[4,2,256,256]{3,2,1,0:T(8,128)S(1)}, u32[]{:S(2)}) %copy-start.16) | copy-done | bytes 2097176
  15.3 3.5 %collective-permute-start.1 = (f32[2,128,512]{2,1,0:T(8,128)S(1)}, f32[2,128,512]{2,1,0:T(8,128)S(1)}, u32[]{:S(2)}, u32[]{:S(2)}) collective-permute-start(f32[2,128,512]{2,1,0:T(8,128)S(1)} %collective-permute-done.near_ref), channel_id=1, source_target_pairs={{0,1},{1,0},{2,3},{3,2},{4,5},{5,4},{6,7},{7,6},{8,9},{9,8},{10,11... | collective-permute-start | bytes 1572872 | tf_op jit(solution)/shard_map/ppermute | solution.py:482
  18.8 1.5 %collective-permute-done.1.far_ref = f32[2,128,512]{2,1,0:T(8,128)S(1)} collective-permute-done((f32[2,128,512]{2,1,0:T(8,128)S(1)}, f32[2,128,512]{2,1,0:T(8,128)S(1)}, u32[]{:S(2)}, u32[]{:S(2)}) %collective-permute-start.1) | collective-permute-done | bytes 524320 | tf_op jit(solution)/shard_map/ppermute | solution.py:482
  20.3 1.6 %copy-done.17 = f32[4,2,256,256]{3,2,1,0:T(8,128)S(1)} copy-done((f32[4,2,256,256]{3,2,1,0:T(8,128)S(1)}, f32[4,2,256,256]{3,2,1,0:T(8,128)}, u32[]{:S(2)}) %copy-start.17) | copy-done | bytes 2097176
  21.9 9.3 %shard_map.95 = (f32[2,104,256]{2,1,0:T(8,128)S(1)}, f32[2,104,256]{2,1,0:T(8,128)}, f32[2,104,256]{2,1,0:T(8,128)}, f32[2,104,256]{2,1,0:T(8,128)}, bf16[1024,1...) custom-call(s32[1,2]{1,0:T(1,128)S(1)} %copy-done.10, s32[1,1]{1,0:T(1,128)} %bitcast.owner_ref, f32[2,256,512]{2,1,0:T(8,128)S(1)} %copy-done, ...), custom_call_target="tpu_custom_call" | custom-call | flops 8000000000 | bytes 1000000 | tf_op jit(solution)/shard_map/pallas_call | solution.py:485
  31.2 4.2 %shard_map.96 = (f32[32,9,8,128]{3,2,1,0:T(8,128)S(1)}, f32[32,9,8,128]{3,2,1,0:T(8,128)S(1)}) custom-call(s32[1,2]{1,0:T(1,128)S(1)} %copy-done.10, s32[1,1]{1,0:T(1,128)} %bitcast.owner_ref, bf16[1024,1024]{1,0:T(8,128)(2,1)S(1)} %get-tuple-element.32.staged_ref, f32[256,256]{1,0:T(8,128)S(1)} %get-tuple-element.33.mass_ref, f32[4,256,256]{2,1,0:T(8,128)S(1)} %copy-done.15), custom_call_target="tpu_custom_call" | custom-call | flops 5000000000 | bytes 1000000 | tf_op jit(solution)/shard_map/pallas_call | solution.py:506
  35.9 1.4 %collective-permute-start.3 = (f32[2,104,256]{2,1,0:T(8,128)}, f32[2,104,256]{2,1,0:T(8,128)}, u32[]{:S(2)}, u32[]{:S(2)}) collective-permute-start(f32[2,104,256]{2,1,0:T(8,128)} %get-tuple-element.38), channel_id=1, source_target_pairs={{0,2},{2,4},{4,6},{6,0},{1,3},{3,5},{5,7},{7,1},{8,10},{10,12},{12... | collective-permute-start | bytes 638984 | tf_op jit(solution)/shard_map/ppermute | solution.py:525
  37.3 2.4 %collective-permute-start.4 = (f32[2,104,256]{2,1,0:T(8,128)}, f32[2,104,256]{2,1,0:T(8,128)}, u32[]{:S(2)}, u32[]{:S(2)}) collective-permute-start(f32[2,104,256]{2,1,0:T(8,128)} %get-tuple-element.39), channel_id=1, source_target_pairs={{0,4},{2,6},{4,0},{6,2},{1,5},{3,7},{5,1},{7,3},{8,12},{10,14},{12... | collective-permute-start | bytes 638984 | tf_op jit(solution)/shard_map/ppermute | solution.py:525
  39.8 1.1 collective-permute-start.5
  40.9 1.1 add.11
  42.0 8.0 %all-to-all-start = ((f32[32,9,8,128]{3,2,1,0:T(8,128)}), f32[32,9,8,128]{3,2,1,0:T(8,128)S(1)}, u32[]{:S(2)}, u32[]{:S(2)}) async-start(f32[32,9,8,128]{3,2,1,0:T(8,128)} %add.11), calls=%async_computation | async-start | bytes 2359296 | tf_op jit(solution)/shard_map/all_to_all | solution.py:537
  50.1 1.3 %collective-permute-start.6 = (f32[2,104,256]{2,1,0:T(8,128)}, f32[2,104,256]{2,1,0:T(8,128)S(1)}, u32[]{:S(2)}, u32[]{:S(2)}) collective-permute-start(f32[2,104,256]{2,1,0:T(8,128)} %copy-done.6), channel_id=1, source_target_pairs={{0,1},{1,0},{2,3},{3,2},{4,5},{5,4},{6,7},{7,6},{8,9},{9,8},{10,11... | collective-permute-start | bytes 638984 | tf_op jit(solution)/shard_map/ppermute | solution.py:527
  54.6 1.5 %shard_map.97 = (f32[3,32,512]{2,1,0:T(8,128)S(1)}, f32[3,32,512]{2,1,0:T(8,128)S(1)}) custom-call(s32[1,1]{1,0:T(1,128)} %bitcast.owner_ref, f32[2,104,256]{2,1,0:T(8,128)S(1)} %copy-done.7, f32[2,104,256]{2,1,0:T(8,128)} %collective-permute-done.3.rest_1_, f32[2,104,256]{2,1,0:T(8,128)} %collective-permute-done.4.rest_2_, ...), custom_call_target="tpu_custom_call" | custom-call | flops 12000000000 | bytes 1000000 | tf_op jit(solution)/shard_map/pallas_call | solution.py:528
  56.1 3.4 %collective-permute-start.10 = (f32[3,32,512]{2,1,0:T(8,128)S(1)}, f32[3,32,512]{2,1,0:T(8,128)S(1)}, u32[]{:S(2)}, u32[]{:S(2)}) collective-permute-start(f32[3,32,512]{2,1,0:T(8,128)S(1)} %get-tuple-element.42), channel_id=1, source_target_pairs={{0,8},{8,16},{16,24},{24,32},{32,40},{40,48},{48,56},{56,64},{64,7... | collective-permute-start | bytes 589832 | tf_op jit(solution)/shard_map/ppermute | solution.py:549
  59.6 4.5 %shard_map.99 = f32[1,2]{1,0:T(1,128)} custom-call(s32[1,1]{1,0:T(1,128)} %bitcast.1.core_ref, f32[4,2,256,256]{3,2,1,0:T(8,128)S(1)} %copy-done.2, f32[2,256,256]{2,1,0:T(8,128)S(1)} %copy-done.11, f32[32,9,8,128]{3,2,1,0:T(8,128)S(1)} %get-tuple-element.35.keep_ref, f32[32,9,8,128]{3,2,1,0:T(8,128)S(1)} %copy-done.4), custom_call_target="tpu_custom_call" | custom-call | flops 8000000000 | bytes 1000000 | tf_op jit(solution)/shard_map/pallas_call | solution.py:539
  64.1 4.6 %collective-permute-done.10.spilled_ref = f32[3,32,512]{2,1,0:T(8,128)S(1)} collective-permute-done((f32[3,32,512]{2,1,0:T(8,128)S(1)}, f32[3,32,512]{2,1,0:T(8,128)S(1)}, u32[]{:S(2)}, u32[]{:S(2)}) %collective-permute-start.10) | collective-permute-done | bytes 196640 | tf_op jit(solution)/shard_map/ppermute | solution.py:549
  68.8 8.2 %collective-permute-start.13 = (f32[9,8,128]{2,1,0:T(8,128)S(1)}, f32[9,8,128]{2,1,0:T(8,128)S(1)}, u32[]{:S(2)}, u32[]{:S(2)}) collective-permute-start(f32[9,8,128]{2,1,0:T(8,128)S(1)} %shard_map.100.first_ref), channel_id=1, source_target_pairs={{0,192},{64,0},{128,64},{192,128},{1,193},{65,1},{129,65},{193,129... | collective-permute-start | bytes 110600 | tf_op jit(solution)/shard_map/ppermute | solution.py:562
  77.0 2.0 %collective-permute-start.12 = (f32[9,8,128]{2,1,0:T(8,128)S(1)}, f32[9,8,128]{2,1,0:T(8,128)S(1)}, u32[]{:S(2)}, u32[]{:S(2)}) collective-permute-start(f32[9,8,128]{2,1,0:T(8,128)S(1)} %shard_map.100.first_ref), channel_id=1, source_target_pairs={{0,128},{64,192},{128,0},{192,64},{1,129},{65,193},{129,1},{193,65... | collective-permute-start | bytes 110600 | tf_op jit(solution)/shard_map/ppermute | solution.py:562
  79.0 1.3 %collective-permute-start.11 = (f32[9,8,128]{2,1,0:T(8,128)S(1)}, f32[9,8,128]{2,1,0:T(8,128)S(1)}, u32[]{:S(2)}, u32[]{:S(2)}) collective-permute-start(f32[9,8,128]{2,1,0:T(8,128)S(1)} %shard_map.100.first_ref), channel_id=1, source_target_pairs={{0,64},{64,128},{128,192},{192,0},{1,65},{65,129},{129,193},{193,1... | collective-permute-start | bytes 110600 | tf_op jit(solution)/shard_map/ppermute | solution.py:562
  80.2 3.5 %collective-permute-done.12.third_ref = f32[9,8,128]{2,1,0:T(8,128)S(1)} collective-permute-done((f32[9,8,128]{2,1,0:T(8,128)S(1)}, f32[9,8,128]{2,1,0:T(8,128)S(1)}, u32[]{:S(2)}, u32[]{:S(2)}) %collective-permute-start.12) | collective-permute-done | bytes 36896 | tf_op jit(solution)/shard_map/ppermute | solution.py:562
  84.1 1.6 %collective-permute-start.16 = (f32[2,32,512]{2,1,0:T(8,128)S(1)}, f32[2,32,512]{2,1,0:T(8,128)S(1)}, u32[]{:S(2)}, u32[]{:S(2)}) collective-permute-start(f32[2,32,512]{2,1,0:T(8,128)S(1)} %shard_map.98), channel_id=1, source_target_pairs={{0,6},{2,0},{4,2},{6,4},{1,7},{3,1},{5,3},{7,5},{8,14},{10,8},{12,... | collective-permute-start | bytes 393224 | tf_op jit(solution)/shard_map/ppermute | solution.py:562
  87.2 1.1 shard_map.101
  88.3 6.6 %all-to-all-start.1 = ((f32[32,8,8,128]{3,2,1,0:T(8,128)}), f32[32,8,8,128]{3,2,1,0:T(8,128)S(1)}, u32[]{:S(2)}, u32[]{:S(2)}) async-start(f32[32,8,8,128]{3,2,1,0:T(8,128)} %shard_map.101), calls=%async_computation.1 | async-start | bytes 2097152 | tf_op jit(solution)/shard_map/all_to_all | solution.py:582
  95.0 3.0 %collective-permute-start.17 = (f32[4,2,32,512]{3,2,1,0:T(8,128)S(1)}, f32[4,2,32,512]{3,2,1,0:T(8,128)S(1)}, u32[]{:S(2)}, u32[]{:S(2)}) collective-permute-start(f32[4,2,32,512]{3,2,1,0:T(8,128)S(1)} %pad_maximum_fusion.strip_ref), channel_id=1, source_target_pairs={{0,1},{1,0},{2,3},{3,2},{4,5},{5,4},{6,7},{7,6},{8,9},{9,8},{10,11... | collective-permute-start | bytes 1572872 | tf_op jit(solution)/shard_map/ppermute | solution.py:585
  98.0 1.5 %collective-permute-done.17.other_ref = f32[4,2,32,512]{3,2,1,0:T(8,128)S(1)} collective-permute-done((f32[4,2,32,512]{3,2,1,0:T(8,128)S(1)}, f32[4,2,32,512]{3,2,1,0:T(8,128)S(1)}, u32[]{:S(2)}, u32[]{:S(2)}) %collective-permute-start.17) | collective-permute-done | bytes 524320 | tf_op jit(solution)/shard_map/ppermute | solution.py:585
  100.6 7.6 %all-to-all-done.1.own_ref = f32[32,8,8,128]{3,2,1,0:T(8,128)S(1)} async-done(((f32[32,8,8,128]{3,2,1,0:T(8,128)}), f32[32,8,8,128]{3,2,1,0:T(8,128)S(1)}, u32[]{:S(2)}, u32[]{:S(2)}) %all-to-all-start.1) | async-done | bytes 1048608 | tf_op jit(solution)/shard_map/all_to_all | solution.py:582
  108.1 4.5 %collective-permute-start.18 = (f32[32,8,8,128]{3,2,1,0:T(8,128)S(1)}, f32[32,8,8,128]{3,2,1,0:T(8,128)S(1)}, u32[]{:S(2)}, u32[]{:S(2)}) collective-permute-start(f32[32,8,8,128]{3,2,1,0:T(8,128)S(1)} %all-to-all-done.1.own_ref), channel_id=1, source_target_pairs={{0,1},{1,0},{2,3},{3,2},{4,5},{5,4},{6,7},{7,6},{8,9},{9,8},{10,11... | collective-permute-start | bytes 3145736 | tf_op jit(solution)/shard_map/ppermute | solution.py:596
  112.7 2.3 %collective-permute-done.18.other_ref = f32[32,8,8,128]{3,2,1,0:T(8,128)S(1)} collective-permute-done((f32[32,8,8,128]{3,2,1,0:T(8,128)S(1)}, f32[32,8,8,128]{3,2,1,0:T(8,128)S(1)}, u32[]{:S(2)}, u32[]{:S(2)}) %collective-permute-start.18) | collective-permute-done | bytes 1048608 | tf_op jit(solution)/shard_map/ppermute | solution.py:596
  114.9 1.5 %shard_map.103 = f32[4,2,256,256]{3,2,1,0:T(8,128)} custom-call(s32[1,1]{1,0:T(1,128)} %bitcast.1.core_ref, f32[32,8,8,128]{3,2,1,0:T(8,128)S(1)} %all-to-all-done.1.own_ref, f32[32,8,8,128]{3,2,1,0:T(8,128)S(1)} %collective-permute-done.18.other_ref), custom_call_target="tpu_custom_call" | custom-call | flops 1000000000 | bytes 1000000 | tf_op jit(solution)/shard_map/pallas_call | solution.py:597
  (59 shorter events, 11.3 us)
Async XLA Ops:
  1.7 18.6 %copy-start = (f32[2,256,512]{2,1,0:T(8,128)S(1)}, f32[2,256,512]{2,1,0:T(8,128)}, u32[]{:S(2)}) copy-start(f32[2,256,512]{2,1,0:T(8,128)} %object_ref.3) | copy-start | bytes 3145732
  1.7 13.5 %collective-permute-start = (f32[2,128,512]{2,1,0:T(8,128)S(1)}, f32[2,128,512]{2,1,0:T(8,128)S(1)}, u32[]{:S(2)}, u32[]{:S(2)}) collective-permute-start(f32[2,128,512]{2,1,0:T(8,128)S(1)} %constant_dynamic-slice_fusion), channel_id=1, source_target_pairs={{8,0},{16,8},{24,16},{32,24},{40,32},{48,40},{56,48},{64,56},{72,6... | collective-permute-start | bytes 1572872 | tf_op jit(solution)/shard_map/ppermute | solution.py:469
  3.2 1.6 %copy-start.1 = (f32[4,2,256,256]{3,2,1,0:T(8,128)S(1)}, f32[4,2,256,256]{3,2,1,0:T(8,128)}, u32[]{:S(2)}) copy-start(f32[4,2,256,256]{3,2,1,0:T(8,128)} %probe_ref.3) | copy-start | bytes 6291460
  7.1 13.2 %copy-start.5 = (f32[1,256,256]{2,1,0:T(8,128)S(1)}, f32[1,256,256]{2,1,0:T(8,128)}, u32[]{:S(2)}) copy-start(f32[1,256,256]{2,1,0:T(8,128)} %amplitude_ref.1) | copy-start | bytes 786436
  7.1 13.2 %copy-start.10 = (s32[1,2]{1,0:T(1,128)S(1)}, s32[1,2]{1,0:T(1,128)}, u32[]{:S(2)}) copy-start(s32[1,2]{1,0:T(1,128)} %corner_ref.5) | copy-start | bytes 28
  7.1 13.2 %copy-start.13 = (f32[2,256,256]{2,1,0:T(8,128)S(1)}, f32[2,256,256]{2,1,0:T(8,128)}, u32[]{:S(2)}) copy-start(f32[2,256,256]{2,1,0:T(8,128)} %constant.20.clone.forward_ref) | copy-start | bytes 1572868
  15.3 5.0 %collective-permute-start.1 = (f32[2,128,512]{2,1,0:T(8,128)S(1)}, f32[2,128,512]{2,1,0:T(8,128)S(1)}, u32[]{:S(2)}, u32[]{:S(2)}) collective-permute-start(f32[2,128,512]{2,1,0:T(8,128)S(1)} %collective-permute-done.near_ref), channel_id=1, source_target_pairs={{0,1},{1,0},{2,3},{3,2},{4,5},{5,4},{6,7},{7,6},{8,9},{9,8},{10,11... | collective-permute-start | bytes 1572872 | tf_op jit(solution)/shard_map/ppermute | solution.py:482
  21.9 9.3 %copy-start.15 = (f32[4,256,256]{2,1,0:T(8,128)S(1)}, f32[4,256,256]{2,1,0:T(8,128)}, u32[]{:S(2)}) copy-start(f32[4,256,256]{2,1,0:T(8,128)} %copy-done.14) | copy-start | bytes 3145732
  31.2 4.2 %copy-start.6 = (f32[2,104,256]{2,1,0:T(8,128)}, f32[2,104,256]{2,1,0:T(8,128)S(1)}, u32[]{:S(2)}) copy-start(f32[2,104,256]{2,1,0:T(8,128)S(1)} %get-tuple-element.37.rest_0_) | copy-start | bytes 638980
  35.5 6.6 %copy-start.3 = (f32[32,9,8,128]{3,2,1,0:T(8,128)}, f32[32,9,8,128]{3,2,1,0:T(8,128)S(1)}, u32[]{:S(2)}) copy-start(f32[32,9,8,128]{3,2,1,0:T(8,128)S(1)} %get-tuple-element.36.send_ref) | copy-start | bytes 3538948
  35.5 5.4 %collective-permute-start.2 = (f32[32,9,8,128]{3,2,1,0:T(8,128)S(1)}, f32[32,9,8,128]{3,2,1,0:T(8,128)S(1)}, u32[]{:S(2)}, u32[]{:S(2)}) collective-permute-start(f32[32,9,8,128]{3,2,1,0:T(8,128)S(1)} %get-tuple-element.36.send_ref), channel_id=1, source_target_pairs={{0,1},{1,0},{2,3},{3,2},{4,5},{5,4},{6,7},{7,6},{8,9},{9,8},{10,11... | collective-permute-start | bytes 3538952 | tf_op jit(solution)/shard_map/ppermute | solution.py:526
  35.9 15.4 %collective-permute-start.3 = (f32[2,104,256]{2,1,0:T(8,128)}, f32[2,104,256]{2,1,0:T(8,128)}, u32[]{:S(2)}, u32[]{:S(2)}) collective-permute-start(f32[2,104,256]{2,1,0:T(8,128)} %get-tuple-element.38), channel_id=1, source_target_pairs={{0,2},{2,4},{4,6},{6,0},{1,3},{3,5},{5,7},{7,1},{8,10},{10,12},{12... | collective-permute-start | bytes 638984 | tf_op jit(solution)/shard_map/ppermute | solution.py:525
  37.3 14.4 %collective-permute-start.4 = (f32[2,104,256]{2,1,0:T(8,128)}, f32[2,104,256]{2,1,0:T(8,128)}, u32[]{:S(2)}, u32[]{:S(2)}) collective-permute-start(f32[2,104,256]{2,1,0:T(8,128)} %get-tuple-element.39), channel_id=1, source_target_pairs={{0,4},{2,6},{4,0},{6,2},{1,5},{3,7},{5,1},{7,3},{8,12},{10,14},{12... | collective-permute-start | bytes 638984 | tf_op jit(solution)/shard_map/ppermute | solution.py:525
  39.8 12.1 %collective-permute-start.5 = (f32[2,104,256]{2,1,0:T(8,128)}, f32[2,104,256]{2,1,0:T(8,128)}, u32[]{:S(2)}, u32[]{:S(2)}) collective-permute-start(f32[2,104,256]{2,1,0:T(8,128)} %get-tuple-element.40), channel_id=1, source_target_pairs={{0,6},{2,0},{4,2},{6,4},{1,7},{3,1},{5,3},{7,5},{8,14},{10,8},{12,... | collective-permute-start | bytes 638984 | tf_op jit(solution)/shard_map/ppermute | solution.py:525
  42.0 26.6 %all-to-all-start = ((f32[32,9,8,128]{3,2,1,0:T(8,128)}), f32[32,9,8,128]{3,2,1,0:T(8,128)S(1)}, u32[]{:S(2)}, u32[]{:S(2)}) async-start(f32[32,9,8,128]{3,2,1,0:T(8,128)} %add.11), calls=%async_computation | async-start | bytes 2359296 | tf_op jit(solution)/shard_map/all_to_all | solution.py:537
  50.0 9.5 %copy-start.2 = (f32[4,2,256,256]{3,2,1,0:T(8,128)S(1)}, f32[4,2,256,256]{3,2,1,0:T(8,128)}, u32[]{:S(2)}) copy-start(f32[4,2,256,256]{3,2,1,0:T(8,128)} %probe_ref.3) | copy-start | bytes 6291460
  50.1 9.5 %copy-start.4 = (f32[32,9,8,128]{3,2,1,0:T(8,128)S(1)}, f32[32,9,8,128]{3,2,1,0:T(8,128)}, u32[]{:S(2)}) copy-start(f32[32,9,8,128]{3,2,1,0:T(8,128)} %copy-done.3) | copy-start | bytes 3538948
  50.1 2.6 %collective-permute-start.6 = (f32[2,104,256]{2,1,0:T(8,128)}, f32[2,104,256]{2,1,0:T(8,128)S(1)}, u32[]{:S(2)}, u32[]{:S(2)}) collective-permute-start(f32[2,104,256]{2,1,0:T(8,128)} %copy-done.6), channel_id=1, source_target_pairs={{0,1},{1,0},{2,3},{3,2},{4,5},{5,4},{6,7},{7,6},{8,9},{9,8},{10,11... | collective-permute-start | bytes 638984 | tf_op jit(solution)/shard_map/ppermute | solution.py:527
  51.3 1.7 %collective-permute-start.7 = (f32[2,104,256]{2,1,0:T(8,128)}, f32[2,104,256]{2,1,0:T(8,128)S(1)}, u32[]{:S(2)}, u32[]{:S(2)}) collective-permute-start(f32[2,104,256]{2,1,0:T(8,128)} %collective-permute-done.3.rest_1_), channel_id=1, source_target_pairs={{0,1},{1,0},{2,3},{3,2},{4,5},{5,4},{6,7},{7,6},{8,9},{9,8},{10,11... | collective-permute-start | bytes 638984 | tf_op jit(solution)/shard_map/ppermute | solution.py:527
  51.7 1.7 %collective-permute-start.8 = (f32[2,104,256]{2,1,0:T(8,128)}, f32[2,104,256]{2,1,0:T(8,128)S(1)}, u32[]{:S(2)}, u32[]{:S(2)}) collective-permute-start(f32[2,104,256]{2,1,0:T(8,128)} %collective-permute-done.4.rest_2_), channel_id=1, source_target_pairs={{0,1},{1,0},{2,3},{3,2},{4,5},{5,4},{6,7},{7,6},{8,9},{9,8},{10,11... | collective-permute-start | bytes 638984 | tf_op jit(solution)/shard_map/ppermute | solution.py:527
  51.9 1.8 %collective-permute-start.9 = (f32[2,104,256]{2,1,0:T(8,128)}, f32[2,104,256]{2,1,0:T(8,128)S(1)}, u32[]{:S(2)}, u32[]{:S(2)}) collective-permute-start(f32[2,104,256]{2,1,0:T(8,128)} %collective-permute-done.5.rest_3_), channel_id=1, source_target_pairs={{0,1},{1,0},{2,3},{3,2},{4,5},{5,4},{6,7},{7,6},{8,9},{9,8},{10,11... | collective-permute-start | bytes 638984 | tf_op jit(solution)/shard_map/ppermute | solution.py:527
  54.6 5.0 %copy-start.11 = (f32[2,256,256]{2,1,0:T(8,128)S(1)}, f32[2,256,256]{2,1,0:T(8,128)}, u32[]{:S(2)}) copy-start(f32[2,256,256]{2,1,0:T(8,128)} %constant.21.clone.slope_ref) | copy-start | bytes 1572868
  56.1 12.5 %collective-permute-start.10 = (f32[3,32,512]{2,1,0:T(8,128)S(1)}, f32[3,32,512]{2,1,0:T(8,128)S(1)}, u32[]{:S(2)}, u32[]{:S(2)}) collective-permute-start(f32[3,32,512]{2,1,0:T(8,128)S(1)} %get-tuple-element.42), channel_id=1, source_target_pairs={{0,8},{8,16},{16,24},{24,32},{32,40},{40,48},{48,56},{56,64},{64,7... | collective-permute-start | bytes 589832 | tf_op jit(solution)/shard_map/ppermute | solution.py:549
  68.8 11.5 %collective-permute-start.13 = (f32[9,8,128]{2,1,0:T(8,128)S(1)}, f32[9,8,128]{2,1,0:T(8,128)S(1)}, u32[]{:S(2)}, u32[]{:S(2)}) collective-permute-start(f32[9,8,128]{2,1,0:T(8,128)S(1)} %shard_map.100.first_ref), channel_id=1, source_target_pairs={{0,192},{64,0},{128,64},{192,128},{1,193},{65,1},{129,65},{193,129... | collective-permute-start | bytes 110600 | tf_op jit(solution)/shard_map/ppermute | solution.py:562
  77.0 6.7 %collective-permute-start.12 = (f32[9,8,128]{2,1,0:T(8,128)S(1)}, f32[9,8,128]{2,1,0:T(8,128)S(1)}, u32[]{:S(2)}, u32[]{:S(2)}) collective-permute-start(f32[9,8,128]{2,1,0:T(8,128)S(1)} %shard_map.100.first_ref), channel_id=1, source_target_pairs={{0,128},{64,192},{128,0},{192,64},{1,129},{65,193},{129,1},{193,65... | collective-permute-start | bytes 110600 | tf_op jit(solution)/shard_map/ppermute | solution.py:562
  79.0 5.2 %collective-permute-start.11 = (f32[9,8,128]{2,1,0:T(8,128)S(1)}, f32[9,8,128]{2,1,0:T(8,128)S(1)}, u32[]{:S(2)}, u32[]{:S(2)}) collective-permute-start(f32[9,8,128]{2,1,0:T(8,128)S(1)} %shard_map.100.first_ref), channel_id=1, source_target_pairs={{0,64},{64,128},{128,192},{192,0},{1,65},{65,129},{129,193},{193,1... | collective-permute-start | bytes 110600 | tf_op jit(solution)/shard_map/ppermute | solution.py:562
  84.1 10.7 %collective-permute-start.16 = (f32[2,32,512]{2,1,0:T(8,128)S(1)}, f32[2,32,512]{2,1,0:T(8,128)S(1)}, u32[]{:S(2)}, u32[]{:S(2)}) collective-permute-start(f32[2,32,512]{2,1,0:T(8,128)S(1)} %shard_map.98), channel_id=1, source_target_pairs={{0,6},{2,0},{4,2},{6,4},{1,7},{3,1},{5,3},{7,5},{8,14},{10,8},{12,... | collective-permute-start | bytes 393224 | tf_op jit(solution)/shard_map/ppermute | solution.py:562
  85.8 9.1 %collective-permute-start.15 = (f32[2,32,512]{2,1,0:T(8,128)S(1)}, f32[2,32,512]{2,1,0:T(8,128)S(1)}, u32[]{:S(2)}, u32[]{:S(2)}) collective-permute-start(f32[2,32,512]{2,1,0:T(8,128)S(1)} %shard_map.98), channel_id=1, source_target_pairs={{0,4},{2,6},{4,0},{6,2},{1,5},{3,7},{5,1},{7,3},{8,12},{10,14},{12... | collective-permute-start | bytes 393224 | tf_op jit(solution)/shard_map/ppermute | solution.py:562
  86.6 8.3 %collective-permute-start.14 = (f32[2,32,512]{2,1,0:T(8,128)S(1)}, f32[2,32,512]{2,1,0:T(8,128)S(1)}, u32[]{:S(2)}, u32[]{:S(2)}) collective-permute-start(f32[2,32,512]{2,1,0:T(8,128)S(1)} %shard_map.98), channel_id=1, source_target_pairs={{0,2},{2,4},{4,6},{6,0},{1,3},{3,5},{5,7},{7,1},{8,10},{10,12},{12... | collective-permute-start | bytes 393224 | tf_op jit(solution)/shard_map/ppermute | solution.py:562
  88.3 19.8 %all-to-all-start.1 = ((f32[32,8,8,128]{3,2,1,0:T(8,128)}), f32[32,8,8,128]{3,2,1,0:T(8,128)S(1)}, u32[]{:S(2)}, u32[]{:S(2)}) async-start(f32[32,8,8,128]{3,2,1,0:T(8,128)} %shard_map.101), calls=%async_computation.1 | async-start | bytes 2097152 | tf_op jit(solution)/shard_map/all_to_all | solution.py:582
  95.0 4.6 %collective-permute-start.17 = (f32[4,2,32,512]{3,2,1,0:T(8,128)S(1)}, f32[4,2,32,512]{3,2,1,0:T(8,128)S(1)}, u32[]{:S(2)}, u32[]{:S(2)}) collective-permute-start(f32[4,2,32,512]{3,2,1,0:T(8,128)S(1)} %pad_maximum_fusion.strip_ref), channel_id=1, source_target_pairs={{0,1},{1,0},{2,3},{3,2},{4,5},{5,4},{6,7},{7,6},{8,9},{9,8},{10,11... | collective-permute-start | bytes 1572872 | tf_op jit(solution)/shard_map/ppermute | solution.py:585
  108.1 6.8 %collective-permute-start.18 = (f32[32,8,8,128]{3,2,1,0:T(8,128)S(1)}, f32[32,8,8,128]{3,2,1,0:T(8,128)S(1)}, u32[]{:S(2)}, u32[]{:S(2)}) collective-permute-start(f32[32,8,8,128]{3,2,1,0:T(8,128)S(1)} %all-to-all-done.1.own_ref), channel_id=1, source_target_pairs={{0,1},{1,0},{2,3},{3,2},{4,5},{5,4},{6,7},{7,6},{8,9},{9,8},{10,11... | collective-permute-start | bytes 3145736 | tf_op jit(solution)/shard_map/ppermute | solution.py:596
  (7 other events, 7.2 us)

commit v4 on v3

--- a/solution.py
+++ b/solution.py
@@ -474,7 +474,7 @@
         in_specs=[SMEM, SMEM, VMEM, VMEM],
         out_specs=(VMEM,) * 2,
         scratch_shapes=[stage, stage_left, wide, tall, matrix_right, matrix_left],
-        compiler_params=params(22),
+        compiler_params=params(60),
         cost_estimate=cost(8, 2048),
     )(positions, shifts, probe_modes, forward_table)
 
@@ -555,7 +555,7 @@
         compiler_params=params(4),
         cost_estimate=cost(1),
     )(owner_block, object_field, own, spilled)
-    scattered, updated, shift_grad = lax.optimization_barrier((scattered, updated, shift_grad))
+    scattered, shift_grad = lax.optimization_barrier((scattered, shift_grad))
 
     def around(value, axis):
         turns = [[(i, (i + step) % 4) for i in range(4)] for step in range(1, 4)]

time: 117 us -> 114 us (0.974)
  local copies, waits for them, and re-layouts: 9.87 us -> 4.34 us
  Pallas kernels: 29 us -> 33 us
    unnamed x36 -> x28, local copies, waits for them, and re-layouts: 8.78 us -> 3.26 us
    ppermute x1, waiting for transfers between devices: 4.57 us -> 0.01 us  [on_device(): spilled = lax.ppermute(spill, TILE, [(i, i + 1) for i in range(tiles - 1)])]
    ppermute x1, waiting for transfers between devices: 0.09 us -> 3.88 us  [on_device(): near = lax.ppermute(part_rows, TILE, [(i + 1, i) for i in range(tiles - 1)])]
    pallas_call x1, Pallas kernels: 5.76 us -> 8.23 us  [on_device(): pl.pallas_call(probe_kernel, out_shape=(shape(MODES, 2, SIDE, SIDE), shap...]
    ppermute x6, starting transfers between devices: 14.5 us -> 12.5 us  [around(): return [value] + [lax.ppermute(value, axis, turn) for turn in turns]]
  transfers between devices with their start and end apart: 21 -> 21, of which waited for: 12 -> 11; matrix products, arithmetic and copies ran while one was open for 1% -> 1% of each run, Pallas kernels for 12% -> 16%
where the time goes in v4:
time: 114 us
  starting transfers between devices  52.4 us (46%)
  Pallas kernels  33 us (29%)
  waiting for transfers between devices  22 us (19%)
  local copies, waits for them, and re-layouts  4.34 us (4%)
  other arithmetic  1.17 us (1%)
    ppermute x6, starting transfers between devices, around(): return [value] + [lax.ppermute(value, axis, turn) for turn in turns]  12.5 us
    pallas_call x1, Pallas kernels, on_device(): pl.pallas_call(pattern_kernel, out_shape=(shape(2, 3 * ROWS + 8, SIDE),)...  9.3 us
    pallas_call x1, Pallas kernels, on_device(): pl.pallas_call(probe_kernel, out_shape=(shape(MODES, 2, SIDE, SIDE), shap...  8.23 us
    all_to_all x1, starting transfers between devices, on_device(): scattered = lax.all_to_all(summed, PLANE, 0, 0)  7.97 us
    all_to_all x1, starting transfers between devices, on_device(): spread = lax.all_to_all(direction, PLANE, 0, 0)  7.51 us
    all_to_all x1, waiting for transfers between devices, on_device(): spread = lax.all_to_all(direction, PLANE, 0, 0)  7.3 us
    ppermute x3, starting transfers between devices, on_device(): lax.ppermute(blocks[steps], 'x', [(i, (i + steps) % 4) for i in range(4)])  4.98 us
    ppermute x1, starting transfers between devices, on_device(): spread_other = lax.ppermute(spread, 'c', cores)  4.63 us
  transfers between devices with their start and end apart: 21, of which 11 were waited for; matrix products, arithmetic and copies ran while one was open for 1% of the time, Pallas kernels for 16%

profile of v4, /device:TPU:1, one launch (start us, length us, event | category | flops | bytes accessed | tf_op | source)
XLA Modules:
  0.0 113.7 jit_solution(11234600702171999790)
XLA Ops:
  0.6 1.1 constant_dynamic-slice_fusion
  1.8 1.4 %collective-permute-start = (f32[2,128,512]{2,1,0:T(8,128)S(1)}, f32[2,128,512]{2,1,0:T(8,128)S(1)}, u32[]{:S(2)}, u32[]{:S(2)}) collective-permute-start(f32[2,128,512]{2,1,0:T(8,128)S(1)} %constant_dynamic-slice_fusion), channel_id=1, source_target_pairs={{8,0},{16,8},{24,16},{32,24},{40,32},{48,40},{56,48},{64,56},{72,6... | collective-permute-start | bytes 1572872 | tf_op jit(solution)/shard_map/ppermute | solution.py:469
  3.2 8.2 %shard_map.94 = (f32[4,2,256,256]{3,2,1,0:T(8,128)}, f32[4,256,256]{2,1,0:T(8,128)}) custom-call(s32[1,2]{1,0:T(1,128)} %corner_ref.5, f32[1,2]{1,0:T(1,128)} %shift_ref.1, f32[4,2,256,256]{3,2,1,0:T(8,128)} %probe_ref.3, f32[2,256,256]{2,1,0:T(8,128)} %constant.20.clone.forward_ref), custom_call_target="tpu_custom_call" | custom-call | flops 8000000000 | bytes 1000000 | tf_op jit(solution)/shard_map/pallas_call | solution.py:471
  11.4 3.9 %collective-permute-done.near_ref = f32[2,128,512]{2,1,0:T(8,128)S(1)} collective-permute-done((f32[2,128,512]{2,1,0:T(8,128)S(1)}, f32[2,128,512]{2,1,0:T(8,128)S(1)}, u32[]{:S(2)}, u32[]{:S(2)}) %collective-permute-start) | collective-permute-done | bytes 524320 | tf_op jit(solution)/shard_map/ppermute | solution.py:469
  15.3 3.5 %collective-permute-start.1 = (f32[2,128,512]{2,1,0:T(8,128)S(1)}, f32[2,128,512]{2,1,0:T(8,128)S(1)}, u32[]{:S(2)}, u32[]{:S(2)}) collective-permute-start(f32[2,128,512]{2,1,0:T(8,128)S(1)} %collective-permute-done.near_ref), channel_id=1, source_target_pairs={{0,1},{1,0},{2,3},{3,2},{4,5},{5,4},{6,7},{7,6},{8,9},{9,8},{10,11... | collective-permute-start | bytes 1572872 | tf_op jit(solution)/shard_map/ppermute | solution.py:482
  18.8 1.5 %collective-permute-done.1.far_ref = f32[2,128,512]{2,1,0:T(8,128)S(1)} collective-permute-done((f32[2,128,512]{2,1,0:T(8,128)S(1)}, f32[2,128,512]{2,1,0:T(8,128)S(1)}, u32[]{:S(2)}, u32[]{:S(2)}) %collective-permute-start.1) | collective-permute-done | bytes 524320 | tf_op jit(solution)/shard_map/ppermute | solution.py:482
  20.4 1.6 %copy-done.13 = f32[4,2,256,256]{3,2,1,0:T(8,128)S(1)} copy-done((f32[4,2,256,256]{3,2,1,0:T(8,128)S(1)}, f32[4,2,256,256]{3,2,1,0:T(8,128)}, u32[]{:S(2)}) %copy-start.13) | copy-done | bytes 2097176
  22.0 9.3 %shard_map.95 = (f32[2,104,256]{2,1,0:T(8,128)S(1)}, f32[2,104,256]{2,1,0:T(8,128)}, f32[2,104,256]{2,1,0:T(8,128)}, f32[2,104,256]{2,1,0:T(8,128)}, bf16[1024,1...) custom-call(s32[1,2]{1,0:T(1,128)S(1)} %copy-done.7, s32[1,1]{1,0:T(1,128)} %bitcast.owner_ref, f32[2,256,512]{2,1,0:T(8,128)S(1)} %copy-done, ...), custom_call_target="tpu_custom_call" | custom-call | flops 8000000000 | bytes 1000000 | tf_op jit(solution)/shard_map/pallas_call | solution.py:485
  31.3 4.2 %shard_map.96 = (f32[32,9,8,128]{3,2,1,0:T(8,128)S(1)}, f32[32,9,8,128]{3,2,1,0:T(8,128)S(1)}) custom-call(s32[1,2]{1,0:T(1,128)S(1)} %copy-done.7, s32[1,1]{1,0:T(1,128)} %bitcast.owner_ref, bf16[1024,1024]{1,0:T(8,128)(2,1)S(1)} %get-tuple-element.31.staged_ref, f32[256,256]{1,0:T(8,128)S(1)} %get-tuple-element.32.mass_ref, f32[4,256,256]{2,1,0:T(8,128)S(1)} %copy-done.12), custom_call_target="tpu_custom_call" | custom-call | flops 5000000000 | bytes 1000000 | tf_op jit(solution)/shard_map/pallas_call | solution.py:506
  36.0 1.4 %collective-permute-start.6 = (f32[2,104,256]{2,1,0:T(8,128)}, f32[2,104,256]{2,1,0:T(8,128)}, u32[]{:S(2)}, u32[]{:S(2)}) collective-permute-start(f32[2,104,256]{2,1,0:T(8,128)} %get-tuple-element.38), channel_id=1, source_target_pairs={{0,2},{2,4},{4,6},{6,0},{1,3},{3,5},{5,7},{7,1},{8,10},{10,12},{12... | collective-permute-start | bytes 638984 | tf_op jit(solution)/shard_map/ppermute | solution.py:525
  37.3 2.5 %collective-permute-start.7 = (f32[2,104,256]{2,1,0:T(8,128)}, f32[2,104,256]{2,1,0:T(8,128)}, u32[]{:S(2)}, u32[]{:S(2)}) collective-permute-start(f32[2,104,256]{2,1,0:T(8,128)} %get-tuple-element.39), channel_id=1, source_target_pairs={{0,4},{2,6},{4,0},{6,2},{1,5},{3,7},{5,1},{7,3},{8,12},{10,14},{12... | collective-permute-start | bytes 638984 | tf_op jit(solution)/shard_map/ppermute | solution.py:525
  39.8 1.1 %collective-permute-start.8 = (f32[2,104,256]{2,1,0:T(8,128)}, f32[2,104,256]{2,1,0:T(8,128)}, u32[]{:S(2)}, u32[]{:S(2)}) collective-permute-start(f32[2,104,256]{2,1,0:T(8,128)} %get-tuple-element.40), channel_id=1, source_target_pairs={{0,6},{2,0},{4,2},{6,4},{1,7},{3,1},{5,3},{7,5},{8,14},{10,8},{12,... | collective-permute-start | bytes 638984 | tf_op jit(solution)/shard_map/ppermute | solution.py:525
  41.0 1.1 add.11
  42.1 8.0 %all-to-all-start = ((f32[32,9,8,128]{3,2,1,0:T(8,128)}), f32[32,9,8,128]{3,2,1,0:T(8,128)S(1)}, u32[]{:S(2)}, u32[]{:S(2)}) async-start(f32[32,9,8,128]{3,2,1,0:T(8,128)} %add.11), calls=%async_computation | async-start | bytes 2359296 | tf_op jit(solution)/shard_map/all_to_all | solution.py:537
  50.1 1.3 %collective-permute-start.9 = (f32[2,104,256]{2,1,0:T(8,128)}, f32[2,104,256]{2,1,0:T(8,128)S(1)}, u32[]{:S(2)}, u32[]{:S(2)}) collective-permute-start(f32[2,104,256]{2,1,0:T(8,128)} %copy-done.5), channel_id=1, source_target_pairs={{0,1},{1,0},{2,3},{3,2},{4,5},{5,4},{6,7},{7,6},{8,9},{9,8},{10,11... | collective-permute-start | bytes 638984 | tf_op jit(solution)/shard_map/ppermute | solution.py:527
  54.6 2.1 %shard_map.99 = (f32[3,32,512]{2,1,0:T(8,128)S(1)}, f32[3,32,512]{2,1,0:T(8,128)}) custom-call(s32[1,1]{1,0:T(1,128)} %bitcast.owner_ref, f32[2,104,256]{2,1,0:T(8,128)S(1)} %copy-done.6, f32[2,104,256]{2,1,0:T(8,128)} %collective-permute-done.6.rest_1_, f32[2,104,256]{2,1,0:T(8,128)} %collective-permute-done.7.rest_2_, ...), custom_call_target="tpu_custom_call" | custom-call | flops 12000000000 | bytes 1000000 | tf_op jit(solution)/shard_map/pallas_call | solution.py:528
  57.4 4.1 %collective-permute-start.13 = (f32[3,32,512]{2,1,0:T(8,128)}, f32[3,32,512]{2,1,0:T(8,128)}, u32[]{:S(2)}, u32[]{:S(2)}) collective-permute-start(f32[3,32,512]{2,1,0:T(8,128)} %get-tuple-element.42), channel_id=1, source_target_pairs={{0,8},{8,16},{16,24},{24,32},{32,40},{40,48},{48,56},{56,64},{64,7... | collective-permute-start | bytes 589832 | tf_op jit(solution)/shard_map/ppermute | solution.py:549
  61.5 4.5 %shard_map.97 = f32[1,2]{1,0:T(1,128)} custom-call(s32[1,1]{1,0:T(1,128)} %bitcast.1.core_ref, f32[4,2,256,256]{3,2,1,0:T(8,128)S(1)} %copy-done.1, f32[2,256,256]{2,1,0:T(8,128)S(1)} %copy-done.8, f32[32,9,8,128]{3,2,1,0:T(8,128)S(1)} %get-tuple-element.34.keep_ref, f32[32,9,8,128]{3,2,1,0:T(8,128)S(1)} %copy-done.3), custom_call_target="tpu_custom_call" | custom-call | flops 8000000000 | bytes 1000000 | tf_op jit(solution)/shard_map/pallas_call | solution.py:539
  66.1 4.8 %collective-permute-start.5 = (f32[9,8,128]{2,1,0:T(8,128)S(1)}, f32[9,8,128]{2,1,0:T(8,128)S(1)}, u32[]{:S(2)}, u32[]{:S(2)}) collective-permute-start(f32[9,8,128]{2,1,0:T(8,128)S(1)} %shard_map.98.first_ref), channel_id=1, source_target_pairs={{0,192},{64,0},{128,64},{192,128},{1,193},{65,1},{129,65},{193,129... | collective-permute-start | bytes 110600 | tf_op jit(solution)/shard_map/ppermute | solution.py:562
  70.9 3.9 %collective-permute-start.4 = (f32[9,8,128]{2,1,0:T(8,128)S(1)}, f32[9,8,128]{2,1,0:T(8,128)S(1)}, u32[]{:S(2)}, u32[]{:S(2)}) collective-permute-start(f32[9,8,128]{2,1,0:T(8,128)S(1)} %shard_map.98.first_ref), channel_id=1, source_target_pairs={{0,128},{64,192},{128,0},{192,64},{1,129},{65,193},{129,1},{193,65... | collective-permute-start | bytes 110600 | tf_op jit(solution)/shard_map/ppermute | solution.py:562
  75.8 1.9 %collective-permute-done.4.third_ref = f32[9,8,128]{2,1,0:T(8,128)S(1)} collective-permute-done((f32[9,8,128]{2,1,0:T(8,128)S(1)}, f32[9,8,128]{2,1,0:T(8,128)S(1)}, u32[]{:S(2)}, u32[]{:S(2)}) %collective-permute-start.4) | collective-permute-done | bytes 36896 | tf_op jit(solution)/shard_map/ppermute | solution.py:562
  77.7 2.1 %collective-permute-done.3.second_ref = f32[9,8,128]{2,1,0:T(8,128)S(1)} collective-permute-done((f32[9,8,128]{2,1,0:T(8,128)S(1)}, f32[9,8,128]{2,1,0:T(8,128)S(1)}, u32[]{:S(2)}, u32[]{:S(2)}) %collective-permute-start.3) | collective-permute-done | bytes 36896 | tf_op jit(solution)/shard_map/ppermute | solution.py:562
  80.8 2.4 %collective-permute-start.15 = (f32[2,32,512]{2,1,0:T(8,128)S(1)}, f32[2,32,512]{2,1,0:T(8,128)S(1)}, u32[]{:S(2)}, u32[]{:S(2)}) collective-permute-start(f32[2,32,512]{2,1,0:T(8,128)S(1)} %shard_map.100), channel_id=1, source_target_pairs={{0,4},{2,6},{4,0},{6,2},{1,5},{3,7},{5,1},{7,3},{8,12},{10,14},{12... | collective-permute-start | bytes 393224 | tf_op jit(solution)/shard_map/ppermute | solution.py:562
  83.5 1.1 shard_map.101
  84.6 7.5 %all-to-all-start.1 = ((f32[32,8,8,128]{3,2,1,0:T(8,128)}), f32[32,8,8,128]{3,2,1,0:T(8,128)S(1)}, u32[]{:S(2)}, u32[]{:S(2)}) async-start(f32[32,8,8,128]{3,2,1,0:T(8,128)} %shard_map.101), calls=%async_computation.1 | async-start | bytes 2097152 | tf_op jit(solution)/shard_map/all_to_all | solution.py:582
  92.2 3.2 %collective-permute-start.17 = (f32[4,2,32,512]{3,2,1,0:T(8,128)S(1)}, f32[4,2,32,512]{3,2,1,0:T(8,128)S(1)}, u32[]{:S(2)}, u32[]{:S(2)}) collective-permute-start(f32[4,2,32,512]{3,2,1,0:T(8,128)S(1)} %pad_maximum_fusion.strip_ref), channel_id=1, source_target_pairs={{0,1},{1,0},{2,3},{3,2},{4,5},{5,4},{6,7},{7,6},{8,9},{9,8},{10,11... | collective-permute-start | bytes 1572872 | tf_op jit(solution)/shard_map/ppermute | solution.py:585
  95.4 1.5 %collective-permute-done.17.other_ref = f32[4,2,32,512]{3,2,1,0:T(8,128)S(1)} collective-permute-done((f32[4,2,32,512]{3,2,1,0:T(8,128)S(1)}, f32[4,2,32,512]{3,2,1,0:T(8,128)S(1)}, u32[]{:S(2)}, u32[]{:S(2)}) %collective-permute-start.17) | collective-permute-done | bytes 524320 | tf_op jit(solution)/shard_map/ppermute | solution.py:585
  97.0 1.0 shard_map.102
  98.0 7.3 %all-to-all-done.1.own_ref = f32[32,8,8,128]{3,2,1,0:T(8,128)S(1)} async-done(((f32[32,8,8,128]{3,2,1,0:T(8,128)}), f32[32,8,8,128]{3,2,1,0:T(8,128)S(1)}, u32[]{:S(2)}, u32[]{:S(2)}) %all-to-all-start.1) | async-done | bytes 1048608 | tf_op jit(solution)/shard_map/all_to_all | solution.py:582
  105.3 4.6 %collective-permute-start.18 = (f32[32,8,8,128]{3,2,1,0:T(8,128)S(1)}, f32[32,8,8,128]{3,2,1,0:T(8,128)S(1)}, u32[]{:S(2)}, u32[]{:S(2)}) collective-permute-start(f32[32,8,8,128]{3,2,1,0:T(8,128)S(1)} %all-to-all-done.1.own_ref), channel_id=1, source_target_pairs={{0,1},{1,0},{2,3},{3,2},{4,5},{5,4},{6,7},{7,6},{8,9},{9,8},{10,11... | collective-permute-start | bytes 3145736 | tf_op jit(solution)/shard_map/ppermute | solution.py:596
  109.9 2.3 %collective-permute-done.18.other_ref = f32[32,8,8,128]{3,2,1,0:T(8,128)S(1)} collective-permute-done((f32[32,8,8,128]{3,2,1,0:T(8,128)S(1)}, f32[32,8,8,128]{3,2,1,0:T(8,128)S(1)}, u32[]{:S(2)}, u32[]{:S(2)}) %collective-permute-start.18) | collective-permute-done | bytes 1048608 | tf_op jit(solution)/shard_map/ppermute | solution.py:596
  112.2 1.5 %shard_map.103 = f32[4,2,256,256]{3,2,1,0:T(8,128)} custom-call(s32[1,1]{1,0:T(1,128)} %bitcast.1.core_ref, f32[32,8,8,128]{3,2,1,0:T(8,128)S(1)} %all-to-all-done.1.own_ref, f32[32,8,8,128]{3,2,1,0:T(8,128)S(1)} %collective-permute-done.18.other_ref), custom_call_target="tpu_custom_call" | custom-call | flops 1000000000 | bytes 1000000 | tf_op jit(solution)/shard_map/pallas_call | solution.py:597
  (51 shorter events, 7.0 us)
Async XLA Ops:
  1.7 18.6 %copy-start = (f32[2,256,512]{2,1,0:T(8,128)S(1)}, f32[2,256,512]{2,1,0:T(8,128)}, u32[]{:S(2)}) copy-start(f32[2,256,512]{2,1,0:T(8,128)} %object_ref.3) | copy-start | bytes 3145732
  1.7 18.6 %copy-start.4 = (f32[1,256,256]{2,1,0:T(8,128)S(1)}, f32[1,256,256]{2,1,0:T(8,128)}, u32[]{:S(2)}) copy-start(f32[1,256,256]{2,1,0:T(8,128)} %amplitude_ref.1) | copy-start | bytes 786436
  1.7 18.6 %copy-start.7 = (s32[1,2]{1,0:T(1,128)S(1)}, s32[1,2]{1,0:T(1,128)}, u32[]{:S(2)}) copy-start(s32[1,2]{1,0:T(1,128)} %corner_ref.5) | copy-start | bytes 28
  1.8 18.6 %copy-start.9 = (f32[2,256,256]{2,1,0:T(8,128)S(1)}, f32[2,256,256]{2,1,0:T(8,128)}, u32[]{:S(2)}) copy-start(f32[2,256,256]{2,1,0:T(8,128)} %constant.20.clone.forward_ref) | copy-start | bytes 1572868
  1.8 13.5 %collective-permute-start = (f32[2,128,512]{2,1,0:T(8,128)S(1)}, f32[2,128,512]{2,1,0:T(8,128)S(1)}, u32[]{:S(2)}, u32[]{:S(2)}) collective-permute-start(f32[2,128,512]{2,1,0:T(8,128)S(1)} %constant_dynamic-slice_fusion), channel_id=1, source_target_pairs={{8,0},{16,8},{24,16},{32,24},{40,32},{48,40},{56,48},{64,56},{72,6... | collective-permute-start | bytes 1572872 | tf_op jit(solution)/shard_map/ppermute | solution.py:469
  15.3 5.0 %collective-permute-start.1 = (f32[2,128,512]{2,1,0:T(8,128)S(1)}, f32[2,128,512]{2,1,0:T(8,128)S(1)}, u32[]{:S(2)}, u32[]{:S(2)}) collective-permute-start(f32[2,128,512]{2,1,0:T(8,128)S(1)} %collective-permute-done.near_ref), channel_id=1, source_target_pairs={{0,1},{1,0},{2,3},{3,2},{4,5},{5,4},{6,7},{7,6},{8,9},{9,8},{10,11... | collective-permute-start | bytes 1572872 | tf_op jit(solution)/shard_map/ppermute | solution.py:482
  22.0 9.3 %copy-start.12 = (f32[4,256,256]{2,1,0:T(8,128)S(1)}, f32[4,256,256]{2,1,0:T(8,128)}, u32[]{:S(2)}) copy-start(f32[4,256,256]{2,1,0:T(8,128)} %get-tuple-element.33.adjoint_ref) | copy-start | bytes 3145732
  31.3 4.2 %copy-start.5 = (f32[2,104,256]{2,1,0:T(8,128)}, f32[2,104,256]{2,1,0:T(8,128)S(1)}, u32[]{:S(2)}) copy-start(f32[2,104,256]{2,1,0:T(8,128)S(1)} %get-tuple-element.37.rest_0_) | copy-start | bytes 638980
  35.5 6.6 %copy-start.2 = (f32[32,9,8,128]{3,2,1,0:T(8,128)}, f32[32,9,8,128]{3,2,1,0:T(8,128)S(1)}, u32[]{:S(2)}) copy-start(f32[32,9,8,128]{3,2,1,0:T(8,128)S(1)} %get-tuple-element.35.send_ref) | copy-start | bytes 3538948
  35.5 5.4 %collective-permute-start.2 = (f32[32,9,8,128]{3,2,1,0:T(8,128)S(1)}, f32[32,9,8,128]{3,2,1,0:T(8,128)S(1)}, u32[]{:S(2)}, u32[]{:S(2)}) collective-permute-start(f32[32,9,8,128]{3,2,1,0:T(8,128)S(1)} %get-tuple-element.35.send_ref), channel_id=1, source_target_pairs={{0,1},{1,0},{2,3},{3,2},{4,5},{5,4},{6,7},{7,6},{8,9},{9,8},{10,11... | collective-permute-start | bytes 3538952 | tf_op jit(solution)/shard_map/ppermute | solution.py:526
  36.0 15.4 %collective-permute-start.6 = (f32[2,104,256]{2,1,0:T(8,128)}, f32[2,104,256]{2,1,0:T(8,128)}, u32[]{:S(2)}, u32[]{:S(2)}) collective-permute-start(f32[2,104,256]{2,1,0:T(8,128)} %get-tuple-element.38), channel_id=1, source_target_pairs={{0,2},{2,4},{4,6},{6,0},{1,3},{3,5},{5,7},{7,1},{8,10},{10,12},{12... | collective-permute-start | bytes 638984 | tf_op jit(solution)/shard_map/ppermute | solution.py:525
  37.3 14.4 %collective-permute-start.7 = (f32[2,104,256]{2,1,0:T(8,128)}, f32[2,104,256]{2,1,0:T(8,128)}, u32[]{:S(2)}, u32[]{:S(2)}) collective-permute-start(f32[2,104,256]{2,1,0:T(8,128)} %get-tuple-element.39), channel_id=1, source_target_pairs={{0,4},{2,6},{4,0},{6,2},{1,5},{3,7},{5,1},{7,3},{8,12},{10,14},{12... | collective-permute-start | bytes 638984 | tf_op jit(solution)/shard_map/ppermute | solution.py:525
  39.8 12.1 %collective-permute-start.8 = (f32[2,104,256]{2,1,0:T(8,128)}, f32[2,104,256]{2,1,0:T(8,128)}, u32[]{:S(2)}, u32[]{:S(2)}) collective-permute-start(f32[2,104,256]{2,1,0:T(8,128)} %get-tuple-element.40), channel_id=1, source_target_pairs={{0,6},{2,0},{4,2},{6,4},{1,7},{3,1},{5,3},{7,5},{8,14},{10,8},{12,... | collective-permute-start | bytes 638984 | tf_op jit(solution)/shard_map/ppermute | solution.py:525
  42.1 23.9 %all-to-all-start = ((f32[32,9,8,128]{3,2,1,0:T(8,128)}), f32[32,9,8,128]{3,2,1,0:T(8,128)S(1)}, u32[]{:S(2)}, u32[]{:S(2)}) async-start(f32[32,9,8,128]{3,2,1,0:T(8,128)} %add.11), calls=%async_computation | async-start | bytes 2359296 | tf_op jit(solution)/shard_map/all_to_all | solution.py:537
  50.1 11.4 %copy-start.1 = (f32[4,2,256,256]{3,2,1,0:T(8,128)S(1)}, f32[4,2,256,256]{3,2,1,0:T(8,128)}, u32[]{:S(2)}) copy-start(f32[4,2,256,256]{3,2,1,0:T(8,128)} %probe_ref.3) | copy-start | bytes 6291460
  50.1 11.4 %copy-start.3 = (f32[32,9,8,128]{3,2,1,0:T(8,128)S(1)}, f32[32,9,8,128]{3,2,1,0:T(8,128)}, u32[]{:S(2)}) copy-start(f32[32,9,8,128]{3,2,1,0:T(8,128)} %copy-done.2) | copy-start | bytes 3538948
  50.1 2.6 %collective-permute-start.9 = (f32[2,104,256]{2,1,0:T(8,128)}, f32[2,104,256]{2,1,0:T(8,128)S(1)}, u32[]{:S(2)}, u32[]{:S(2)}) collective-permute-start(f32[2,104,256]{2,1,0:T(8,128)} %copy-done.5), channel_id=1, source_target_pairs={{0,1},{1,0},{2,3},{3,2},{4,5},{5,4},{6,7},{7,6},{8,9},{9,8},{10,11... | collective-permute-start | bytes 638984 | tf_op jit(solution)/shard_map/ppermute | solution.py:527
  51.4 1.7 %collective-permute-start.10 = (f32[2,104,256]{2,1,0:T(8,128)}, f32[2,104,256]{2,1,0:T(8,128)S(1)}, u32[]{:S(2)}, u32[]{:S(2)}) collective-permute-start(f32[2,104,256]{2,1,0:T(8,128)} %collective-permute-done.6.rest_1_), channel_id=1, source_target_pairs={{0,1},{1,0},{2,3},{3,2},{4,5},{5,4},{6,7},{7,6},{8,9},{9,8},{10,11... | collective-permute-start | bytes 638984 | tf_op jit(solution)/shard_map/ppermute | solution.py:527
  51.7 1.7 %collective-permute-start.11 = (f32[2,104,256]{2,1,0:T(8,128)}, f32[2,104,256]{2,1,0:T(8,128)S(1)}, u32[]{:S(2)}, u32[]{:S(2)}) collective-permute-start(f32[2,104,256]{2,1,0:T(8,128)} %collective-permute-done.7.rest_2_), channel_id=1, source_target_pairs={{0,1},{1,0},{2,3},{3,2},{4,5},{5,4},{6,7},{7,6},{8,9},{9,8},{10,11... | collective-permute-start | bytes 638984 | tf_op jit(solution)/shard_map/ppermute | solution.py:527
  51.9 1.8 %collective-permute-start.12 = (f32[2,104,256]{2,1,0:T(8,128)}, f32[2,104,256]{2,1,0:T(8,128)S(1)}, u32[]{:S(2)}, u32[]{:S(2)}) collective-permute-start(f32[2,104,256]{2,1,0:T(8,128)} %collective-permute-done.8.rest_3_), channel_id=1, source_target_pairs={{0,1},{1,0},{2,3},{3,2},{4,5},{5,4},{6,7},{7,6},{8,9},{9,8},{10,11... | collective-permute-start | bytes 638984 | tf_op jit(solution)/shard_map/ppermute | solution.py:527
  54.6 6.9 %copy-start.8 = (f32[2,256,256]{2,1,0:T(8,128)S(1)}, f32[2,256,256]{2,1,0:T(8,128)}, u32[]{:S(2)}) copy-start(f32[2,256,256]{2,1,0:T(8,128)} %constant.21.clone.slope_ref) | copy-start | bytes 1572868
  57.4 17.5 %collective-permute-start.13 = (f32[3,32,512]{2,1,0:T(8,128)}, f32[3,32,512]{2,1,0:T(8,128)}, u32[]{:S(2)}, u32[]{:S(2)}) collective-permute-start(f32[3,32,512]{2,1,0:T(8,128)} %get-tuple-element.42), channel_id=1, source_target_pairs={{0,8},{8,16},{16,24},{24,32},{32,40},{40,48},{48,56},{56,64},{64,7... | collective-permute-start | bytes 589832 | tf_op jit(solution)/shard_map/ppermute | solution.py:549
  66.0 8.8 %copy-start.11 = (f32[3,32,512]{2,1,0:T(8,128)S(1)}, f32[3,32,512]{2,1,0:T(8,128)}, u32[]{:S(2)}) copy-start(f32[3,32,512]{2,1,0:T(8,128)} %copy-done.10) | copy-start | bytes 589828
  66.1 9.7 %collective-permute-start.5 = (f32[9,8,128]{2,1,0:T(8,128)S(1)}, f32[9,8,128]{2,1,0:T(8,128)S(1)}, u32[]{:S(2)}, u32[]{:S(2)}) collective-permute-start(f32[9,8,128]{2,1,0:T(8,128)S(1)} %shard_map.98.first_ref), channel_id=1, source_target_pairs={{0,192},{64,0},{128,64},{192,128},{1,193},{65,1},{129,65},{193,129... | collective-permute-start | bytes 110600 | tf_op jit(solution)/shard_map/ppermute | solution.py:562
  70.9 6.7 %collective-permute-start.4 = (f32[9,8,128]{2,1,0:T(8,128)S(1)}, f32[9,8,128]{2,1,0:T(8,128)S(1)}, u32[]{:S(2)}, u32[]{:S(2)}) collective-permute-start(f32[9,8,128]{2,1,0:T(8,128)S(1)} %shard_map.98.first_ref), channel_id=1, source_target_pairs={{0,128},{64,192},{128,0},{192,64},{1,129},{65,193},{129,1},{193,65... | collective-permute-start | bytes 110600 | tf_op jit(solution)/shard_map/ppermute | solution.py:562
  74.8 4.9 %collective-permute-start.3 = (f32[9,8,128]{2,1,0:T(8,128)S(1)}, f32[9,8,128]{2,1,0:T(8,128)S(1)}, u32[]{:S(2)}, u32[]{:S(2)}) collective-permute-start(f32[9,8,128]{2,1,0:T(8,128)S(1)} %shard_map.98.first_ref), channel_id=1, source_target_pairs={{0,64},{64,128},{128,192},{192,0},{1,65},{65,129},{129,193},{193,1... | collective-permute-start | bytes 110600 | tf_op jit(solution)/shard_map/ppermute | solution.py:562
  79.7 12.4 %collective-permute-start.16 = (f32[2,32,512]{2,1,0:T(8,128)S(1)}, f32[2,32,512]{2,1,0:T(8,128)S(1)}, u32[]{:S(2)}, u32[]{:S(2)}) collective-permute-start(f32[2,32,512]{2,1,0:T(8,128)S(1)} %shard_map.100), channel_id=1, source_target_pairs={{0,6},{2,0},{4,2},{6,4},{1,7},{3,1},{5,3},{7,5},{8,14},{10,8},{12,... | collective-permute-start | bytes 393224 | tf_op jit(solution)/shard_map/ppermute | solution.py:562
  80.8 11.4 %collective-permute-start.15 = (f32[2,32,512]{2,1,0:T(8,128)S(1)}, f32[2,32,512]{2,1,0:T(8,128)S(1)}, u32[]{:S(2)}, u32[]{:S(2)}) collective-permute-start(f32[2,32,512]{2,1,0:T(8,128)S(1)} %shard_map.100), channel_id=1, source_target_pairs={{0,4},{2,6},{4,0},{6,2},{1,5},{3,7},{5,1},{7,3},{8,12},{10,14},{12... | collective-permute-start | bytes 393224 | tf_op jit(solution)/shard_map/ppermute | solution.py:562
  83.1 9.0 %collective-permute-start.14 = (f32[2,32,512]{2,1,0:T(8,128)S(1)}, f32[2,32,512]{2,1,0:T(8,128)S(1)}, u32[]{:S(2)}, u32[]{:S(2)}) collective-permute-start(f32[2,32,512]{2,1,0:T(8,128)S(1)} %shard_map.100), channel_id=1, source_target_pairs={{0,2},{2,4},{4,6},{6,0},{1,3},{3,5},{5,7},{7,1},{8,10},{10,12},{12... | collective-permute-start | bytes 393224 | tf_op jit(solution)/shard_map/ppermute | solution.py:562
  84.6 20.7 %all-to-all-start.1 = ((f32[32,8,8,128]{3,2,1,0:T(8,128)}), f32[32,8,8,128]{3,2,1,0:T(8,128)S(1)}, u32[]{:S(2)}, u32[]{:S(2)}) async-start(f32[32,8,8,128]{3,2,1,0:T(8,128)} %shard_map.101), calls=%async_computation.1 | async-start | bytes 2097152 | tf_op jit(solution)/shard_map/all_to_all | solution.py:582
  92.2 4.7 %collective-permute-start.17 = (f32[4,2,32,512]{3,2,1,0:T(8,128)S(1)}, f32[4,2,32,512]{3,2,1,0:T(8,128)S(1)}, u32[]{:S(2)}, u32[]{:S(2)}) collective-permute-start(f32[4,2,32,512]{3,2,1,0:T(8,128)S(1)} %pad_maximum_fusion.strip_ref), channel_id=1, source_target_pairs={{0,1},{1,0},{2,3},{3,2},{4,5},{5,4},{6,7},{7,6},{8,9},{9,8},{10,11... | collective-permute-start | bytes 1572872 | tf_op jit(solution)/shard_map/ppermute | solution.py:585
  105.3 6.9 %collective-permute-start.18 = (f32[32,8,8,128]{3,2,1,0:T(8,128)S(1)}, f32[32,8,8,128]{3,2,1,0:T(8,128)S(1)}, u32[]{:S(2)}, u32[]{:S(2)}) collective-permute-start(f32[32,8,8,128]{3,2,1,0:T(8,128)S(1)} %all-to-all-done.1.own_ref), channel_id=1, source_target_pairs={{0,1},{1,0},{2,3},{3,2},{4,5},{5,4},{6,7},{7,6},{8,9},{9,8},{10,11... | collective-permute-start | bytes 3145736 | tf_op jit(solution)/shard_map/ppermute | solution.py:596
  (3 other events, 3.2 us)

commit v5 on v4

--- a/solution.py
+++ b/solution.py
@@ -109,8 +109,11 @@
     shift_ref,
     probe_ref,
     forward_ref,
+    slope_ref,
     shifted_ref,
     adjoint_ref,
+    slope_rows_ref,
+    slope_cols_ref,
     stage,
     stage_left,
     wide,
@@ -163,6 +166,15 @@
         cols = slice(k * SIDE, (k + 1) * SIDE)
         shifted_ref[k, 0] = tall[:SIDE, cols]
         shifted_ref[k, 1] = tall[SIDE:, cols]
+
+    slope_real = slope_ref[0]
+    slope_imag = slope_ref[1]
+    fill_left(matrix_left, slope_real, slope_imag)
+    fill_right(matrix_right, slope_real.T, slope_imag.T)
+    for k in range(MODES):
+        put_left(stage_left, k * SIDE, probe_ref[k, 0], probe_ref[k, 1])
+    slope_rows_ref[...] = from_left(matrix_left, stage_left)
+    slope_cols_ref[...] = from_right(stage, matrix_right)
 
 
 def partner(owner, steps, turn):
@@ -307,30 +319,8 @@
         scatter(target, 2 * MODES, mass[pl.ds(base, half), :])
 
 
-def slope_kernel(
-    core_ref,
-    probe_ref,
-    slope_ref,
-    keep_ref,
-    send_ref,
-    shift_grad_ref,
-    stage,
-    stage_left,
-    wide,
-    tall,
-    matrix_left,
-    matrix_right,
-):
+def slope_kernel(core_ref, tall, wide, keep_ref, send_ref, shift_grad_ref):
     first = core_ref[0, 0] == 0
-    slope_real = slope_ref[0]
-    slope_imag = slope_ref[1]
-    fill_left(matrix_left, slope_real, slope_imag)
-    fill_right(matrix_right, slope_real.T, slope_imag.T)
-    for k in range(MODES):
-        put_right(stage, k * SIDE, probe_ref[k, 0], probe_ref[k, 1])
-        put_left(stage_left, k * SIDE, probe_ref[k, 0], probe_ref[k, 1])
-    tall[...] = from_left(matrix_left, stage_left)
-    wide[...] = from_right(stage, matrix_right)
     row_dot = jnp.zeros((8, LANES), f32)
     col_dot = jnp.zeros((8, LANES), f32)
     for piece in range(2 * PARTS):
@@ -468,15 +458,16 @@
     part_rows = lax.dynamic_slice_in_dim(object_field, core * half, half, axis=1)
     near = lax.ppermute(part_rows, TILE, [(i + 1, i) for i in range(tiles - 1)])
 
-    shifted, adjoint = pl.pallas_call(
+    shifted, adjoint, slope_rows, slope_cols = pl.pallas_call(
         probe_kernel,
-        out_shape=(shape(MODES, 2, SIDE, SIDE), shape(4, SIDE, SIDE)),
-        in_specs=[SMEM, SMEM, VMEM, VMEM],
-        out_specs=(VMEM,) * 2,
+        out_shape=(shape(MODES, 2, SIDE, SIDE), shape(4, SIDE, SIDE))
+        + (shape(WIDE, MODES * SIDE), shape(MODES * SIDE, WIDE)),
+        in_specs=[SMEM, SMEM, VMEM, VMEM, VMEM],
+        out_specs=(VMEM,) * 4,
         scratch_shapes=[stage, stage_left, wide, tall, matrix_right, matrix_left],
         compiler_params=params(60),
         cost_estimate=cost(8, 2048),
-    )(positions, shifts, probe_modes, forward_table)
+    )(positions, shifts, probe_modes, forward_table, jnp.asarray(two_parts(slope)))
 
     near, shifted, adjoint = lax.optimization_barrier((near, shifted, adjoint))
     far = lax.ppermute(near, "c", cores)
@@ -541,10 +532,9 @@
         out_shape=shape(1, 2),
         in_specs=[SMEM] + [VMEM] * 4,
         out_specs=SMEM,
-        scratch_shapes=[stage, stage_left, wide, tall, matrix_left, matrix_right],
-        compiler_params=params(22),
+        compiler_params=params(12),
         cost_estimate=cost(8),
-    )(core_block, probe_modes, jnp.asarray(two_parts(slope)), keep, send)
+    )(core_block, slope_rows, slope_cols, keep, send)
 
     spilled = lax.ppermute(spill, TILE, [(i, i + 1) for i in range(tiles - 1)])
     updated = pl.pallas_call(

time: 114 us -> 113 us (level)
  waiting for transfers between devices: 22 us -> 19.1 us
  starting transfers between devices: 52.4 us -> 53.7 us
    ppermute x1, waiting for transfers between devices: 3.88 us -> 0.46 us  [on_device(): near = lax.ppermute(part_rows, TILE, [(i + 1, i) for i in range(tiles - 1)])]
    pallas_call x1, Pallas kernels: 8.23 us -> 11.7 us  [on_device(): pl.pallas_call(probe_kernel, out_shape=(shape(MODES, 2, SIDE, SIDE), shap...]
    pallas_call x1, Pallas kernels: 4.5 us -> 1.18 us  [on_device(): pl.pallas_call(slope_kernel, out_shape=shape(1, 2), in_specs=[SMEM] + [VM...]
    all_to_all x1, waiting for transfers between devices: 0.03 us -> 3.29 us  [on_device(): scattered = lax.all_to_all(summed, PLANE, 0, 0)]
    all_to_all x1, waiting for transfers between devices: 7.3 us -> 4.6 us  [on_device(): spread = lax.all_to_all(direction, PLANE, 0, 0)]
    ppermute x1, starting transfers between devices: 4.63 us -> 5.99 us  [on_device(): spread_other = lax.ppermute(spread, 'c', cores)]
    ppermute x1, starting transfers between devices: 3.19 us -> 4.53 us  [on_device(): strip_other = lax.ppermute(strip, 'c', cores)]
  transfers between devices with their start and end apart: 21 -> 21, of which waited for: 11 -> 12; matrix products, arithmetic and copies ran while one was open for 1% -> 1% of each run, Pallas kernels for 16% -> 16%
where the time goes in v5:
time: 113 us; the launch traced here: 112 us
  starting transfers between devices  53.7 us (48%)
  Pallas kernels  33.1 us (29%)
  waiting for transfers between devices  19.1 us (17%)
  local copies, waits for them, and re-layouts  4.34 us (4%)
  other arithmetic  1.17 us (1%)
    ppermute x6, starting transfers between devices, around(): return [value] + [lax.ppermute(value, axis, turn) for turn in turns]  12.2 us
    pallas_call x1, Pallas kernels, on_device(): pl.pallas_call(probe_kernel, out_shape=(shape(MODES, 2, SIDE, SIDE), shap...  11.7 us
    pallas_call x1, Pallas kernels, on_device(): pl.pallas_call(pattern_kernel, out_shape=(shape(2, 3 * ROWS + 8, SIDE),)...  9.29 us
    all_to_all x1, starting transfers between devices, on_device(): scattered = lax.all_to_all(summed, PLANE, 0, 0)  7.97 us
    all_to_all x1, starting transfers between devices, on_device(): spread = lax.all_to_all(direction, PLANE, 0, 0)  6.49 us
    ppermute x1, starting transfers between devices, on_device(): spread_other = lax.ppermute(spread, 'c', cores)  5.99 us
    ppermute x3, starting transfers between devices, on_device(): lax.ppermute(blocks[steps], 'x', [(i, (i + steps) % 4) for i in range(4)])  4.98 us
    all_to_all x1, waiting for transfers between devices, on_device(): spread = lax.all_to_all(direction, PLANE, 0, 0)  4.6 us
  transfers between devices with their start and end apart: 21, of which 12 were waited for; matrix products, arithmetic and copies ran while one was open for 1% of the time, Pallas kernels for 16%

profile of v5, /device:TPU:1, one launch (start us, length us, event | category | flops | bytes accessed | tf_op | source)
XLA Modules:
  0.0 112.3 jit_solution(11811105931776619100)
XLA Ops:
  0.6 1.1 constant_dynamic-slice_fusion
  1.8 1.4 %collective-permute-start = (f32[2,128,512]{2,1,0:T(8,128)S(1)}, f32[2,128,512]{2,1,0:T(8,128)S(1)}, u32[]{:S(2)}, u32[]{:S(2)}) collective-permute-start(f32[2,128,512]{2,1,0:T(8,128)S(1)} %constant_dynamic-slice_fusion), channel_id=1, source_target_pairs={{8,0},{16,8},{24,16},{32,24},{40,32},{48,40},{56,48},{64,56},{72,6... | collective-permute-start | bytes 1572872 | tf_op jit(solution)/shard_map/ppermute | solution.py:459
  3.2 11.7 %shard_map.94 = (f32[4,2,256,256]{3,2,1,0:T(8,128)}, f32[4,256,256]{2,1,0:T(8,128)}, f32[512,1024]{1,0:T(8,128)}, f32[1024,512]{1,0:T(8,128)}) custom-call(s32[1,2]{1,0:T(1,128)} %corner_ref.5, f32[1,2]{1,0:T(1,128)} %shift_ref.1, f32[4,2,256,256]{3,2,1,0:T(8,128)} %probe_ref.1, f32[2,256,256]{2,1,0:T(8,128)} %constant.20.clone.forward_ref, ...), custom_call_target="tpu_custom_call" | custom-call | flops 8000000000 | bytes 1000000 | tf_op jit(solution)/shard_map/pallas_call | solution.py:461
  15.3 3.5 %collective-permute-start.1 = (f32[2,128,512]{2,1,0:T(8,128)S(1)}, f32[2,128,512]{2,1,0:T(8,128)S(1)}, u32[]{:S(2)}, u32[]{:S(2)}) collective-permute-start(f32[2,128,512]{2,1,0:T(8,128)S(1)} %collective-permute-done.near_ref), channel_id=1, source_target_pairs={{0,1},{1,0},{2,3},{3,2},{4,5},{5,4},{6,7},{7,6},{8,9},{9,8},{10,11... | collective-permute-start | bytes 1572872 | tf_op jit(solution)/shard_map/ppermute | solution.py:473
  18.8 1.5 %collective-permute-done.1.far_ref = f32[2,128,512]{2,1,0:T(8,128)S(1)} collective-permute-done((f32[2,128,512]{2,1,0:T(8,128)S(1)}, f32[2,128,512]{2,1,0:T(8,128)S(1)}, u32[]{:S(2)}, u32[]{:S(2)}) %collective-permute-start.1) | collective-permute-done | bytes 524320 | tf_op jit(solution)/shard_map/ppermute | solution.py:473
  20.4 1.6 %copy-done.13 = f32[4,2,256,256]{3,2,1,0:T(8,128)S(1)} copy-done((f32[4,2,256,256]{3,2,1,0:T(8,128)S(1)}, f32[4,2,256,256]{3,2,1,0:T(8,128)}, u32[]{:S(2)}) %copy-start.13) | copy-done | bytes 2097176
  22.0 9.3 %shard_map.95 = (f32[2,104,256]{2,1,0:T(8,128)S(1)}, f32[2,104,256]{2,1,0:T(8,128)}, f32[2,104,256]{2,1,0:T(8,128)}, f32[2,104,256]{2,1,0:T(8,128)}, bf16[1024,1...) custom-call(s32[1,2]{1,0:T(1,128)S(1)} %copy-done.6, s32[1,1]{1,0:T(1,128)} %bitcast.owner_ref, f32[2,256,512]{2,1,0:T(8,128)S(1)} %copy-done, ...), custom_call_target="tpu_custom_call" | custom-call | flops 8000000000 | bytes 1000000 | tf_op jit(solution)/shard_map/pallas_call | solution.py:476
  31.3 4.2 %shard_map.96 = (f32[32,9,8,128]{3,2,1,0:T(8,128)S(1)}, f32[32,9,8,128]{3,2,1,0:T(8,128)S(1)}) custom-call(s32[1,2]{1,0:T(1,128)S(1)} %copy-done.6, s32[1,1]{1,0:T(1,128)} %bitcast.owner_ref, bf16[1024,1024]{1,0:T(8,128)(2,1)S(1)} %get-tuple-element.33.staged_ref, f32[256,256]{1,0:T(8,128)S(1)} %get-tuple-element.34.mass_ref, f32[4,256,256]{2,1,0:T(8,128)S(1)} %copy-done.10), custom_call_target="tpu_custom_call" | custom-call | flops 5000000000 | bytes 1000000 | tf_op jit(solution)/shard_map/pallas_call | solution.py:497
  36.0 1.4 %collective-permute-start.6 = (f32[2,104,256]{2,1,0:T(8,128)}, f32[2,104,256]{2,1,0:T(8,128)}, u32[]{:S(2)}, u32[]{:S(2)}) collective-permute-start(f32[2,104,256]{2,1,0:T(8,128)} %get-tuple-element.42), channel_id=1, source_target_pairs={{0,2},{2,4},{4,6},{6,0},{1,3},{3,5},{5,7},{7,1},{8,10},{10,12},{12... | collective-permute-start | bytes 638984 | tf_op jit(solution)/shard_map/ppermute | solution.py:516
  37.3 2.5 %collective-permute-start.7 = (f32[2,104,256]{2,1,0:T(8,128)}, f32[2,104,256]{2,1,0:T(8,128)}, u32[]{:S(2)}, u32[]{:S(2)}) collective-permute-start(f32[2,104,256]{2,1,0:T(8,128)} %get-tuple-element.43), channel_id=1, source_target_pairs={{0,4},{2,6},{4,0},{6,2},{1,5},{3,7},{5,1},{7,3},{8,12},{10,14},{12... | collective-permute-start | bytes 638984 | tf_op jit(solution)/shard_map/ppermute | solution.py:516
  39.8 1.1 %collective-permute-start.8 = (f32[2,104,256]{2,1,0:T(8,128)}, f32[2,104,256]{2,1,0:T(8,128)}, u32[]{:S(2)}, u32[]{:S(2)}) collective-permute-start(f32[2,104,256]{2,1,0:T(8,128)} %get-tuple-element.44), channel_id=1, source_target_pairs={{0,6},{2,0},{4,2},{6,4},{1,7},{3,1},{5,3},{7,5},{8,14},{10,8},{12,... | collective-permute-start | bytes 638984 | tf_op jit(solution)/shard_map/ppermute | solution.py:516
  41.0 1.1 %add.11 = f32[32,9,8,128]{3,2,1,0:T(8,128)} add(f32[32,9,8,128]{3,2,1,0:T(8,128)S(1)} %get-tuple-element.36.keep_ref, f32[32,9,8,128]{3,2,1,0:T(8,128)S(1)} %collective-permute-done.2) | non-fusion elementwise | flops 294912 | bytes 3538944 | tf_op jit(solution)/shard_map/add | solution.py:527
  42.1 8.0 %all-to-all-start = ((f32[32,9,8,128]{3,2,1,0:T(8,128)}), f32[32,9,8,128]{3,2,1,0:T(8,128)S(1)}, u32[]{:S(2)}, u32[]{:S(2)}) async-start(f32[32,9,8,128]{3,2,1,0:T(8,128)} %add.11), calls=%async_computation | async-start | bytes 2359296 | tf_op jit(solution)/shard_map/all_to_all | solution.py:528
  50.1 1.3 %collective-permute-start.9 = (f32[2,104,256]{2,1,0:T(8,128)}, f32[2,104,256]{2,1,0:T(8,128)S(1)}, u32[]{:S(2)}, u32[]{:S(2)}) collective-permute-start(f32[2,104,256]{2,1,0:T(8,128)} %copy-done.4), channel_id=1, source_target_pairs={{0,1},{1,0},{2,3},{3,2},{4,5},{5,4},{6,7},{7,6},{8,9},{9,8},{10,11... | collective-permute-start | bytes 638984 | tf_op jit(solution)/shard_map/ppermute | solution.py:518
  54.6 2.1 %shard_map.99 = (f32[3,32,512]{2,1,0:T(8,128)S(1)}, f32[3,32,512]{2,1,0:T(8,128)}) custom-call(s32[1,1]{1,0:T(1,128)} %bitcast.owner_ref, f32[2,104,256]{2,1,0:T(8,128)S(1)} %copy-done.5, f32[2,104,256]{2,1,0:T(8,128)} %collective-permute-done.6.rest_1_, f32[2,104,256]{2,1,0:T(8,128)} %collective-permute-done.7.rest_2_, ...), custom_call_target="tpu_custom_call" | custom-call | flops 12000000000 | bytes 1000000 | tf_op jit(solution)/shard_map/pallas_call | solution.py:519
  57.4 4.1 %collective-permute-start.13 = (f32[3,32,512]{2,1,0:T(8,128)}, f32[3,32,512]{2,1,0:T(8,128)}, u32[]{:S(2)}, u32[]{:S(2)}) collective-permute-start(f32[3,32,512]{2,1,0:T(8,128)} %get-tuple-element.46), channel_id=1, source_target_pairs={{0,8},{8,16},{16,24},{24,32},{32,40},{40,48},{48,56},{56,64},{64,7... | collective-permute-start | bytes 589832 | tf_op jit(solution)/shard_map/ppermute | solution.py:539
  61.5 1.2 %shard_map.97 = f32[1,2]{1,0:T(1,128)} custom-call(s32[1,1]{1,0:T(1,128)} %bitcast.1.core_ref, f32[512,1024]{1,0:T(8,128)S(1)} %copy-done.11, f32[1024,512]{1,0:T(8,128)S(1)} %copy-done.12, f32[32,9,8,128]{3,2,1,0:T(8,128)S(1)} %get-tuple-element.36.keep_ref, f32[32,9,8,128]{3,2,1,0:T(8,128)S(1)} %copy-done.2), custom_call_target="tpu_custom_call" | custom-call | flops 8000000000 | bytes 1000000 | tf_op jit(solution)/shard_map/pallas_call | solution.py:530
  62.7 3.3 %all-to-all-done.parts_ref = f32[32,9,8,128]{3,2,1,0:T(8,128)S(1)} async-done(((f32[32,9,8,128]{3,2,1,0:T(8,128)}), f32[32,9,8,128]{3,2,1,0:T(8,128)S(1)}, u32[]{:S(2)}, u32[]{:S(2)}) %all-to-all-start) | async-done | bytes 1179680 | tf_op jit(solution)/shard_map/all_to_all | solution.py:528
  66.1 4.9 %collective-permute-start.5 = (f32[9,8,128]{2,1,0:T(8,128)S(1)}, f32[9,8,128]{2,1,0:T(8,128)S(1)}, u32[]{:S(2)}, u32[]{:S(2)}) collective-permute-start(f32[9,8,128]{2,1,0:T(8,128)S(1)} %shard_map.98.first_ref), channel_id=1, source_target_pairs={{0,192},{64,0},{128,64},{192,128},{1,193},{65,1},{129,65},{193,129... | collective-permute-start | bytes 110600 | tf_op jit(solution)/shard_map/ppermute | solution.py:552
  71.0 3.8 %collective-permute-start.4 = (f32[9,8,128]{2,1,0:T(8,128)S(1)}, f32[9,8,128]{2,1,0:T(8,128)S(1)}, u32[]{:S(2)}, u32[]{:S(2)}) collective-permute-start(f32[9,8,128]{2,1,0:T(8,128)S(1)} %shard_map.98.first_ref), channel_id=1, source_target_pairs={{0,128},{64,192},{128,0},{192,64},{1,129},{65,193},{129,1},{193,65... | collective-permute-start | bytes 110600 | tf_op jit(solution)/shard_map/ppermute | solution.py:552
  75.8 1.9 %collective-permute-done.4.third_ref = f32[9,8,128]{2,1,0:T(8,128)S(1)} collective-permute-done((f32[9,8,128]{2,1,0:T(8,128)S(1)}, f32[9,8,128]{2,1,0:T(8,128)S(1)}, u32[]{:S(2)}, u32[]{:S(2)}) %collective-permute-start.4) | collective-permute-done | bytes 36896 | tf_op jit(solution)/shard_map/ppermute | solution.py:552
  77.7 2.0 %collective-permute-done.3.second_ref = f32[9,8,128]{2,1,0:T(8,128)S(1)} collective-permute-done((f32[9,8,128]{2,1,0:T(8,128)S(1)}, f32[9,8,128]{2,1,0:T(8,128)S(1)}, u32[]{:S(2)}, u32[]{:S(2)}) %collective-permute-start.3) | collective-permute-done | bytes 36896 | tf_op jit(solution)/shard_map/ppermute | solution.py:552
  80.7 2.4 %collective-permute-start.15 = (f32[2,32,512]{2,1,0:T(8,128)S(1)}, f32[2,32,512]{2,1,0:T(8,128)S(1)}, u32[]{:S(2)}, u32[]{:S(2)}) collective-permute-start(f32[2,32,512]{2,1,0:T(8,128)S(1)} %shard_map.100), channel_id=1, source_target_pairs={{0,4},{2,6},{4,0},{6,2},{1,5},{3,7},{5,1},{7,3},{8,12},{10,14},{12... | collective-permute-start | bytes 393224 | tf_op jit(solution)/shard_map/ppermute | solution.py:552
  83.2 1.1 shard_map.101
  84.3 6.5 %all-to-all-start.1 = ((f32[32,8,8,128]{3,2,1,0:T(8,128)}), f32[32,8,8,128]{3,2,1,0:T(8,128)S(1)}, u32[]{:S(2)}, u32[]{:S(2)}) async-start(f32[32,8,8,128]{3,2,1,0:T(8,128)} %shard_map.101), calls=%async_computation.1 | async-start | bytes 2097152 | tf_op jit(solution)/shard_map/all_to_all | solution.py:572
  90.9 4.5 %collective-permute-start.17 = (f32[4,2,32,512]{3,2,1,0:T(8,128)S(1)}, f32[4,2,32,512]{3,2,1,0:T(8,128)S(1)}, u32[]{:S(2)}, u32[]{:S(2)}) collective-permute-start(f32[4,2,32,512]{3,2,1,0:T(8,128)S(1)} %pad_maximum_fusion.strip_ref), channel_id=1, source_target_pairs={{0,1},{1,0},{2,3},{3,2},{4,5},{5,4},{6,7},{7,6},{8,9},{9,8},{10,11... | collective-permute-start | bytes 1572872 | tf_op jit(solution)/shard_map/ppermute | solution.py:575
  95.4 1.5 %collective-permute-done.17.other_ref = f32[4,2,32,512]{3,2,1,0:T(8,128)S(1)} collective-permute-done((f32[4,2,32,512]{3,2,1,0:T(8,128)S(1)}, f32[4,2,32,512]{3,2,1,0:T(8,128)S(1)}, u32[]{:S(2)}, u32[]{:S(2)}) %collective-permute-start.17) | collective-permute-done | bytes 524320 | tf_op jit(solution)/shard_map/ppermute | solution.py:575
  96.9 1.0 shard_map.102
  98.0 4.6 %all-to-all-done.1.own_ref = f32[32,8,8,128]{3,2,1,0:T(8,128)S(1)} async-done(((f32[32,8,8,128]{3,2,1,0:T(8,128)}), f32[32,8,8,128]{3,2,1,0:T(8,128)S(1)}, u32[]{:S(2)}, u32[]{:S(2)}) %all-to-all-start.1) | async-done | bytes 1048608 | tf_op jit(solution)/shard_map/all_to_all | solution.py:572
  102.6 6.0 %collective-permute-start.18 = (f32[32,8,8,128]{3,2,1,0:T(8,128)S(1)}, f32[32,8,8,128]{3,2,1,0:T(8,128)S(1)}, u32[]{:S(2)}, u32[]{:S(2)}) collective-permute-start(f32[32,8,8,128]{3,2,1,0:T(8,128)S(1)} %all-to-all-done.1.own_ref), channel_id=1, source_target_pairs={{0,1},{1,0},{2,3},{3,2},{4,5},{5,4},{6,7},{7,6},{8,9},{9,8},{10,11... | collective-permute-start | bytes 3145736 | tf_op jit(solution)/shard_map/ppermute | solution.py:586
  108.6 2.3 %collective-permute-done.18.other_ref = f32[32,8,8,128]{3,2,1,0:T(8,128)S(1)} collective-permute-done((f32[32,8,8,128]{3,2,1,0:T(8,128)S(1)}, f32[32,8,8,128]{3,2,1,0:T(8,128)S(1)}, u32[]{:S(2)}, u32[]{:S(2)}) %collective-permute-start.18) | collective-permute-done | bytes 1048608 | tf_op jit(solution)/shard_map/ppermute | solution.py:586
  110.8 1.5 %shard_map.103 = f32[4,2,256,256]{3,2,1,0:T(8,128)} custom-call(s32[1,1]{1,0:T(1,128)} %bitcast.1.core_ref, f32[32,8,8,128]{3,2,1,0:T(8,128)S(1)} %all-to-all-done.1.own_ref, f32[32,8,8,128]{3,2,1,0:T(8,128)S(1)} %collective-permute-done.18.other_ref), custom_call_target="tpu_custom_call" | custom-call | flops 1000000000 | bytes 1000000 | tf_op jit(solution)/shard_map/pallas_call | solution.py:587
  (51 shorter events, 7.1 us)
Async XLA Ops:
  1.7 18.6 %copy-start = (f32[2,256,512]{2,1,0:T(8,128)S(1)}, f32[2,256,512]{2,1,0:T(8,128)}, u32[]{:S(2)}) copy-start(f32[2,256,512]{2,1,0:T(8,128)} %object_ref.3) | copy-start | bytes 3145732
  1.7 18.6 %copy-start.3 = (f32[1,256,256]{2,1,0:T(8,128)S(1)}, f32[1,256,256]{2,1,0:T(8,128)}, u32[]{:S(2)}) copy-start(f32[1,256,256]{2,1,0:T(8,128)} %amplitude_ref.1) | copy-start | bytes 786436
  1.7 18.6 %copy-start.6 = (s32[1,2]{1,0:T(1,128)S(1)}, s32[1,2]{1,0:T(1,128)}, u32[]{:S(2)}) copy-start(s32[1,2]{1,0:T(1,128)} %corner_ref.5) | copy-start | bytes 28
  1.8 18.6 %copy-start.7 = (f32[2,256,256]{2,1,0:T(8,128)S(1)}, f32[2,256,256]{2,1,0:T(8,128)}, u32[]{:S(2)}) copy-start(f32[2,256,256]{2,1,0:T(8,128)} %constant.20.clone.forward_ref) | copy-start | bytes 1572868
  1.8 13.5 %collective-permute-start = (f32[2,128,512]{2,1,0:T(8,128)S(1)}, f32[2,128,512]{2,1,0:T(8,128)S(1)}, u32[]{:S(2)}, u32[]{:S(2)}) collective-permute-start(f32[2,128,512]{2,1,0:T(8,128)S(1)} %constant_dynamic-slice_fusion), channel_id=1, source_target_pairs={{8,0},{16,8},{24,16},{32,24},{40,32},{48,40},{56,48},{64,56},{72,6... | collective-permute-start | bytes 1572872 | tf_op jit(solution)/shard_map/ppermute | solution.py:459
  15.3 5.0 %collective-permute-start.1 = (f32[2,128,512]{2,1,0:T(8,128)S(1)}, f32[2,128,512]{2,1,0:T(8,128)S(1)}, u32[]{:S(2)}, u32[]{:S(2)}) collective-permute-start(f32[2,128,512]{2,1,0:T(8,128)S(1)} %collective-permute-done.near_ref), channel_id=1, source_target_pairs={{0,1},{1,0},{2,3},{3,2},{4,5},{5,4},{6,7},{7,6},{8,9},{9,8},{10,11... | collective-permute-start | bytes 1572872 | tf_op jit(solution)/shard_map/ppermute | solution.py:473
  22.0 9.3 %copy-start.10 = (f32[4,256,256]{2,1,0:T(8,128)S(1)}, f32[4,256,256]{2,1,0:T(8,128)}, u32[]{:S(2)}) copy-start(f32[4,256,256]{2,1,0:T(8,128)} %get-tuple-element.35.adjoint_ref) | copy-start | bytes 3145732
  31.3 4.2 %copy-start.4 = (f32[2,104,256]{2,1,0:T(8,128)}, f32[2,104,256]{2,1,0:T(8,128)S(1)}, u32[]{:S(2)}) copy-start(f32[2,104,256]{2,1,0:T(8,128)S(1)} %get-tuple-element.41.rest_0_) | copy-start | bytes 638980
  35.5 6.6 %copy-start.1 = (f32[32,9,8,128]{3,2,1,0:T(8,128)}, f32[32,9,8,128]{3,2,1,0:T(8,128)S(1)}, u32[]{:S(2)}) copy-start(f32[32,9,8,128]{3,2,1,0:T(8,128)S(1)} %get-tuple-element.37.send_ref) | copy-start | bytes 3538948
  35.5 5.5 %collective-permute-start.2 = (f32[32,9,8,128]{3,2,1,0:T(8,128)S(1)}, f32[32,9,8,128]{3,2,1,0:T(8,128)S(1)}, u32[]{:S(2)}, u32[]{:S(2)}) collective-permute-start(f32[32,9,8,128]{3,2,1,0:T(8,128)S(1)} %get-tuple-element.37.send_ref), channel_id=1, source_target_pairs={{0,1},{1,0},{2,3},{3,2},{4,5},{5,4},{6,7},{7,6},{8,9},{9,8},{10,11... | collective-permute-start | bytes 3538952 | tf_op jit(solution)/shard_map/ppermute | solution.py:517
  36.0 15.4 %collective-permute-start.6 = (f32[2,104,256]{2,1,0:T(8,128)}, f32[2,104,256]{2,1,0:T(8,128)}, u32[]{:S(2)}, u32[]{:S(2)}) collective-permute-start(f32[2,104,256]{2,1,0:T(8,128)} %get-tuple-element.42), channel_id=1, source_target_pairs={{0,2},{2,4},{4,6},{6,0},{1,3},{3,5},{5,7},{7,1},{8,10},{10,12},{12... | collective-permute-start | bytes 638984 | tf_op jit(solution)/shard_map/ppermute | solution.py:516
  37.3 14.4 %collective-permute-start.7 = (f32[2,104,256]{2,1,0:T(8,128)}, f32[2,104,256]{2,1,0:T(8,128)}, u32[]{:S(2)}, u32[]{:S(2)}) collective-permute-start(f32[2,104,256]{2,1,0:T(8,128)} %get-tuple-element.43), channel_id=1, source_target_pairs={{0,4},{2,6},{4,0},{6,2},{1,5},{3,7},{5,1},{7,3},{8,12},{10,14},{12... | collective-permute-start | bytes 638984 | tf_op jit(solution)/shard_map/ppermute | solution.py:516
  39.8 12.1 %collective-permute-start.8 = (f32[2,104,256]{2,1,0:T(8,128)}, f32[2,104,256]{2,1,0:T(8,128)}, u32[]{:S(2)}, u32[]{:S(2)}) collective-permute-start(f32[2,104,256]{2,1,0:T(8,128)} %get-tuple-element.44), channel_id=1, source_target_pairs={{0,6},{2,0},{4,2},{6,4},{1,7},{3,1},{5,3},{7,5},{8,14},{10,8},{12,... | collective-permute-start | bytes 638984 | tf_op jit(solution)/shard_map/ppermute | solution.py:516
  42.1 23.9 %all-to-all-start = ((f32[32,9,8,128]{3,2,1,0:T(8,128)}), f32[32,9,8,128]{3,2,1,0:T(8,128)S(1)}, u32[]{:S(2)}, u32[]{:S(2)}) async-start(f32[32,9,8,128]{3,2,1,0:T(8,128)} %add.11), calls=%async_computation | async-start | bytes 2359296 | tf_op jit(solution)/shard_map/all_to_all | solution.py:528
  50.1 11.5 %copy-start.2 = (f32[32,9,8,128]{3,2,1,0:T(8,128)S(1)}, f32[32,9,8,128]{3,2,1,0:T(8,128)}, u32[]{:S(2)}) copy-start(f32[32,9,8,128]{3,2,1,0:T(8,128)} %copy-done.1) | copy-start | bytes 3538948
  50.1 2.6 %collective-permute-start.9 = (f32[2,104,256]{2,1,0:T(8,128)}, f32[2,104,256]{2,1,0:T(8,128)S(1)}, u32[]{:S(2)}, u32[]{:S(2)}) collective-permute-start(f32[2,104,256]{2,1,0:T(8,128)} %copy-done.4), channel_id=1, source_target_pairs={{0,1},{1,0},{2,3},{3,2},{4,5},{5,4},{6,7},{7,6},{8,9},{9,8},{10,11... | collective-permute-start | bytes 638984 | tf_op jit(solution)/shard_map/ppermute | solution.py:518
  51.4 1.7 %collective-permute-start.10 = (f32[2,104,256]{2,1,0:T(8,128)}, f32[2,104,256]{2,1,0:T(8,128)S(1)}, u32[]{:S(2)}, u32[]{:S(2)}) collective-permute-start(f32[2,104,256]{2,1,0:T(8,128)} %collective-permute-done.6.rest_1_), channel_id=1, source_target_pairs={{0,1},{1,0},{2,3},{3,2},{4,5},{5,4},{6,7},{7,6},{8,9},{9,8},{10,11... | collective-permute-start | bytes 638984 | tf_op jit(solution)/shard_map/ppermute | solution.py:518
  51.7 1.7 %collective-permute-start.11 = (f32[2,104,256]{2,1,0:T(8,128)}, f32[2,104,256]{2,1,0:T(8,128)S(1)}, u32[]{:S(2)}, u32[]{:S(2)}) collective-permute-start(f32[2,104,256]{2,1,0:T(8,128)} %collective-permute-done.7.rest_2_), channel_id=1, source_target_pairs={{0,1},{1,0},{2,3},{3,2},{4,5},{5,4},{6,7},{7,6},{8,9},{9,8},{10,11... | collective-permute-start | bytes 638984 | tf_op jit(solution)/shard_map/ppermute | solution.py:518
  51.9 1.8 %collective-permute-start.12 = (f32[2,104,256]{2,1,0:T(8,128)}, f32[2,104,256]{2,1,0:T(8,128)S(1)}, u32[]{:S(2)}, u32[]{:S(2)}) collective-permute-start(f32[2,104,256]{2,1,0:T(8,128)} %collective-permute-done.8.rest_3_), channel_id=1, source_target_pairs={{0,1},{1,0},{2,3},{3,2},{4,5},{5,4},{6,7},{7,6},{8,9},{9,8},{10,11... | collective-permute-start | bytes 638984 | tf_op jit(solution)/shard_map/ppermute | solution.py:518
  54.6 6.9 %copy-start.11 = (f32[512,1024]{1,0:T(8,128)S(1)}, f32[512,1024]{1,0:T(8,128)}, u32[]{:S(2)}) copy-start(f32[512,1024]{1,0:T(8,128)} %get-tuple-element.38.tall) | copy-start | bytes 6291460
  54.6 6.9 %copy-start.12 = (f32[1024,512]{1,0:T(8,128)S(1)}, f32[1024,512]{1,0:T(8,128)}, u32[]{:S(2)}) copy-start(f32[1024,512]{1,0:T(8,128)} %get-tuple-element.39.wide) | copy-start | bytes 6291460
  57.4 17.4 %collective-permute-start.13 = (f32[3,32,512]{2,1,0:T(8,128)}, f32[3,32,512]{2,1,0:T(8,128)}, u32[]{:S(2)}, u32[]{:S(2)}) collective-permute-start(f32[3,32,512]{2,1,0:T(8,128)} %get-tuple-element.46), channel_id=1, source_target_pairs={{0,8},{8,16},{16,24},{24,32},{32,40},{40,48},{48,56},{56,64},{64,7... | collective-permute-start | bytes 589832 | tf_op jit(solution)/shard_map/ppermute | solution.py:539
  62.7 12.1 %copy-start.9 = (f32[3,32,512]{2,1,0:T(8,128)S(1)}, f32[3,32,512]{2,1,0:T(8,128)}, u32[]{:S(2)}) copy-start(f32[3,32,512]{2,1,0:T(8,128)} %copy-done.8) | copy-start | bytes 589828
  66.1 9.7 %collective-permute-start.5 = (f32[9,8,128]{2,1,0:T(8,128)S(1)}, f32[9,8,128]{2,1,0:T(8,128)S(1)}, u32[]{:S(2)}, u32[]{:S(2)}) collective-permute-start(f32[9,8,128]{2,1,0:T(8,128)S(1)} %shard_map.98.first_ref), channel_id=1, source_target_pairs={{0,192},{64,0},{128,64},{192,128},{1,193},{65,1},{129,65},{193,129... | collective-permute-start | bytes 110600 | tf_op jit(solution)/shard_map/ppermute | solution.py:552
  71.0 6.7 %collective-permute-start.4 = (f32[9,8,128]{2,1,0:T(8,128)S(1)}, f32[9,8,128]{2,1,0:T(8,128)S(1)}, u32[]{:S(2)}, u32[]{:S(2)}) collective-permute-start(f32[9,8,128]{2,1,0:T(8,128)S(1)} %shard_map.98.first_ref), channel_id=1, source_target_pairs={{0,128},{64,192},{128,0},{192,64},{1,129},{65,193},{129,1},{193,65... | collective-permute-start | bytes 110600 | tf_op jit(solution)/shard_map/ppermute | solution.py:552
  74.8 4.9 %collective-permute-start.3 = (f32[9,8,128]{2,1,0:T(8,128)S(1)}, f32[9,8,128]{2,1,0:T(8,128)S(1)}, u32[]{:S(2)}, u32[]{:S(2)}) collective-permute-start(f32[9,8,128]{2,1,0:T(8,128)S(1)} %shard_map.98.first_ref), channel_id=1, source_target_pairs={{0,64},{64,128},{128,192},{192,0},{1,65},{65,129},{129,193},{193,1... | collective-permute-start | bytes 110600 | tf_op jit(solution)/shard_map/ppermute | solution.py:552
  79.7 11.1 %collective-permute-start.16 = (f32[2,32,512]{2,1,0:T(8,128)S(1)}, f32[2,32,512]{2,1,0:T(8,128)S(1)}, u32[]{:S(2)}, u32[]{:S(2)}) collective-permute-start(f32[2,32,512]{2,1,0:T(8,128)S(1)} %shard_map.100), channel_id=1, source_target_pairs={{0,6},{2,0},{4,2},{6,4},{1,7},{3,1},{5,3},{7,5},{8,14},{10,8},{12,... | collective-permute-start | bytes 393224 | tf_op jit(solution)/shard_map/ppermute | solution.py:552
  80.7 10.1 %collective-permute-start.15 = (f32[2,32,512]{2,1,0:T(8,128)S(1)}, f32[2,32,512]{2,1,0:T(8,128)S(1)}, u32[]{:S(2)}, u32[]{:S(2)}) collective-permute-start(f32[2,32,512]{2,1,0:T(8,128)S(1)} %shard_map.100), channel_id=1, source_target_pairs={{0,4},{2,6},{4,0},{6,2},{1,5},{3,7},{5,1},{7,3},{8,12},{10,14},{12... | collective-permute-start | bytes 393224 | tf_op jit(solution)/shard_map/ppermute | solution.py:552
  83.1 7.7 %collective-permute-start.14 = (f32[2,32,512]{2,1,0:T(8,128)S(1)}, f32[2,32,512]{2,1,0:T(8,128)S(1)}, u32[]{:S(2)}, u32[]{:S(2)}) collective-permute-start(f32[2,32,512]{2,1,0:T(8,128)S(1)} %shard_map.100), channel_id=1, source_target_pairs={{0,2},{2,4},{4,6},{6,0},{1,3},{3,5},{5,7},{7,1},{8,10},{10,12},{12... | collective-permute-start | bytes 393224 | tf_op jit(solution)/shard_map/ppermute | solution.py:552
  84.3 18.3 %all-to-all-start.1 = ((f32[32,8,8,128]{3,2,1,0:T(8,128)}), f32[32,8,8,128]{3,2,1,0:T(8,128)S(1)}, u32[]{:S(2)}, u32[]{:S(2)}) async-start(f32[32,8,8,128]{3,2,1,0:T(8,128)} %shard_map.101), calls=%async_computation.1 | async-start | bytes 2097152 | tf_op jit(solution)/shard_map/all_to_all | solution.py:572
  90.9 6.1 %collective-permute-start.17 = (f32[4,2,32,512]{3,2,1,0:T(8,128)S(1)}, f32[4,2,32,512]{3,2,1,0:T(8,128)S(1)}, u32[]{:S(2)}, u32[]{:S(2)}) collective-permute-start(f32[4,2,32,512]{3,2,1,0:T(8,128)S(1)} %pad_maximum_fusion.strip_ref), channel_id=1, source_target_pairs={{0,1},{1,0},{2,3},{3,2},{4,5},{5,4},{6,7},{7,6},{8,9},{9,8},{10,11... | collective-permute-start | bytes 1572872 | tf_op jit(solution)/shard_map/ppermute | solution.py:575
  102.6 8.3 %collective-permute-start.18 = (f32[32,8,8,128]{3,2,1,0:T(8,128)S(1)}, f32[32,8,8,128]{3,2,1,0:T(8,128)S(1)}, u32[]{:S(2)}, u32[]{:S(2)}) collective-permute-start(f32[32,8,8,128]{3,2,1,0:T(8,128)S(1)} %all-to-all-done.1.own_ref), channel_id=1, source_target_pairs={{0,1},{1,0},{2,3},{3,2},{4,5},{5,4},{6,7},{7,6},{8,9},{9,8},{10,11... | collective-permute-start | bytes 3145736 | tf_op jit(solution)/shard_map/ppermute | solution.py:586
  (3 other events, 3.2 us)
